TPU v7x, 32 devices: a whole 2x2x4 slice. The times are simulated.
32 devices in a mesh: ex: 8 (over z, x), ey: 4 (over y, core).
Axes of the slice: x: 2, y: 2, z: 4, core: 2. Of those that a mesh axis runs over, the one named last changes fastest.
Arguments:
- crm_state: float32 [5, 12, 32, 4096], P(None, None, None, ('ex', 'ey')), may hold values from -6 to 6
- gcm_state: float32 [5, 12, 32, 8, 4, 4], P(None, None, 'ex', 'ey'), may hold values from -6 to 6
- mass: float32 [12, 32, 8, 4, 4], P(None, 'ex', 'ey'), may hold values from 0.5 to 2
- dest: int32 [4096, 1], P(('ex', 'ey')), may hold values from 0 to 31; in each aligned block of 128 rows (0 to 127, 128 to 255, ...) at most 8 rows name the same one
- cost_class: int32 [4096], P(('ex', 'ey')), may hold values from 1 to 2
Outputs:
- cloud_slots: float32 [5, 12, 32, 8192], P(None, None, None, ('ex', 'ey'))
- gcm_out: float32 [5, 12, 32, 8, 4, 4], P(None, None, 'ex', 'ey')
Inputs may be any that keep to these rules, and one draw needn't show every extreme that they name: Among the 128 columns of one device's block, at most 8 have the same dest, and some block reaches 8.
All inputs are finite; a program needn't handle non-finite values.
Results may differ from a plain program's by a relative error of at most 0.00002.
Values sent between devices are 32-bit elements; how exact they have to be, the bound alone decides.
No kernel may reach another device: no remote copies, remote signals or barrier semaphores. Data moves between devices by JAX's collectives and lax.ppermute only.
A program may use at most 128 MiB of HBM per device.

v0:
```python
import functools

import jax
import jax.numpy as jnp
from jax import lax
from jax.experimental import pallas as pl
from jax.experimental.pallas import tpu as pltpu
from jax.sharding import PartitionSpec as P

diffusion = 0.1
advection = 0.15
buoyancy = 0.3
latent_heat = 0.5
fallout = 0.2
condense_rate = 0.4
nudging = 0.5

NT = (((1,), (1,)), ((), ()))
VMEM_LIMIT = 48 * 1024 * 1024


def substep_level(values_at, profile_row, z, levels, field_count, active):
    values = [values_at(f, z) for f in range(field_count)]
    width = values[0].shape[0]
    x_wind = values[0]
    condensed = condense_rate * jnp.maximum(values[3], 0.0)
    drift = (advection * 0.5) * x_wind
    results = []
    for f in range(field_count):
        v = values[f]
        east = pltpu.roll(v, width - 1, 0)
        west = pltpu.roll(v, 1, 0)
        around = east + west
        if z + 1 < levels:
            around = around + values_at(f, z + 1)
        if z > 0:
            around = around + values_at(f, z - 1)
        mean = jnp.sum(v, axis=0, keepdims=True) * (1.0 / width)
        nudged = nudging * (profile_row(f, z) - mean)
        change = diffusion * (around - 4.0 * v) - drift * (east - west) + nudged
        if f == 1:
            change = change + buoyancy * values[2]
        elif f == 2:
            change = change - buoyancy * values[1] + latent_heat * condensed
        elif f == 3:
            change = change - condensed
        elif f == 4:
            change = change + condensed - fallout * v
        results.append(jnp.where(active, v + change, v))
    return results


def cloud_kernel(devices, capacity, crm_ref, gcm_ref, mass_ref, dest_ref, cost_ref,
                 send_ref, nodes_ref, low_ref, high_ref, first_ref, second_ref, prof_ref, tend_ref):
    field_count, levels, width, owned = crm_ref.shape
    used = field_count * levels
    total = used + levels
    nodes = gcm_ref.shape[1]
    mass = mass_ref[...]
    spare = nodes - total
    grid_fields = jnp.concatenate(
        [gcm_ref[f] for f in range(field_count)] + [mass, jnp.zeros((nodes, spare), jnp.float32)], axis=1
    )
    prof_ref[...] = grid_fields.T
    tend_ref[...] = jnp.zeros_like(tend_ref)
    cost = cost_ref[...]
    once = jnp.broadcast_to(cost >= 1, (width, owned))
    twice = jnp.broadcast_to(cost >= 2, (width, owned))

    def profile_row(f, z):
        return prof_ref[pl.ds(f * levels + z, 1), :]

    for z in range(levels):
        fresh = substep_level(lambda f, k: crm_ref[f, k], profile_row, z, levels, field_count, once)
        for f in range(field_count):
            first_ref[f, z] = fresh[f]
    for z in range(levels):
        fresh = substep_level(lambda f, k: first_ref[f, k], profile_row, z, levels, field_count, twice)
        for f in range(field_count):
            second_ref[f, z] = fresh[f]
            gained = jnp.sum(fresh[f] - crm_ref[f, z], axis=0, keepdims=True) * (1.0 / width)
            tend_ref[pl.ds(f * levels + z, 1), :] = gained

    dest_row = jnp.broadcast_to(dest_ref[...].astype(jnp.float32), (owned, owned))
    dest_col = dest_row.T
    rows = lax.broadcasted_iota(jnp.int32, (owned, owned), 0)
    cols = lax.broadcasted_iota(jnp.int32, (owned, owned), 1)
    earlier = jnp.where((dest_row == dest_col) & (rows < cols), 1, 0)
    rank = jnp.sum(earlier, axis=0, keepdims=True)
    slot = dest_ref[...] * capacity + rank
    slots = devices * capacity
    slot_rows = lax.broadcasted_iota(jnp.int32, (slots, owned), 0)
    picks = jnp.where(slot_rows == slot, 1.0, 0.0).astype(jnp.bfloat16)

    group = owned // width
    for f in range(field_count):
        for z in range(0, levels, group):
            block = second_ref[f, pl.ds(z, group)].reshape(group * width, owned)
            high = block.astype(jnp.bfloat16)
            rest = block - high.astype(jnp.float32)
            middle = rest.astype(jnp.bfloat16)
            low = (rest - middle.astype(jnp.float32)).astype(jnp.bfloat16)
            moved = lax.dot_general(picks, high, NT, preferred_element_type=jnp.float32)
            moved = moved + lax.dot_general(picks, middle, NT, preferred_element_type=jnp.float32)
            moved = moved + lax.dot_general(picks, low, NT, preferred_element_type=jnp.float32)
            at = (f * levels + z) * width
            send_ref[:, at:at + group * width] = moved

    factors = jnp.concatenate(
        [mass] * field_count + [jnp.ones((nodes, nodes - used), jnp.float32)], axis=1
    )
    weighted = (grid_fields + tend_ref[...].T) * factors
    nodes_ref[...] = weighted


def edges_x(elx, ely, side, nodes_ref, low_ref, high_ref):
    step = side * side
    for b in range(ely):
        low_ref[b * side:(b + 1) * side, :] = nodes_ref[b * step:b * step + side, :]
        start = (elx - 1) * ely * step + b * step + (side - 1) * side
        high_ref[b * side:(b + 1) * side, :] = nodes_ref[start:start + side, :]


def kernel_a(devices, capacity, elx, ely, side, *refs):
    cloud_kernel(devices, capacity, *refs)
    edges_x(elx, ely, side, *refs[6:9])


def kernel_x(elx, ely, side, nodes_ref, west_ref, east_ref, sum_ref, low_ref, high_ref):
    step = side * side
    sum_ref[...] = nodes_ref[...]
    for a in range(elx):
        for b in range(ely):
            base = (a * ely + b) * step
            last = base + (side - 1) * side
            if a > 0:
                before = ((a - 1) * ely + b) * step + (side - 1) * side
                gain = nodes_ref[before:before + side, :]
            else:
                gain = west_ref[b * side:(b + 1) * side, :]
            sum_ref[base:base + side, :] = nodes_ref[base:base + side, :] + gain
            if a + 1 < elx:
                after = ((a + 1) * ely + b) * step
                gain = nodes_ref[after:after + side, :]
            else:
                gain = east_ref[b * side:(b + 1) * side, :]
            sum_ref[last:last + side, :] = nodes_ref[last:last + side, :] + gain
    for a in range(elx):
        first = a * ely * step
        final = (a * ely + ely - 1) * step + side - 1
        low_ref[a * side:(a + 1) * side, :] = sum_ref[pl.ds(first, side, stride=side), :]
        high_ref[a * side:(a + 1) * side, :] = sum_ref[pl.ds(final, side, stride=side), :]


def kernel_y(elx, ely, side, sum_ref, south_ref, north_ref, out_ref, full_ref):
    step = side * side
    field_count, nodes, levels = out_ref.shape
    full_ref[...] = sum_ref[...]
    for a in range(elx):
        for b in range(ely):
            base = (a * ely + b) * step
            if b > 0:
                gain = sum_ref[pl.ds(base - step + side - 1, side, stride=side), :]
            else:
                gain = south_ref[a * side:(a + 1) * side, :]
            here = pl.ds(base, side, stride=side)
            full_ref[here, :] = sum_ref[here, :] + gain
            if b + 1 < ely:
                gain = sum_ref[pl.ds(base + step, side, stride=side), :]
            else:
                gain = north_ref[a * side:(a + 1) * side, :]
            here = pl.ds(base + side - 1, side, stride=side)
            full_ref[here, :] = sum_ref[here, :] + gain
    full = full_ref[...]
    divisor = full[:, field_count * levels:(field_count + 1) * levels]
    for f in range(field_count):
        out_ref[f] = full[:, f * levels:(f + 1) * levels] / divisor


def kernel_out(devices, capacity, recv_ref, out_ref):
    ranked = [recv_ref[pl.ds(r, devices, stride=capacity), :] for r in range(capacity)]
    out_ref[...] = jnp.concatenate(ranked, axis=0).T


def params(**more):
    return pltpu.CompilerParams(vmem_limit_bytes=VMEM_LIMIT, **more)


def cost(flops, byte_count):
    return pl.CostEstimate(flops=flops, bytes_accessed=byte_count, transcendentals=0)


def shift(face, axis, by):
    count = lax.axis_size(axis)
    return lax.ppermute(face, axis, [(i, (i + by) % count) for i in range(count)])


def body(crm_state, gcm_state, mass, dest, cost_class):
    devices = lax.axis_size(("ex", "ey"))
    field_count, levels, width, owned = crm_state.shape
    elx, ely, side = gcm_state.shape[2:5]
    capacity = max(2, 2 * owned // devices)
    slots = capacity * devices
    values = field_count * levels * width
    f32 = jnp.float32
    gcm_nodes = gcm_state.transpose(0, 2, 3, 4, 5, 1).reshape(field_count, owned, levels)
    mass_nodes = mass.transpose(1, 2, 3, 4, 0).reshape(owned, levels)
    sizes = (elx, ely, side)
    face_x = jax.ShapeDtypeStruct((ely * side, owned), f32)
    face_y = jax.ShapeDtypeStruct((elx * side, owned), f32)
    square = jax.ShapeDtypeStruct((owned, owned), f32)
    send, nodes, low, high = pl.pallas_call(
        functools.partial(kernel_a, devices, capacity, *sizes),
        out_shape=(jax.ShapeDtypeStruct((slots, values), f32), square, face_x, face_x),
        scratch_shapes=[
            pltpu.VMEM(crm_state.shape, f32),
            pltpu.VMEM(crm_state.shape, f32),
            pltpu.VMEM((owned, owned), f32),
            pltpu.VMEM((owned, owned), f32),
        ],
        compiler_params=params(),
        name="cloud_models",
    )(crm_state, gcm_nodes, mass_nodes, dest.reshape(1, owned), cost_class.reshape(1, owned))
    received = lax.all_to_all(
        send.reshape(devices, capacity, values), ("ex", "ey"), split_axis=0, concat_axis=0, tiled=True
    )
    east = shift(low, "ex", -1)
    west = shift(high, "ex", 1)
    summed, low, high = pl.pallas_call(
        functools.partial(kernel_x, *sizes),
        out_shape=(square, face_y, face_y),
        compiler_params=params(),
        cost_estimate=cost(10**5, 10**5),
        name="edge_sum_first",
    )(nodes, west, east)
    north = shift(low, "ey", -1)
    south = shift(high, "ey", 1)
    gcm_out = pl.pallas_call(
        functools.partial(kernel_y, *sizes),
        out_shape=jax.ShapeDtypeStruct((field_count, owned, levels), f32),
        scratch_shapes=[pltpu.VMEM((owned, owned), f32)],
        compiler_params=params(),
        cost_estimate=cost(10**5, 10**5),
        name="edge_sum_second",
    )(summed, south, north)
    gcm_out = gcm_out.reshape(field_count, elx, ely, side, side, levels).transpose(0, 5, 1, 2, 3, 4)
    block = owned
    cloud = pl.pallas_call(
        functools.partial(kernel_out, devices, capacity),
        grid=(values // block,),
        in_specs=[pl.BlockSpec((slots, block), lambda i: (0, i))],
        out_specs=pl.BlockSpec((block, slots), lambda i: (i, 0)),
        out_shape=jax.ShapeDtypeStruct((values, slots), f32),
        compiler_params=params(),
        name="cloud_slots",
    )(received.reshape(slots, values))
    return cloud.reshape(field_count, levels, width, slots), gcm_out


def solution(mesh):
    return jax.shard_map(
        body,
        mesh=mesh,
        in_specs=(
            P(None, None, None, ("ex", "ey")),
            P(None, None, "ex", "ey", None, None),
            P(None, "ex", "ey", None, None),
            P(("ex", "ey"), None),
            P(("ex", "ey")),
        ),
        out_specs=(P(None, None, None, ("ex", "ey")), P(None, None, "ex", "ey", None, None)),
        check_vma=False,
    )
```

profile of v0, /device:TPU:17, one launch (start us, length us, event | category | flops | bytes accessed | tf_op | source)
XLA Modules:
  0.0 72.1 jit_solution(8488253787753767685)
XLA Ops:
  0.6 0.0 copy-start.1
  0.6 1.2 %copy-done.1 = f32[5,12,32,128]{3,2,1,0:T(8,128)S(1)} copy-done((f32[5,12,32,128]{3,2,1,0:T(8,128)S(1)}, f32[5,12,32,128]{3,2,1,0:T(8,128)}, u32[]{:S(2)}) %copy-start.1) | copy-done | bytes 983064
  1.8 0.0 copy-start.2
  1.8 1.0 %copy-done.2 = f32[5,12,4,2,4,4]{1,5,4,3,2,0:T(4,128)S(1)} copy-done((f32[5,12,4,2,4,4]{1,5,4,3,2,0:T(4,128)S(1)}, f32[5,12,4,2,4,4]{1,5,4,3,2,0:T(4,128)}, u32[]{:S(2)}) %copy-start.2) | copy-done | bytes 30744
  2.8 0.0 copy-start.3
  2.8 0.8 %copy-done.3 = f32[12,4,2,4,4]{0,4,3,2,1:T(4,128)S(1)} copy-done((f32[12,4,2,4,4]{0,4,3,2,1:T(4,128)S(1)}, f32[12,4,2,4,4]{0,4,3,2,1:T(4,128)}, u32[]{:S(2)}) %copy-start.3) | copy-done | bytes 6168
  3.6 0.0 copy-start.4
  3.6 0.7 copy-done.4
  4.3 0.0 copy-start.5
  4.3 0.7 copy-done.5
  5.0 2.6 %cloud_models.1 = (f32[256,1920]{1,0:T(8,128)S(1)}, f32[128,128]{1,0:T(8,128)S(1)}, f32[8,128]{1,0:T(8,128)S(1)}, f32[8,128]{1,0:T(8,128)S(1)}) custom-call(f32[5,12,32,128]{3,2,1,0:T(8,128)S(1)} %copy-done.1, f32[5,128,12]{2,1,0:T(8,128)S(1)} %bitcast.16, f32[128,12]{1,0:T(8,128)S(1)} %bitcast.17, s32[1,128]{1,0:T(1,128)S(1)} %bitcast.18, s32[1,128]{1,0:T(1,128)S(1)} %bitcast.19), custom_call_target="tpu_custom_call" | custom-call | tf_op jit(solution)/shard_map/cloud_models/pallas_call | solution.py:212
  7.6 0.0 copy-start
  7.6 1.3 %copy-done = f32[256,1920]{1,0:T(8,128)} copy-done((f32[256,1920]{1,0:T(8,128)}, f32[256,1920]{1,0:T(8,128)S(1)}, u32[]{:S(2)}) %copy-start) | copy-done | bytes 1966104
  8.9 6.2 %all-to-all-start = ((f32[32,8,1920]{2,1,0:T(8,128)}), f32[32,8,1920]{2,1,0:T(8,128)S(1)}, u32[]{:S(2)}, u32[]{:S(2)}) async-start(f32[32,8,1920]{2,1,0:T(8,128)} %bitcast.15), calls=%async_computation | async-start | bytes 3932160 | tf_op jit(solution)/shard_map/all_to_all | solution.py:224
  15.1 1.2 %collective-permute-start = (f32[8,128]{1,0:T(8,128)S(1)}, f32[8,128]{1,0:T(8,128)S(1)}, u32[]{:S(2)}, u32[]{:S(2)}) collective-permute-start(f32[8,128]{1,0:T(8,128)S(1)} %get-tuple-element.11), channel_id=1, source_target_pairs={{0,4},{4,8},{8,12},{12,16},{16,20},{20,24},{24,28},{28,0},{1,5},{5... | collective-permute-start | bytes 12296 | tf_op jit(solution)/shard_map/ppermute | solution.py:195
  16.4 1.2 %collective-permute-start.1 = (f32[8,128]{1,0:T(8,128)S(1)}, f32[8,128]{1,0:T(8,128)S(1)}, u32[]{:S(2)}, u32[]{:S(2)}) collective-permute-start(f32[8,128]{1,0:T(8,128)S(1)} %get-tuple-element.12), channel_id=1, source_target_pairs={{0,28},{4,0},{8,4},{12,8},{16,12},{20,16},{24,20},{28,24},{1,29},{... | collective-permute-start | bytes 12296 | tf_op jit(solution)/shard_map/ppermute | solution.py:195
  17.6 42.0 %collective-permute-done.west_ref = f32[8,128]{1,0:T(8,128)S(1)} collective-permute-done((f32[8,128]{1,0:T(8,128)S(1)}, f32[8,128]{1,0:T(8,128)S(1)}, u32[]{:S(2)}, u32[]{:S(2)}) %collective-permute-start) | collective-permute-done | bytes 4128 | tf_op jit(solution)/shard_map/ppermute | solution.py:195
  59.6 0.0 collective-permute-done.1.east_ref
  59.6 2.2 %collective-permute-start.2 = (f32[16,128]{1,0:T(8,128)S(1)}, f32[16,128]{1,0:T(8,128)S(1)}, u32[]{:S(2)}, u32[]{:S(2)}) collective-permute-start(f32[16,128]{1,0:T(8,128)S(1)} %get-tuple-element.14), channel_id=1, source_target_pairs={{0,1},{1,2},{2,3},{3,0},{4,5},{5,6},{6,7},{7,4},{8,9},{9,10},{10,1... | collective-permute-start | bytes 24584 | tf_op jit(solution)/shard_map/ppermute | solution.py:195
  61.8 0.0 collective-permute-start.3
  61.8 0.8 %collective-permute-done.2.south_ref = f32[16,128]{1,0:T(8,128)S(1)} collective-permute-done((f32[16,128]{1,0:T(8,128)S(1)}, f32[16,128]{1,0:T(8,128)S(1)}, u32[]{:S(2)}, u32[]{:S(2)}) %collective-permute-start.2) | collective-permute-done | bytes 8224 | tf_op jit(solution)/shard_map/ppermute | solution.py:195
  62.6 2.3 %collective-permute-done.3.north_ref = f32[16,128]{1,0:T(8,128)S(1)} collective-permute-done((f32[16,128]{1,0:T(8,128)S(1)}, f32[16,128]{1,0:T(8,128)S(1)}, u32[]{:S(2)}, u32[]{:S(2)}) %collective-permute-start.3) | collective-permute-done | bytes 8224 | tf_op jit(solution)/shard_map/ppermute | solution.py:195
  64.9 1.0 %edge_sum_second.1 = f32[5,128,12]{2,1,0:T(8,128)} custom-call(f32[128,128]{1,0:T(8,128)S(1)} %get-tuple-element.13.sum_ref, f32[16,128]{1,0:T(8,128)S(1)} %collective-permute-done.2.south_ref, f32[16,128]{1,0:T(8,128)S(1)} %collective-permute-done.3.north_ref), custom_call_target="tpu_custom_call" | custom-call | flops 100000 | bytes 100000 | tf_op jit(solution)/shard_map/edge_sum_second/pallas_call | solution.py:238
  65.9 0.0 all-to-all-done
  65.9 6.1 %cloud_slots.1 = f32[1920,256]{1,0:T(8,128)} custom-call(f32[256,1920]{1,0:T(8,128)S(1)} %bitcast.14), custom_call_target="tpu_custom_call" | custom-call | tf_op jit(solution)/shard_map/cloud_slots/pallas_call | solution.py:248
  (1 shorter events, 0.0 us)
Async XLA Ops:
  0.6 1.2 %copy-start.1 = (f32[5,12,32,128]{3,2,1,0:T(8,128)S(1)}, f32[5,12,32,128]{3,2,1,0:T(8,128)}, u32[]{:S(2)}) copy-start(f32[5,12,32,128]{3,2,1,0:T(8,128)} %refs_0_.1) | copy-start | bytes 2949124
  1.8 1.0 %copy-start.2 = (f32[5,12,4,2,4,4]{1,5,4,3,2,0:T(4,128)S(1)}, f32[5,12,4,2,4,4]{1,5,4,3,2,0:T(4,128)}, u32[]{:S(2)}) copy-start(f32[5,12,4,2,4,4]{1,5,4,3,2,0:T(4,128)} %param.6) | copy-start | bytes 92164
  2.8 0.8 %copy-start.3 = (f32[12,4,2,4,4]{0,4,3,2,1:T(4,128)S(1)}, f32[12,4,2,4,4]{0,4,3,2,1:T(4,128)}, u32[]{:S(2)}) copy-start(f32[12,4,2,4,4]{0,4,3,2,1:T(4,128)} %param.7) | copy-start | bytes 18436
  3.6 0.7 copy-start.4
  4.3 0.7 copy-start.5
  7.6 1.3 %copy-start = (f32[256,1920]{1,0:T(8,128)}, f32[256,1920]{1,0:T(8,128)S(1)}, u32[]{:S(2)}) copy-start(f32[256,1920]{1,0:T(8,128)S(1)} %get-tuple-element.9) | copy-start | bytes 5898244
  8.9 57.0 %all-to-all-start = ((f32[32,8,1920]{2,1,0:T(8,128)}), f32[32,8,1920]{2,1,0:T(8,128)S(1)}, u32[]{:S(2)}, u32[]{:S(2)}) async-start(f32[32,8,1920]{2,1,0:T(8,128)} %bitcast.15), calls=%async_computation | async-start | bytes 3932160 | tf_op jit(solution)/shard_map/all_to_all | solution.py:224
  15.1 44.4 %collective-permute-start = (f32[8,128]{1,0:T(8,128)S(1)}, f32[8,128]{1,0:T(8,128)S(1)}, u32[]{:S(2)}, u32[]{:S(2)}) collective-permute-start(f32[8,128]{1,0:T(8,128)S(1)} %get-tuple-element.11), channel_id=1, source_target_pairs={{0,4},{4,8},{8,12},{12,16},{16,20},{20,24},{24,28},{28,0},{1,5},{5... | collective-permute-start | bytes 12296 | tf_op jit(solution)/shard_map/ppermute | solution.py:195
  16.4 43.2 %collective-permute-start.1 = (f32[8,128]{1,0:T(8,128)S(1)}, f32[8,128]{1,0:T(8,128)S(1)}, u32[]{:S(2)}, u32[]{:S(2)}) collective-permute-start(f32[8,128]{1,0:T(8,128)S(1)} %get-tuple-element.12), channel_id=1, source_target_pairs={{0,28},{4,0},{8,4},{12,8},{16,12},{20,16},{24,20},{28,24},{1,29},{... | collective-permute-start | bytes 12296 | tf_op jit(solution)/shard_map/ppermute | solution.py:195
  59.6 3.0 %collective-permute-start.2 = (f32[16,128]{1,0:T(8,128)S(1)}, f32[16,128]{1,0:T(8,128)S(1)}, u32[]{:S(2)}, u32[]{:S(2)}) collective-permute-start(f32[16,128]{1,0:T(8,128)S(1)} %get-tuple-element.14), channel_id=1, source_target_pairs={{0,1},{1,2},{2,3},{3,0},{4,5},{5,6},{6,7},{7,4},{8,9},{9,10},{10,1... | collective-permute-start | bytes 24584 | tf_op jit(solution)/shard_map/ppermute | solution.py:195
  61.8 3.1 %collective-permute-start.3 = (f32[16,128]{1,0:T(8,128)S(1)}, f32[16,128]{1,0:T(8,128)S(1)}, u32[]{:S(2)}, u32[]{:S(2)}) collective-permute-start(f32[16,128]{1,0:T(8,128)S(1)} %get-tuple-element.15), channel_id=1, source_target_pairs={{0,3},{1,0},{2,1},{3,2},{4,7},{5,4},{6,5},{7,6},{8,11},{9,8},{10,9... | collective-permute-start | bytes 24584 | tf_op jit(solution)/shard_map/ppermute | solution.py:195
where the time goes:
time: 72.4 us; the launch traced here: 72.1 us
  waiting for transfers between devices  45.1 us (62%)
  starting transfers between devices  10.9 us (15%)
  Pallas kernels  9.82 us (14%)
  local copies, waits for them, and re-layouts  5.58 us (8%)
    ppermute x4, waiting for transfers between devices, shift(): lax.ppermute(face, axis, [(i, (i + by) % count) for i in range(count)])  45.1 us
    all_to_all x1, starting transfers between devices, body(): lax.all_to_all(send.reshape(devices, capacity, values), ('ex', 'ey'), spl...  6.25 us
    pallas_call x1, Pallas kernels, body(): pl.pallas_call(functools.partial(kernel_out, devices, capacity), grid=(va...  6.13 us
    unnamed x12, local copies, waits for them, and re-layouts  5.58 us
    ppermute x4, starting transfers between devices, shift(): lax.ppermute(face, axis, [(i, (i + by) % count) for i in range(count)])  4.66 us
    pallas_call x1, Pallas kernels, body(): pl.pallas_call(functools.partial(kernel_a, devices, capacity, *sizes), ou...  2.64 us
  transfers between devices with their start and end apart: 5, of which 3 were waited for; matrix products, arithmetic and copies ran while one was open for 0% of the time, Pallas kernels for 1%

commit v1 on v0

--- a/solution.py
+++ b/solution.py
@@ -50,9 +50,29 @@
     return results
 
 
-def cloud_kernel(devices, capacity, crm_ref, gcm_ref, mass_ref, dest_ref, cost_ref,
-                 send_ref, nodes_ref, low_ref, high_ref, first_ref, second_ref, prof_ref, tend_ref):
+def fetch(source, target, sem):
+    copy = pltpu.make_async_copy(source, target, sem)
+    copy.start()
+    return copy
+
+
+def cloud_kernel(devices, capacity, crm_hbm, gcm_hbm, mass_hbm, dest_hbm, cost_hbm,
+                 send_hbm, nodes_ref, low_ref, high_ref, first_ref, second_ref, prof_ref, tend_ref,
+                 crm_ref, gcm_ref, mass_ref, dest_ref, cost_ref, send_ref, small_sem, crm_sem, send_sem):
     field_count, levels, width, owned = crm_ref.shape
+    small = [
+        fetch(gcm_hbm, gcm_ref, small_sem.at[0]),
+        fetch(mass_hbm, mass_ref, small_sem.at[1]),
+        fetch(dest_hbm, dest_ref, small_sem.at[2]),
+        fetch(cost_hbm, cost_ref, small_sem.at[3]),
+    ]
+    group = owned // width
+    pieces = [
+        fetch(crm_hbm.at[:, pl.ds(z, group)], crm_ref.at[:, pl.ds(z, group)], crm_sem.at[z // group])
+        for z in range(0, levels, group)
+    ]
+    for copy in small:
+        copy.wait()
     used = field_count * levels
     total = used + levels
     nodes = gcm_ref.shape[1]
@@ -71,6 +91,10 @@
         return prof_ref[pl.ds(f * levels + z, 1), :]
 
     for z in range(levels):
+        if z == 0:
+            pieces[0].wait()
+        if (z + 1) % group == 0 and z + 1 < levels:
+            pieces[(z + 1) // group].wait()
         fresh = substep_level(lambda f, k: crm_ref[f, k], profile_row, z, levels, field_count, once)
         for f in range(field_count):
             first_ref[f, z] = fresh[f]
@@ -92,7 +116,9 @@
     slot_rows = lax.broadcasted_iota(jnp.int32, (slots, owned), 0)
     picks = jnp.where(slot_rows == slot, 1.0, 0.0).astype(jnp.bfloat16)
 
-    group = owned // width
+    field_rows = levels // group * capacity
+    aligned = field_rows % 8 == 0
+    sends = []
     for f in range(field_count):
         for z in range(0, levels, group):
             block = second_ref[f, pl.ds(z, group)].reshape(group * width, owned)
@@ -103,14 +129,20 @@
             moved = lax.dot_general(picks, high, NT, preferred_element_type=jnp.float32)
             moved = moved + lax.dot_general(picks, middle, NT, preferred_element_type=jnp.float32)
             moved = moved + lax.dot_general(picks, low, NT, preferred_element_type=jnp.float32)
-            at = (f * levels + z) * width
-            send_ref[:, at:at + group * width] = moved
+            at = (f * levels + z) // group * capacity
+            send_ref[:, at:at + capacity, :] = moved.reshape(devices, capacity, group * width)
+        if aligned:
+            part = pl.ds(f * field_rows, field_rows)
+            sends.append(fetch(send_ref.at[:, part], send_hbm.at[:, part], send_sem.at[f]))
+    if not aligned:
+        sends.append(fetch(send_ref, send_hbm, send_sem.at[0]))
 
     factors = jnp.concatenate(
         [mass] * field_count + [jnp.ones((nodes, nodes - used), jnp.float32)], axis=1
     )
     weighted = (grid_fields + tend_ref[...].T) * factors
     nodes_ref[...] = weighted
+    return sends
 
 
 def edges_x(elx, ely, side, nodes_ref, low_ref, high_ref):
@@ -122,8 +154,10 @@
 
 
 def kernel_a(devices, capacity, elx, ely, side, *refs):
-    cloud_kernel(devices, capacity, *refs)
+    sends = cloud_kernel(devices, capacity, *refs)
     edges_x(elx, ely, side, *refs[6:9])
+    for copy in sends:
+        copy.wait()
 
 
 def kernel_x(elx, ely, side, nodes_ref, west_ref, east_ref, sum_ref, low_ref, high_ref):
@@ -177,9 +211,19 @@
         out_ref[f] = full[:, f * levels:(f + 1) * levels] / divisor
 
 
-def kernel_out(devices, capacity, recv_ref, out_ref):
-    ranked = [recv_ref[pl.ds(r, devices, stride=capacity), :] for r in range(capacity)]
-    out_ref[...] = jnp.concatenate(ranked, axis=0).T
+def kernel_out(devices, capacity, recv_ref, out_hbm, out_ref, sem):
+    values = out_ref.shape[0]
+    block = values // sem.shape[0]
+    pitch = recv_ref.shape[0] // devices
+    copies = []
+    for step, at in enumerate(range(0, values, block)):
+        first = step * capacity
+        ranked = [recv_ref[pl.ds(first + r, devices, stride=pitch), :] for r in range(capacity)]
+        out_ref[at:at + block, :] = jnp.concatenate(ranked, axis=0).T
+        part = pl.ds(at, block)
+        copies.append(fetch(out_ref.at[part], out_hbm.at[part], sem.at[step]))
+    for copy in copies:
+        copy.wait()
 
 
 def params(**more):
@@ -205,24 +249,38 @@
     f32 = jnp.float32
     gcm_nodes = gcm_state.transpose(0, 2, 3, 4, 5, 1).reshape(field_count, owned, levels)
     mass_nodes = mass.transpose(1, 2, 3, 4, 0).reshape(owned, levels)
+    packed = (devices, values // owned * capacity, owned)
     sizes = (elx, ely, side)
     face_x = jax.ShapeDtypeStruct((ely * side, owned), f32)
     face_y = jax.ShapeDtypeStruct((elx * side, owned), f32)
+    in_hbm = pl.BlockSpec(memory_space=pltpu.HBM)
+    in_vmem = pl.BlockSpec(memory_space=pltpu.VMEM)
     square = jax.ShapeDtypeStruct((owned, owned), f32)
     send, nodes, low, high = pl.pallas_call(
         functools.partial(kernel_a, devices, capacity, *sizes),
-        out_shape=(jax.ShapeDtypeStruct((slots, values), f32), square, face_x, face_x),
+        out_shape=(jax.ShapeDtypeStruct(packed, f32), square, face_x, face_x),
+        in_specs=[in_hbm] * 5,
+        out_specs=(in_hbm, in_vmem, in_vmem, in_vmem),
         scratch_shapes=[
             pltpu.VMEM(crm_state.shape, f32),
             pltpu.VMEM(crm_state.shape, f32),
             pltpu.VMEM((owned, owned), f32),
             pltpu.VMEM((owned, owned), f32),
+            pltpu.VMEM(crm_state.shape, f32),
+            pltpu.VMEM(gcm_nodes.shape, f32),
+            pltpu.VMEM(mass_nodes.shape, f32),
+            pltpu.VMEM((1, owned), jnp.int32),
+            pltpu.VMEM((1, owned), jnp.int32),
+            pltpu.VMEM(packed, f32),
+            pltpu.SemaphoreType.DMA((4,)),
+            pltpu.SemaphoreType.DMA((levels * width // owned,)),
+            pltpu.SemaphoreType.DMA((field_count,)),
         ],
         compiler_params=params(),
         name="cloud_models",
     )(crm_state, gcm_nodes, mass_nodes, dest.reshape(1, owned), cost_class.reshape(1, owned))
     received = lax.all_to_all(
-        send.reshape(devices, capacity, values), ("ex", "ey"), split_axis=0, concat_axis=0, tiled=True
+        send, ("ex", "ey"), split_axis=0, concat_axis=0, tiled=True
     )
     east = shift(low, "ex", -1)
     west = shift(high, "ex", 1)
@@ -244,16 +302,15 @@
         name="edge_sum_second",
     )(summed, south, north)
     gcm_out = gcm_out.reshape(field_count, elx, ely, side, side, levels).transpose(0, 5, 1, 2, 3, 4)
-    block = owned
     cloud = pl.pallas_call(
         functools.partial(kernel_out, devices, capacity),
-        grid=(values // block,),
-        in_specs=[pl.BlockSpec((slots, block), lambda i: (0, i))],
-        out_specs=pl.BlockSpec((block, slots), lambda i: (i, 0)),
+        in_specs=[in_vmem],
+        out_specs=in_hbm,
         out_shape=jax.ShapeDtypeStruct((values, slots), f32),
+        scratch_shapes=[pltpu.VMEM((values, slots), f32), pltpu.SemaphoreType.DMA((values // owned,))],
         compiler_params=params(),
         name="cloud_slots",
-    )(received.reshape(slots, values))
+    )(received.reshape(-1, owned))
     return cloud.reshape(field_count, levels, width, slots), gcm_out
 
 

time: 72.4 us -> 69.4 us (0.959)
  Pallas kernels: 9.82 us -> 6.86 us
    pallas_call x1, Pallas kernels: 6.13 us -> 1.49 us  [body(): pl.pallas_call(functools.partial(kernel_out, devices, capacity), in_specs...]
    pallas_call x1, Pallas kernels: 2.64 us -> 4.33 us  [body(): pl.pallas_call(functools.partial(kernel_a, devices, capacity, *sizes), ou...]
  transfers between devices with their start and end apart: 5 -> 5, of which waited for: 3 -> 3; matrix products, arithmetic and copies ran while one was open for 0% -> 0% of each run, Pallas kernels for 1% -> 2%
where the time goes in v1:
time: 69.4 us; the launch traced here: 69.1 us
  waiting for transfers between devices  45.1 us (65%)
  starting transfers between devices  10.9 us (16%)
  Pallas kernels  6.86 us (10%)
  local copies, waits for them, and re-layouts  5.58 us (8%)
    ppermute x4, waiting for transfers between devices, shift(): lax.ppermute(face, axis, [(i, (i + by) % count) for i in range(count)])  45.1 us
    all_to_all x1, starting transfers between devices, body(): lax.all_to_all(send, ('ex', 'ey'), split_axis=0, concat_axis=0, tiled=True)  6.25 us
    unnamed x12, local copies, waits for them, and re-layouts  5.58 us
    ppermute x4, starting transfers between devices, shift(): lax.ppermute(face, axis, [(i, (i + by) % count) for i in range(count)])  4.66 us
    pallas_call x1, Pallas kernels, body(): pl.pallas_call(functools.partial(kernel_a, devices, capacity, *sizes), ou...  4.33 us
    pallas_call x1, Pallas kernels, body(): pl.pallas_call(functools.partial(kernel_out, devices, capacity), in_specs...  1.49 us
  transfers between devices with their start and end apart: 5, of which 3 were waited for; matrix products, arithmetic and copies ran while one was open for 0% of the time, Pallas kernels for 2%

profile of v1, /device:TPU:17, one launch (start us, length us, event | category | flops | bytes accessed | tf_op | source)
XLA Modules:
  0.0 69.1 jit_solution(11261990181943048446)
XLA Ops:
  0.6 0.0 copy-start.1
  0.6 1.2 %copy-done.1 = f32[5,12,32,128]{3,2,1,0:T(8,128)S(1)} copy-done((f32[5,12,32,128]{3,2,1,0:T(8,128)S(1)}, f32[5,12,32,128]{3,2,1,0:T(8,128)}, u32[]{:S(2)}) %copy-start.1) | copy-done | bytes 983064
  1.8 0.0 copy-start.2
  1.8 1.0 %copy-done.2 = f32[5,12,4,2,4,4]{1,5,4,3,2,0:T(4,128)S(1)} copy-done((f32[5,12,4,2,4,4]{1,5,4,3,2,0:T(4,128)S(1)}, f32[5,12,4,2,4,4]{1,5,4,3,2,0:T(4,128)}, u32[]{:S(2)}) %copy-start.2) | copy-done | bytes 30744
  2.8 0.0 copy-start.3
  2.8 0.8 %copy-done.3 = f32[12,4,2,4,4]{0,4,3,2,1:T(4,128)S(1)} copy-done((f32[12,4,2,4,4]{0,4,3,2,1:T(4,128)S(1)}, f32[12,4,2,4,4]{0,4,3,2,1:T(4,128)}, u32[]{:S(2)}) %copy-start.3) | copy-done | bytes 6168
  3.6 0.0 copy-start.4
  3.6 0.7 copy-done.4
  4.3 0.0 copy-start.5
  4.3 0.7 copy-done.5
  5.0 4.3 %cloud_models.1 = (f32[32,120,128]{2,1,0:T(8,128)S(1)}, f32[128,128]{1,0:T(8,128)S(1)}, f32[8,128]{1,0:T(8,128)S(1)}, f32[8,128]{1,0:T(8,128)S(1)}) custom-call(f32[5,12,32,128]{3,2,1,0:T(8,128)S(1)} %copy-done.1, f32[5,128,12]{2,1,0:T(8,128)S(1)} %bitcast.14, f32[128,12]{1,0:T(8,128)S(1)} %bitcast.15, s32[1,128]{1,0:T(1,128)S(1)} %bitcast.16, ...), custom_call_target="tpu_custom_call" | custom-call | tf_op jit(solution)/shard_map/cloud_models/pallas_call | solution.py:259
  9.3 0.0 copy-start
  9.3 1.3 %copy-done = f32[32,120,128]{2,1,0:T(8,128)} copy-done((f32[32,120,128]{2,1,0:T(8,128)}, f32[32,120,128]{2,1,0:T(8,128)S(1)}, u32[]{:S(2)}) %copy-start) | copy-done | bytes 1966104
  10.6 6.3 %all-to-all-start = ((f32[32,120,128]{2,1,0:T(8,128)}), f32[32,120,128]{2,1,0:T(8,128)S(1)}, u32[]{:S(2)}, u32[]{:S(2)}) async-start(f32[32,120,128]{2,1,0:T(8,128)} %copy-done), calls=%async_computation | async-start | bytes 3932160 | tf_op jit(solution)/shard_map/all_to_all | solution.py:282
  16.8 1.2 %collective-permute-start = (f32[8,128]{1,0:T(8,128)S(1)}, f32[8,128]{1,0:T(8,128)S(1)}, u32[]{:S(2)}, u32[]{:S(2)}) collective-permute-start(f32[8,128]{1,0:T(8,128)S(1)} %get-tuple-element.11), channel_id=1, source_target_pairs={{0,4},{4,8},{8,12},{12,16},{16,20},{20,24},{24,28},{28,0},{1,5},{5... | collective-permute-start | bytes 12296 | tf_op jit(solution)/shard_map/ppermute | solution.py:239
  18.1 1.2 %collective-permute-start.1 = (f32[8,128]{1,0:T(8,128)S(1)}, f32[8,128]{1,0:T(8,128)S(1)}, u32[]{:S(2)}, u32[]{:S(2)}) collective-permute-start(f32[8,128]{1,0:T(8,128)S(1)} %get-tuple-element.12), channel_id=1, source_target_pairs={{0,28},{4,0},{8,4},{12,8},{16,12},{20,16},{24,20},{28,24},{1,29},{... | collective-permute-start | bytes 12296 | tf_op jit(solution)/shard_map/ppermute | solution.py:239
  19.2 42.0 %collective-permute-done.west_ref = f32[8,128]{1,0:T(8,128)S(1)} collective-permute-done((f32[8,128]{1,0:T(8,128)S(1)}, f32[8,128]{1,0:T(8,128)S(1)}, u32[]{:S(2)}, u32[]{:S(2)}) %collective-permute-start) | collective-permute-done | bytes 4128 | tf_op jit(solution)/shard_map/ppermute | solution.py:239
  61.2 0.0 collective-permute-done.1.east_ref
  61.3 2.2 %collective-permute-start.2 = (f32[16,128]{1,0:T(8,128)S(1)}, f32[16,128]{1,0:T(8,128)S(1)}, u32[]{:S(2)}, u32[]{:S(2)}) collective-permute-start(f32[16,128]{1,0:T(8,128)S(1)} %get-tuple-element.14), channel_id=1, source_target_pairs={{0,1},{1,2},{2,3},{3,0},{4,5},{5,6},{6,7},{7,4},{8,9},{9,10},{10,1... | collective-permute-start | bytes 24584 | tf_op jit(solution)/shard_map/ppermute | solution.py:239
  63.5 0.0 collective-permute-start.3
  63.5 0.8 %collective-permute-done.2.south_ref = f32[16,128]{1,0:T(8,128)S(1)} collective-permute-done((f32[16,128]{1,0:T(8,128)S(1)}, f32[16,128]{1,0:T(8,128)S(1)}, u32[]{:S(2)}, u32[]{:S(2)}) %collective-permute-start.2) | collective-permute-done | bytes 8224 | tf_op jit(solution)/shard_map/ppermute | solution.py:239
  64.3 2.3 %collective-permute-done.3.north_ref = f32[16,128]{1,0:T(8,128)S(1)} collective-permute-done((f32[16,128]{1,0:T(8,128)S(1)}, f32[16,128]{1,0:T(8,128)S(1)}, u32[]{:S(2)}, u32[]{:S(2)}) %collective-permute-start.3) | collective-permute-done | bytes 8224 | tf_op jit(solution)/shard_map/ppermute | solution.py:239
  66.6 1.0 %edge_sum_second.1 = f32[5,128,12]{2,1,0:T(8,128)} custom-call(f32[128,128]{1,0:T(8,128)S(1)} %get-tuple-element.13.sum_ref, f32[16,128]{1,0:T(8,128)S(1)} %collective-permute-done.2.south_ref, f32[16,128]{1,0:T(8,128)S(1)} %collective-permute-done.3.north_ref), custom_call_target="tpu_custom_call" | custom-call | flops 100000 | bytes 100000 | tf_op jit(solution)/shard_map/edge_sum_second/pallas_call | solution.py:296
  67.6 0.0 all-to-all-done
  67.6 1.5 %cloud_slots.1 = f32[1920,256]{1,0:T(8,128)} custom-call(f32[3840,128]{1,0:T(8,128)S(1)} %bitcast.13), custom_call_target="tpu_custom_call" | custom-call | tf_op jit(solution)/shard_map/cloud_slots/pallas_call | solution.py:305
  (1 shorter events, 0.0 us)
Async XLA Ops:
  0.6 1.2 %copy-start.1 = (f32[5,12,32,128]{3,2,1,0:T(8,128)S(1)}, f32[5,12,32,128]{3,2,1,0:T(8,128)}, u32[]{:S(2)}) copy-start(f32[5,12,32,128]{3,2,1,0:T(8,128)} %refs_0_.1) | copy-start | bytes 2949124
  1.8 1.0 %copy-start.2 = (f32[5,12,4,2,4,4]{1,5,4,3,2,0:T(4,128)S(1)}, f32[5,12,4,2,4,4]{1,5,4,3,2,0:T(4,128)}, u32[]{:S(2)}) copy-start(f32[5,12,4,2,4,4]{1,5,4,3,2,0:T(4,128)} %param.6) | copy-start | bytes 92164
  2.8 0.8 %copy-start.3 = (f32[12,4,2,4,4]{0,4,3,2,1:T(4,128)S(1)}, f32[12,4,2,4,4]{0,4,3,2,1:T(4,128)}, u32[]{:S(2)}) copy-start(f32[12,4,2,4,4]{0,4,3,2,1:T(4,128)} %param.7) | copy-start | bytes 18436
  3.6 0.7 copy-start.4
  4.3 0.7 copy-start.5
  9.3 1.3 %copy-start = (f32[32,120,128]{2,1,0:T(8,128)}, f32[32,120,128]{2,1,0:T(8,128)S(1)}, u32[]{:S(2)}) copy-start(f32[32,120,128]{2,1,0:T(8,128)S(1)} %get-tuple-element.9) | copy-start | bytes 5898244
  10.6 57.0 %all-to-all-start = ((f32[32,120,128]{2,1,0:T(8,128)}), f32[32,120,128]{2,1,0:T(8,128)S(1)}, u32[]{:S(2)}, u32[]{:S(2)}) async-start(f32[32,120,128]{2,1,0:T(8,128)} %copy-done), calls=%async_computation | async-start | bytes 3932160 | tf_op jit(solution)/shard_map/all_to_all | solution.py:282
  16.8 44.4 %collective-permute-start = (f32[8,128]{1,0:T(8,128)S(1)}, f32[8,128]{1,0:T(8,128)S(1)}, u32[]{:S(2)}, u32[]{:S(2)}) collective-permute-start(f32[8,128]{1,0:T(8,128)S(1)} %get-tuple-element.11), channel_id=1, source_target_pairs={{0,4},{4,8},{8,12},{12,16},{16,20},{20,24},{24,28},{28,0},{1,5},{5... | collective-permute-start | bytes 12296 | tf_op jit(solution)/shard_map/ppermute | solution.py:239
  18.1 43.2 %collective-permute-start.1 = (f32[8,128]{1,0:T(8,128)S(1)}, f32[8,128]{1,0:T(8,128)S(1)}, u32[]{:S(2)}, u32[]{:S(2)}) collective-permute-start(f32[8,128]{1,0:T(8,128)S(1)} %get-tuple-element.12), channel_id=1, source_target_pairs={{0,28},{4,0},{8,4},{12,8},{16,12},{20,16},{24,20},{28,24},{1,29},{... | collective-permute-start | bytes 12296 | tf_op jit(solution)/shard_map/ppermute | solution.py:239
  61.3 3.0 %collective-permute-start.2 = (f32[16,128]{1,0:T(8,128)S(1)}, f32[16,128]{1,0:T(8,128)S(1)}, u32[]{:S(2)}, u32[]{:S(2)}) collective-permute-start(f32[16,128]{1,0:T(8,128)S(1)} %get-tuple-element.14), channel_id=1, source_target_pairs={{0,1},{1,2},{2,3},{3,0},{4,5},{5,6},{6,7},{7,4},{8,9},{9,10},{10,1... | collective-permute-start | bytes 24584 | tf_op jit(solution)/shard_map/ppermute | solution.py:239
  63.5 3.1 %collective-permute-start.3 = (f32[16,128]{1,0:T(8,128)S(1)}, f32[16,128]{1,0:T(8,128)S(1)}, u32[]{:S(2)}, u32[]{:S(2)}) collective-permute-start(f32[16,128]{1,0:T(8,128)S(1)} %get-tuple-element.15), channel_id=1, source_target_pairs={{0,3},{1,0},{2,1},{3,2},{4,7},{5,4},{6,5},{7,6},{8,11},{9,8},{10,9... | collective-permute-start | bytes 24584 | tf_op jit(solution)/shard_map/ppermute | solution.py:239

commit v2 on v1

--- a/solution.py
+++ b/solution.py
@@ -16,7 +16,7 @@
 nudging = 0.5
 
 NT = (((1,), (1,)), ((), ()))
-VMEM_LIMIT = 48 * 1024 * 1024
+MIB = 1024 * 1024
 
 
 def substep_level(values_at, profile_row, z, levels, field_count, active):
@@ -226,8 +226,8 @@
         copy.wait()
 
 
-def params(**more):
-    return pltpu.CompilerParams(vmem_limit_bytes=VMEM_LIMIT, **more)
+def params(mib):
+    return pltpu.CompilerParams(vmem_limit_bytes=mib * MIB)
 
 
 def cost(flops, byte_count):
@@ -276,7 +276,7 @@
             pltpu.SemaphoreType.DMA((levels * width // owned,)),
             pltpu.SemaphoreType.DMA((field_count,)),
         ],
-        compiler_params=params(),
+        compiler_params=params(63),
         name="cloud_models",
     )(crm_state, gcm_nodes, mass_nodes, dest.reshape(1, owned), cost_class.reshape(1, owned))
     received = lax.all_to_all(
@@ -287,7 +287,7 @@
     summed, low, high = pl.pallas_call(
         functools.partial(kernel_x, *sizes),
         out_shape=(square, face_y, face_y),
-        compiler_params=params(),
+        compiler_params=params(8),
         cost_estimate=cost(10**5, 10**5),
         name="edge_sum_first",
     )(nodes, west, east)
@@ -297,7 +297,7 @@
         functools.partial(kernel_y, *sizes),
         out_shape=jax.ShapeDtypeStruct((field_count, owned, levels), f32),
         scratch_shapes=[pltpu.VMEM((owned, owned), f32)],
-        compiler_params=params(),
+        compiler_params=params(8),
         cost_estimate=cost(10**5, 10**5),
         name="edge_sum_second",
     )(summed, south, north)
@@ -308,7 +308,7 @@
         out_specs=in_hbm,
         out_shape=jax.ShapeDtypeStruct((values, slots), f32),
         scratch_shapes=[pltpu.VMEM((values, slots), f32), pltpu.SemaphoreType.DMA((values // owned,))],
-        compiler_params=params(),
+        compiler_params=params(16),
         name="cloud_slots",
     )(received.reshape(-1, owned))
     return cloud.reshape(field_count, levels, width, slots), gcm_out

time: 69.4 us -> 64.3 us (0.927)
  local copies, waits for them, and re-layouts: 5.58 us -> 0.01 us
    unnamed x12 -> x6, local copies, waits for them, and re-layouts: 5.58 us -> 0.01 us
where the time goes in v2:
time: 64.3 us; the launch traced here: 64.1 us
  waiting for transfers between devices  45.1 us (70%)
  starting transfers between devices  10.9 us (17%)
  Pallas kernels  7.42 us (12%)
  between operations  0.69 us (1%)
    ppermute x4, waiting for transfers between devices, shift(): lax.ppermute(face, axis, [(i, (i + by) % count) for i in range(count)])  45.1 us
    all_to_all x1, starting transfers between devices, body(): lax.all_to_all(send, ('ex', 'ey'), split_axis=0, concat_axis=0, tiled=True)  6.26 us
    pallas_call x1, Pallas kernels, body(): pl.pallas_call(functools.partial(kernel_a, devices, capacity, *sizes), ou...  4.89 us
    ppermute x4, starting transfers between devices, shift(): lax.ppermute(face, axis, [(i, (i + by) % count) for i in range(count)])  4.66 us
    pallas_call x1, Pallas kernels, body(): pl.pallas_call(functools.partial(kernel_out, devices, capacity), in_specs...  1.49 us
  transfers between devices with their start and end apart: 5, of which 3 were waited for; matrix products, arithmetic and copies ran while one was open for 0% of the time, Pallas kernels for 2%

profile of v2, /device:TPU:17, one launch (start us, length us, event | category | flops | bytes accessed | tf_op | source)
XLA Modules:
  0.0 64.1 jit_solution(3014910557096594426)
XLA Ops:
  0.6 4.9 %cloud_models.1 = (f32[32,120,128]{2,1,0:T(8,128)}, f32[128,128]{1,0:T(8,128)}, f32[8,128]{1,0:T(8,128)}, f32[8,128]{1,0:T(8,128)}) custom-call(f32[5,12,32,128]{3,2,1,0:T(8,128)} %refs_0_.1, f32[5,128,12]{2,1,0:T(8,128)} %bitcast.16, f32[128,12]{1,0:T(8,128)} %bitcast.17, s32[1,128]{1,0:T(1,128)} %bitcast.18, s32[1,128]{1,0:T(1,128)} %bitcast.19), custom_call_target="tpu_custom_call" | custom-call | tf_op jit(solution)/shard_map/cloud_models/pallas_call | solution.py:259
  5.5 0.0 copy-start.2
  5.5 0.0 copy-start.1
  5.6 0.0 copy-start
  5.6 6.3 %all-to-all-start = ((f32[32,120,128]{2,1,0:T(8,128)}), f32[32,120,128]{2,1,0:T(8,128)S(1)}, u32[]{:S(2)}, u32[]{:S(2)}) async-start(f32[32,120,128]{2,1,0:T(8,128)} %get-tuple-element.9), calls=%async_computation | async-start | bytes 3932160 | tf_op jit(solution)/shard_map/all_to_all | solution.py:282
  11.8 0.0 copy-done.2
  11.8 1.2 %collective-permute-start = (f32[8,128]{1,0:T(8,128)S(1)}, f32[8,128]{1,0:T(8,128)S(1)}, u32[]{:S(2)}, u32[]{:S(2)}) collective-permute-start(f32[8,128]{1,0:T(8,128)S(1)} %copy-done.2), channel_id=1, source_target_pairs={{0,4},{4,8},{8,12},{12,16},{16,20},{20,24},{24,28},{28,0},{1,5},{5... | collective-permute-start | bytes 12296 | tf_op jit(solution)/shard_map/ppermute | solution.py:239
  13.1 0.0 copy-done.1
  13.1 1.2 %collective-permute-start.1 = (f32[8,128]{1,0:T(8,128)S(1)}, f32[8,128]{1,0:T(8,128)S(1)}, u32[]{:S(2)}, u32[]{:S(2)}) collective-permute-start(f32[8,128]{1,0:T(8,128)S(1)} %copy-done.1), channel_id=1, source_target_pairs={{0,28},{4,0},{8,4},{12,8},{16,12},{20,16},{24,20},{28,24},{1,29},{... | collective-permute-start | bytes 12296 | tf_op jit(solution)/shard_map/ppermute | solution.py:239
  14.3 42.0 %collective-permute-done.west_ref = f32[8,128]{1,0:T(8,128)S(1)} collective-permute-done((f32[8,128]{1,0:T(8,128)S(1)}, f32[8,128]{1,0:T(8,128)S(1)}, u32[]{:S(2)}, u32[]{:S(2)}) %collective-permute-start) | collective-permute-done | bytes 4128 | tf_op jit(solution)/shard_map/ppermute | solution.py:239
  56.2 0.0 collective-permute-done.1.east_ref
  56.2 0.0 copy-done
  56.3 2.2 %collective-permute-start.2 = (f32[16,128]{1,0:T(8,128)S(1)}, f32[16,128]{1,0:T(8,128)S(1)}, u32[]{:S(2)}, u32[]{:S(2)}) collective-permute-start(f32[16,128]{1,0:T(8,128)S(1)} %get-tuple-element.14), channel_id=1, source_target_pairs={{0,1},{1,2},{2,3},{3,0},{4,5},{5,6},{6,7},{7,4},{8,9},{9,10},{10,1... | collective-permute-start | bytes 24584 | tf_op jit(solution)/shard_map/ppermute | solution.py:239
  58.5 0.0 collective-permute-start.3
  58.5 0.8 %collective-permute-done.2.south_ref = f32[16,128]{1,0:T(8,128)S(1)} collective-permute-done((f32[16,128]{1,0:T(8,128)S(1)}, f32[16,128]{1,0:T(8,128)S(1)}, u32[]{:S(2)}, u32[]{:S(2)}) %collective-permute-start.2) | collective-permute-done | bytes 8224 | tf_op jit(solution)/shard_map/ppermute | solution.py:239
  59.3 2.3 %collective-permute-done.3.north_ref = f32[16,128]{1,0:T(8,128)S(1)} collective-permute-done((f32[16,128]{1,0:T(8,128)S(1)}, f32[16,128]{1,0:T(8,128)S(1)}, u32[]{:S(2)}, u32[]{:S(2)}) %collective-permute-start.3) | collective-permute-done | bytes 8224 | tf_op jit(solution)/shard_map/ppermute | solution.py:239
  61.6 1.0 %edge_sum_second.1 = f32[5,128,12]{2,1,0:T(8,128)} custom-call(f32[128,128]{1,0:T(8,128)S(1)} %get-tuple-element.13.sum_ref, f32[16,128]{1,0:T(8,128)S(1)} %collective-permute-done.2.south_ref, f32[16,128]{1,0:T(8,128)S(1)} %collective-permute-done.3.north_ref), custom_call_target="tpu_custom_call" | custom-call | flops 100000 | bytes 100000 | tf_op jit(solution)/shard_map/edge_sum_second/pallas_call | solution.py:296
  62.6 0.0 all-to-all-done
  62.6 1.5 %cloud_slots.1 = f32[1920,256]{1,0:T(8,128)} custom-call(f32[3840,128]{1,0:T(8,128)S(1)} %bitcast.13), custom_call_target="tpu_custom_call" | custom-call | tf_op jit(solution)/shard_map/cloud_slots/pallas_call | solution.py:305
  (1 shorter events, 0.0 us)
Async XLA Ops:
  5.5 6.3 %copy-start.2 = (f32[8,128]{1,0:T(8,128)S(1)}, f32[8,128]{1,0:T(8,128)}, u32[]{:S(2)}) copy-start(f32[8,128]{1,0:T(8,128)} %get-tuple-element.11) | copy-start | bytes 12292
  5.5 7.5 %copy-start.1 = (f32[8,128]{1,0:T(8,128)S(1)}, f32[8,128]{1,0:T(8,128)}, u32[]{:S(2)}) copy-start(f32[8,128]{1,0:T(8,128)} %get-tuple-element.12) | copy-start | bytes 12292
  5.6 50.7 %copy-start = (f32[128,128]{1,0:T(8,128)S(1)}, f32[128,128]{1,0:T(8,128)}, u32[]{:S(2)}) copy-start(f32[128,128]{1,0:T(8,128)} %get-tuple-element.10.nodes_ref) | copy-start | bytes 196612
  5.6 57.1 %all-to-all-start = ((f32[32,120,128]{2,1,0:T(8,128)}), f32[32,120,128]{2,1,0:T(8,128)S(1)}, u32[]{:S(2)}, u32[]{:S(2)}) async-start(f32[32,120,128]{2,1,0:T(8,128)} %get-tuple-element.9), calls=%async_computation | async-start | bytes 3932160 | tf_op jit(solution)/shard_map/all_to_all | solution.py:282
  11.8 44.4 %collective-permute-start = (f32[8,128]{1,0:T(8,128)S(1)}, f32[8,128]{1,0:T(8,128)S(1)}, u32[]{:S(2)}, u32[]{:S(2)}) collective-permute-start(f32[8,128]{1,0:T(8,128)S(1)} %copy-done.2), channel_id=1, source_target_pairs={{0,4},{4,8},{8,12},{12,16},{16,20},{20,24},{24,28},{28,0},{1,5},{5... | collective-permute-start | bytes 12296 | tf_op jit(solution)/shard_map/ppermute | solution.py:239
  13.1 43.2 %collective-permute-start.1 = (f32[8,128]{1,0:T(8,128)S(1)}, f32[8,128]{1,0:T(8,128)S(1)}, u32[]{:S(2)}, u32[]{:S(2)}) collective-permute-start(f32[8,128]{1,0:T(8,128)S(1)} %copy-done.1), channel_id=1, source_target_pairs={{0,28},{4,0},{8,4},{12,8},{16,12},{20,16},{24,20},{28,24},{1,29},{... | collective-permute-start | bytes 12296 | tf_op jit(solution)/shard_map/ppermute | solution.py:239
  56.3 3.0 %collective-permute-start.2 = (f32[16,128]{1,0:T(8,128)S(1)}, f32[16,128]{1,0:T(8,128)S(1)}, u32[]{:S(2)}, u32[]{:S(2)}) collective-permute-start(f32[16,128]{1,0:T(8,128)S(1)} %get-tuple-element.14), channel_id=1, source_target_pairs={{0,1},{1,2},{2,3},{3,0},{4,5},{5,6},{6,7},{7,4},{8,9},{9,10},{10,1... | collective-permute-start | bytes 24584 | tf_op jit(solution)/shard_map/ppermute | solution.py:239
  58.5 3.1 %collective-permute-start.3 = (f32[16,128]{1,0:T(8,128)S(1)}, f32[16,128]{1,0:T(8,128)S(1)}, u32[]{:S(2)}, u32[]{:S(2)}) collective-permute-start(f32[16,128]{1,0:T(8,128)S(1)} %get-tuple-element.15), channel_id=1, source_target_pairs={{0,3},{1,0},{2,1},{3,2},{4,7},{5,4},{6,5},{7,6},{8,11},{9,8},{10,9... | collective-permute-start | bytes 24584 | tf_op jit(solution)/shard_map/ppermute | solution.py:239

commit v3 on v2

--- a/solution.py
+++ b/solution.py
@@ -145,66 +145,66 @@
     return sends
 
 
-def edges_x(elx, ely, side, nodes_ref, low_ref, high_ref):
+def edges_y(elx, ely, side, nodes_ref, low_ref, high_ref):
     step = side * side
-    for b in range(ely):
-        low_ref[b * side:(b + 1) * side, :] = nodes_ref[b * step:b * step + side, :]
-        start = (elx - 1) * ely * step + b * step + (side - 1) * side
-        high_ref[b * side:(b + 1) * side, :] = nodes_ref[start:start + side, :]
+    for a in range(elx):
+        first = a * ely * step
+        final = (a * ely + ely - 1) * step + side - 1
+        low_ref[a * side:(a + 1) * side, :] = nodes_ref[pl.ds(first, side, stride=side), :]
+        high_ref[a * side:(a + 1) * side, :] = nodes_ref[pl.ds(final, side, stride=side), :]
 
 
 def kernel_a(devices, capacity, elx, ely, side, *refs):
     sends = cloud_kernel(devices, capacity, *refs)
-    edges_x(elx, ely, side, *refs[6:9])
+    edges_y(elx, ely, side, *refs[6:9])
     for copy in sends:
         copy.wait()
 
 
-def kernel_x(elx, ely, side, nodes_ref, west_ref, east_ref, sum_ref, low_ref, high_ref):
+def kernel_y(elx, ely, side, nodes_ref, south_ref, north_ref, sum_ref, low_ref, high_ref):
     step = side * side
     sum_ref[...] = nodes_ref[...]
+    for a in range(elx):
+        for b in range(ely):
+            base = (a * ely + b) * step
+            if b > 0:
+                gain = nodes_ref[pl.ds(base - step + side - 1, side, stride=side), :]
+            else:
+                gain = south_ref[a * side:(a + 1) * side, :]
+            here = pl.ds(base, side, stride=side)
+            sum_ref[here, :] = nodes_ref[here, :] + gain
+            if b + 1 < ely:
+                gain = nodes_ref[pl.ds(base + step, side, stride=side), :]
+            else:
+                gain = north_ref[a * side:(a + 1) * side, :]
+            here = pl.ds(base + side - 1, side, stride=side)
+            sum_ref[here, :] = nodes_ref[here, :] + gain
+    for b in range(ely):
+        low_ref[b * side:(b + 1) * side, :] = sum_ref[b * step:b * step + side, :]
+        start = (elx - 1) * ely * step + b * step + (side - 1) * side
+        high_ref[b * side:(b + 1) * side, :] = sum_ref[start:start + side, :]
+
+
+def kernel_x(elx, ely, side, sum_ref, west_ref, east_ref, out_ref, full_ref):
+    step = side * side
+    field_count, nodes, levels = out_ref.shape
+    full_ref[...] = sum_ref[...]
     for a in range(elx):
         for b in range(ely):
             base = (a * ely + b) * step
             last = base + (side - 1) * side
             if a > 0:
                 before = ((a - 1) * ely + b) * step + (side - 1) * side
-                gain = nodes_ref[before:before + side, :]
+                gain = sum_ref[before:before + side, :]
             else:
                 gain = west_ref[b * side:(b + 1) * side, :]
-            sum_ref[base:base + side, :] = nodes_ref[base:base + side, :] + gain
+            full_ref[base:base + side, :] = sum_ref[base:base + side, :] + gain
             if a + 1 < elx:
                 after = ((a + 1) * ely + b) * step
-                gain = nodes_ref[after:after + side, :]
+                gain = sum_ref[after:after + side, :]
             else:
                 gain = east_ref[b * side:(b + 1) * side, :]
-            sum_ref[last:last + side, :] = nodes_ref[last:last + side, :] + gain
-    for a in range(elx):
-        first = a * ely * step
-        final = (a * ely + ely - 1) * step + side - 1
-        low_ref[a * side:(a + 1) * side, :] = sum_ref[pl.ds(first, side, stride=side), :]
-        high_ref[a * side:(a + 1) * side, :] = sum_ref[pl.ds(final, side, stride=side), :]
-
-
-def kernel_y(elx, ely, side, sum_ref, south_ref, north_ref, out_ref, full_ref):
-    step = side * side
-    field_count, nodes, levels = out_ref.shape
-    full_ref[...] = sum_ref[...]
-    for a in range(elx):
-        for b in range(ely):
-            base = (a * ely + b) * step
-            if b > 0:
-                gain = sum_ref[pl.ds(base - step + side - 1, side, stride=side), :]
-            else:
-                gain = south_ref[a * side:(a + 1) * side, :]
-            here = pl.ds(base, side, stride=side)
-            full_ref[here, :] = sum_ref[here, :] + gain
-            if b + 1 < ely:
-                gain = sum_ref[pl.ds(base + step, side, stride=side), :]
-            else:
-                gain = north_ref[a * side:(a + 1) * side, :]
-            here = pl.ds(base + side - 1, side, stride=side)
-            full_ref[here, :] = sum_ref[here, :] + gain
+            full_ref[last:last + side, :] = sum_ref[last:last + side, :] + gain
     full = full_ref[...]
     divisor = full[:, field_count * levels:(field_count + 1) * levels]
     for f in range(field_count):
@@ -258,7 +258,7 @@
     square = jax.ShapeDtypeStruct((owned, owned), f32)
     send, nodes, low, high = pl.pallas_call(
         functools.partial(kernel_a, devices, capacity, *sizes),
-        out_shape=(jax.ShapeDtypeStruct(packed, f32), square, face_x, face_x),
+        out_shape=(jax.ShapeDtypeStruct(packed, f32), square, face_y, face_y),
         in_specs=[in_hbm] * 5,
         out_specs=(in_hbm, in_vmem, in_vmem, in_vmem),
         scratch_shapes=[
@@ -282,25 +282,25 @@
     received = lax.all_to_all(
         send, ("ex", "ey"), split_axis=0, concat_axis=0, tiled=True
     )
+    north = shift(low, "ey", -1)
+    south = shift(high, "ey", 1)
+    summed, low, high = pl.pallas_call(
+        functools.partial(kernel_y, *sizes),
+        out_shape=(square, face_x, face_x),
+        compiler_params=params(8),
+        cost_estimate=cost(10**5, 10**5),
+        name="edge_sum_second",
+    )(nodes, south, north)
     east = shift(low, "ex", -1)
     west = shift(high, "ex", 1)
-    summed, low, high = pl.pallas_call(
+    gcm_out = pl.pallas_call(
         functools.partial(kernel_x, *sizes),
-        out_shape=(square, face_y, face_y),
-        compiler_params=params(8),
-        cost_estimate=cost(10**5, 10**5),
-        name="edge_sum_first",
-    )(nodes, west, east)
-    north = shift(low, "ey", -1)
-    south = shift(high, "ey", 1)
-    gcm_out = pl.pallas_call(
-        functools.partial(kernel_y, *sizes),
         out_shape=jax.ShapeDtypeStruct((field_count, owned, levels), f32),
         scratch_shapes=[pltpu.VMEM((owned, owned), f32)],
         compiler_params=params(8),
         cost_estimate=cost(10**5, 10**5),
-        name="edge_sum_second",
-    )(summed, south, north)
+        name="edge_sum_first",
+    )(summed, west, east)
     gcm_out = gcm_out.reshape(field_count, elx, ely, side, side, levels).transpose(0, 5, 1, 2, 3, 4)
     cloud = pl.pallas_call(
         functools.partial(kernel_out, devices, capacity),

time: 64.3 us -> 60.6 us (0.942)
  the two profiles are of different devices: /device:TPU:17 before, /device:TPU:0 now
where the time goes in v3:
time: 60.6 us; the launch traced here: 60.4 us
  waiting for transfers between devices  34 us (56%)
  starting transfers between devices  18.2 us (30%)
  Pallas kernels  7.43 us (12%)
  between operations  0.69 us (1%)
    ppermute x4, waiting for transfers between devices, shift(): lax.ppermute(face, axis, [(i, (i + by) % count) for i in range(count)])  26.4 us
    ppermute x4, starting transfers between devices, shift(): lax.ppermute(face, axis, [(i, (i + by) % count) for i in range(count)])  10.9 us
    all_to_all x1, waiting for transfers between devices, body(): lax.all_to_all(send, ('ex', 'ey'), split_axis=0, concat_axis=0, tiled=True)  7.56 us
    all_to_all x1, starting transfers between devices, body(): lax.all_to_all(send, ('ex', 'ey'), split_axis=0, concat_axis=0, tiled=True)  7.3 us
    pallas_call x1, Pallas kernels, body(): pl.pallas_call(functools.partial(kernel_a, devices, capacity, *sizes), ou...  4.9 us
    pallas_call x1, Pallas kernels, body(): pl.pallas_call(functools.partial(kernel_out, devices, capacity), in_specs...  1.49 us
  transfers between devices with their start and end apart: 5, of which 3 were waited for; matrix products, arithmetic and copies ran while one was open for 0% of the time, Pallas kernels for 2%

profile of v3, /device:TPU:0, one launch (start us, length us, event | category | flops | bytes accessed | tf_op | source)
XLA Modules:
  0.0 60.4 jit_solution(18002048641426506544)
XLA Ops:
  0.6 4.9 %cloud_models.1 = (f32[32,120,128]{2,1,0:T(8,128)}, f32[128,128]{1,0:T(8,128)}, f32[16,128]{1,0:T(8,128)}, f32[16,128]{1,0:T(8,128)}) custom-call(f32[5,12,32,128]{3,2,1,0:T(8,128)} %refs_0_.1, f32[5,128,12]{2,1,0:T(8,128)} %bitcast.16, f32[128,12]{1,0:T(8,128)} %bitcast.17, s32[1,128]{1,0:T(1,128)} %bitcast.18, s32[1,128]{1,0:T(1,128)} %bitcast.19), custom_call_target="tpu_custom_call" | custom-call | tf_op jit(solution)/shard_map/cloud_models/pallas_call | solution.py:259
  5.5 0.0 copy-start.2
  5.6 0.0 copy-start.1
  5.6 0.0 copy-start
  5.6 7.3 %all-to-all-start = ((f32[32,120,128]{2,1,0:T(8,128)}), f32[32,120,128]{2,1,0:T(8,128)S(1)}, u32[]{:S(2)}, u32[]{:S(2)}) async-start(f32[32,120,128]{2,1,0:T(8,128)} %get-tuple-element.9), calls=%async_computation | async-start | bytes 3932160 | tf_op jit(solution)/shard_map/all_to_all | solution.py:282
  12.9 0.0 copy-done.2
  12.9 0.3 collective-permute-start
  13.2 0.0 copy-done.1
  13.2 1.5 %collective-permute-start.1 = (f32[16,128]{1,0:T(8,128)S(1)}, f32[16,128]{1,0:T(8,128)S(1)}, u32[]{:S(2)}, u32[]{:S(2)}) collective-permute-start(f32[16,128]{1,0:T(8,128)S(1)} %copy-done.1), channel_id=1, source_target_pairs={{0,3},{1,0},{2,1},{3,2},{4,7},{5,4},{6,5},{7,6},{8,11},{9,8},{10,9... | collective-permute-start | bytes 24584 | tf_op jit(solution)/shard_map/ppermute | solution.py:239
  14.7 3.9 %collective-permute-done.south_ref = f32[16,128]{1,0:T(8,128)S(1)} collective-permute-done((f32[16,128]{1,0:T(8,128)S(1)}, f32[16,128]{1,0:T(8,128)S(1)}, u32[]{:S(2)}, u32[]{:S(2)}) %collective-permute-start) | collective-permute-done | bytes 8224 | tf_op jit(solution)/shard_map/ppermute | solution.py:239
  18.6 0.0 collective-permute-done.1.north_ref
  18.6 0.0 copy-done
  18.6 8.7 %collective-permute-start.2 = (f32[8,128]{1,0:T(8,128)S(1)}, f32[8,128]{1,0:T(8,128)S(1)}, u32[]{:S(2)}, u32[]{:S(2)}) collective-permute-start(f32[8,128]{1,0:T(8,128)S(1)} %get-tuple-element.14), channel_id=1, source_target_pairs={{0,4},{4,8},{8,12},{12,16},{16,20},{20,24},{24,28},{28,0},{1,5},{5... | collective-permute-start | bytes 12296 | tf_op jit(solution)/shard_map/ppermute | solution.py:239
  27.3 0.4 collective-permute-start.3
  27.7 22.6 %collective-permute-done.2.west_ref = f32[8,128]{1,0:T(8,128)S(1)} collective-permute-done((f32[8,128]{1,0:T(8,128)S(1)}, f32[8,128]{1,0:T(8,128)S(1)}, u32[]{:S(2)}, u32[]{:S(2)}) %collective-permute-start.2) | collective-permute-done | bytes 4128 | tf_op jit(solution)/shard_map/ppermute | solution.py:239
  50.3 0.0 collective-permute-done.3.east_ref
  50.3 1.0 %edge_sum_first.1 = f32[5,128,12]{2,1,0:T(8,128)} custom-call(f32[128,128]{1,0:T(8,128)S(1)} %get-tuple-element.13.sum_ref, f32[8,128]{1,0:T(8,128)S(1)} %collective-permute-done.2.west_ref, f32[8,128]{1,0:T(8,128)S(1)} %collective-permute-done.3.east_ref), custom_call_target="tpu_custom_call" | custom-call | flops 100000 | bytes 100000 | tf_op jit(solution)/shard_map/edge_sum_first/pallas_call | solution.py:296
  51.3 7.6 %all-to-all-done = f32[32,120,128]{2,1,0:T(8,128)S(1)} async-done(((f32[32,120,128]{2,1,0:T(8,128)}), f32[32,120,128]{2,1,0:T(8,128)S(1)}, u32[]{:S(2)}, u32[]{:S(2)}) %all-to-all-start) | async-done | bytes 1966112 | tf_op jit(solution)/shard_map/all_to_all | solution.py:282
  58.9 1.5 %cloud_slots.1 = f32[1920,256]{1,0:T(8,128)} custom-call(f32[3840,128]{1,0:T(8,128)S(1)} %bitcast.13), custom_call_target="tpu_custom_call" | custom-call | tf_op jit(solution)/shard_map/cloud_slots/pallas_call | solution.py:305
  (1 shorter events, 0.0 us)
Async XLA Ops:
  5.5 7.3 %copy-start.2 = (f32[16,128]{1,0:T(8,128)S(1)}, f32[16,128]{1,0:T(8,128)}, u32[]{:S(2)}) copy-start(f32[16,128]{1,0:T(8,128)} %get-tuple-element.11) | copy-start | bytes 24580
  5.6 7.7 %copy-start.1 = (f32[16,128]{1,0:T(8,128)S(1)}, f32[16,128]{1,0:T(8,128)}, u32[]{:S(2)}) copy-start(f32[16,128]{1,0:T(8,128)} %get-tuple-element.12) | copy-start | bytes 24580
  5.6 13.0 %copy-start = (f32[128,128]{1,0:T(8,128)S(1)}, f32[128,128]{1,0:T(8,128)}, u32[]{:S(2)}) copy-start(f32[128,128]{1,0:T(8,128)} %get-tuple-element.10.nodes_ref) | copy-start | bytes 196612
  5.6 53.3 %all-to-all-start = ((f32[32,120,128]{2,1,0:T(8,128)}), f32[32,120,128]{2,1,0:T(8,128)S(1)}, u32[]{:S(2)}, u32[]{:S(2)}) async-start(f32[32,120,128]{2,1,0:T(8,128)} %get-tuple-element.9), calls=%async_computation | async-start | bytes 3932160 | tf_op jit(solution)/shard_map/all_to_all | solution.py:282
  12.9 5.7 %collective-permute-start = (f32[16,128]{1,0:T(8,128)S(1)}, f32[16,128]{1,0:T(8,128)S(1)}, u32[]{:S(2)}, u32[]{:S(2)}) collective-permute-start(f32[16,128]{1,0:T(8,128)S(1)} %copy-done.2), channel_id=1, source_target_pairs={{0,1},{1,2},{2,3},{3,0},{4,5},{5,6},{6,7},{7,4},{8,9},{9,10},{10,1... | collective-permute-start | bytes 24584 | tf_op jit(solution)/shard_map/ppermute | solution.py:239
  13.2 5.4 %collective-permute-start.1 = (f32[16,128]{1,0:T(8,128)S(1)}, f32[16,128]{1,0:T(8,128)S(1)}, u32[]{:S(2)}, u32[]{:S(2)}) collective-permute-start(f32[16,128]{1,0:T(8,128)S(1)} %copy-done.1), channel_id=1, source_target_pairs={{0,3},{1,0},{2,1},{3,2},{4,7},{5,4},{6,5},{7,6},{8,11},{9,8},{10,9... | collective-permute-start | bytes 24584 | tf_op jit(solution)/shard_map/ppermute | solution.py:239
  18.6 31.7 %collective-permute-start.2 = (f32[8,128]{1,0:T(8,128)S(1)}, f32[8,128]{1,0:T(8,128)S(1)}, u32[]{:S(2)}, u32[]{:S(2)}) collective-permute-start(f32[8,128]{1,0:T(8,128)S(1)} %get-tuple-element.14), channel_id=1, source_target_pairs={{0,4},{4,8},{8,12},{12,16},{16,20},{20,24},{24,28},{28,0},{1,5},{5... | collective-permute-start | bytes 12296 | tf_op jit(solution)/shard_map/ppermute | solution.py:239
  27.3 23.0 %collective-permute-start.3 = (f32[8,128]{1,0:T(8,128)S(1)}, f32[8,128]{1,0:T(8,128)S(1)}, u32[]{:S(2)}, u32[]{:S(2)}) collective-permute-start(f32[8,128]{1,0:T(8,128)S(1)} %get-tuple-element.15), channel_id=1, source_target_pairs={{0,28},{4,0},{8,4},{12,8},{16,12},{20,16},{24,20},{28,24},{1,29},{... | collective-permute-start | bytes 12296 | tf_op jit(solution)/shard_map/ppermute | solution.py:239

commit v4 on v3

v4 whole, which is shorter than its diff:
```python
import functools

import jax
import jax.numpy as jnp
from jax import lax
from jax.experimental import pallas as pl
from jax.experimental.pallas import tpu as pltpu
from jax.sharding import PartitionSpec as P

diffusion = 0.1
advection = 0.15
buoyancy = 0.3
latent_heat = 0.5
fallout = 0.2
condense_rate = 0.4
nudging = 0.5

AXES = ("ex", "ey")
NT = (((1,), (1,)), ((), ()))
MIB = 1024 * 1024
REGROUP_FLOPS = 6*10**9
EDGE_FLOPS = 10**5
EARLY_BLOCKS = 2
EARLY_FLOPS = 13*10**9


def substep_level(values_at, nudge_row, z, levels, field_count, active=None):
    values = [values_at(f, z) for f in range(field_count)]
    width = values[0].shape[0]
    drift = (advection * 0.5) * values[0]
    from_east, from_west = diffusion - drift, diffusion + drift
    condensed = condense_rate * jnp.maximum(values[3], 0.0)
    results = []
    for f in range(field_count):
        v = values[f]
        east = pltpu.roll(v, width - 1, 0)
        west = pltpu.roll(v, 1, 0)
        fresh = east * from_east + west * from_west
        if 0 < z < levels - 1:
            fresh = fresh + diffusion * (values_at(f, z + 1) + values_at(f, z - 1))
        else:
            fresh = fresh + diffusion * values_at(f, z + 1 if z == 0 else z - 1)
        fresh = fresh + (nudge_row(f, z) - (nudging / width) * jnp.sum(v, axis=0, keepdims=True))
        own = 1.0 - 4.0 * diffusion
        if f == 1:
            fresh = fresh + buoyancy * values[2]
        elif f == 2:
            fresh = fresh - buoyancy * values[1] + latent_heat * condensed
        elif f == 3:
            fresh = fresh - condensed
        elif f == 4:
            fresh = fresh + condensed
            own = own - fallout
        fresh = fresh + own * v
        results.append(fresh if active is None else jnp.where(active, fresh, v))
    return results


def slot_rank(dest):
    owned = dest.shape[1]
    named = jnp.broadcast_to(dest.astype(jnp.float32), (owned, owned))
    rows = lax.broadcasted_iota(jnp.int32, (owned, owned), 0)
    cols = lax.broadcasted_iota(jnp.int32, (owned, owned), 1)
    earlier = jnp.where((named == named.T) & (rows < cols), 1, 0)
    return jnp.sum(earlier, axis=0, keepdims=True)


def one_hot_rows(slot, count):
    rows = lax.broadcasted_iota(jnp.int32, (count, slot.shape[1]), 0)
    return jnp.concatenate([jnp.where(rows == slot, 1.0, 0.0).astype(jnp.bfloat16)] * 3, axis=1)


def hop_bits(devices):
    bits = devices.bit_length() - 1
    return [bits - 1] + list(range(bits - 1))


def hop_order(difference, devices):
    place = jnp.zeros_like(difference)
    for bit in hop_bits(devices):
        place = 2 * place + ((difference >> bit) & 1)
    return place


def picked(picks, block):
    high = block.astype(jnp.bfloat16)
    rest = block - high.astype(jnp.float32)
    middle = rest.astype(jnp.bfloat16)
    low = (rest - middle.astype(jnp.float32)).astype(jnp.bfloat16)
    parts = jnp.concatenate([high, middle, low], axis=1)
    return lax.dot_general(picks, parts, NT, preferred_element_type=jnp.float32)


def fetch(source, target, sem):
    copy = pltpu.make_async_copy(source, target, sem)
    copy.start()
    return copy


def cloud_kernel(devices, capacity, early, me_ref, crm_hbm, gcm_hbm, mass_hbm, dest_hbm, cost_hbm,
                 send_hbm, far_hbm, near_hbm, nodes_ref, low_ref, high_ref, first_ref, second_ref, prof_ref, tend_ref,
                 crm_ref, gcm_ref, mass_ref, dest_ref, cost_ref, send_ref, early_ref, small_sem, crm_sem, send_sem, early_sem):
    field_count, levels, width, owned = crm_ref.shape
    group = owned // width
    small = [
        fetch(dest_hbm, dest_ref, small_sem.at[0]),
        fetch(gcm_hbm, gcm_ref, small_sem.at[1]),
        fetch(cost_hbm, cost_ref, small_sem.at[2]),
    ]
    pieces = [
        fetch(crm_hbm.at[:, pl.ds(z, group)], crm_ref.at[:, pl.ds(z, group)], crm_sem.at[z // group])
        for z in range(0, levels, group)
    ]
    small.append(fetch(mass_hbm, mass_ref, small_sem.at[3]))
    used = field_count * levels
    nodes = gcm_ref.shape[1]

    small[0].wait()
    rank = slot_rank(dest_ref[...])
    picks = one_hot_rows(dest_ref[...] * capacity + rank, devices * capacity)
    if early:
        turned = hop_order(dest_ref[...] ^ me_ref[0], devices)
        early_picks = one_hot_rows(turned * capacity + rank, devices * capacity)
    small[1].wait()
    grid_fields = jnp.concatenate(
        [gcm_ref[f] for f in range(field_count)] + [jnp.zeros((nodes, nodes - used), jnp.float32)], axis=1
    )
    prof_ref[...] = nudging * grid_fields.T
    small[2].wait()
    twice = jnp.broadcast_to(cost_ref[...] >= 2, (width, owned))

    def nudge_row(f, z):
        return prof_ref[pl.ds(f * levels + z, 1), :]

    def first_substep(z):
        fresh = substep_level(lambda f, k: crm_ref[f, k], nudge_row, z, levels, field_count)
        for f in range(field_count):
            first_ref[f, z] = fresh[f]

    def second_substep(z):
        fresh = substep_level(lambda f, k: first_ref[f, k], nudge_row, z, levels, field_count, twice)
        for f in range(field_count):
            second_ref[f, z] = fresh[f]

    pieces[0].wait()
    for z in range(levels):
        if (z + 1) % group == 0 and z + 1 < levels:
            pieces[(z + 1) // group].wait()
        first_substep(z)
    for z in range(levels):
        second_substep(z)

    sends = []
    if early:
        first = levels // group - 1
        at = field_count - early
        block = second_ref[pl.ds(at, early), pl.ds(first * group, group)].reshape(early * group * width, owned)
        moved = picked(early_picks, block)
        for e in range(early):
            rows = moved[:, e * owned:(e + 1) * owned].reshape(devices, capacity, owned)
            early_ref[:, e * capacity:(e + 1) * capacity, :] = rows
        half = devices // 2
        sends.append(fetch(early_ref.at[pl.ds(half, half)], far_hbm, early_sem.at[0]))
        sends.append(fetch(early_ref.at[pl.ds(0, half)], near_hbm, early_sem.at[1]))
    group_rows = field_count * capacity
    aligned = group_rows % 8 == 0
    for number in range(levels // group):
        held = field_count - (early if number == levels // group - 1 else 0)
        blocks = second_ref[pl.ds(0, held), pl.ds(number * group, group)].reshape(held * group * width, owned)
        moved = picked(picks, blocks)
        for f in range(held):
            at = (number * field_count + f) * capacity
            send_ref[:, at:at + capacity, :] = moved[:, f * owned:(f + 1) * owned].reshape(devices, capacity, owned)
        if aligned:
            part = pl.ds(number * group_rows, held * capacity)
            sends.append(fetch(send_ref.at[:, part], send_hbm.at[:, part], send_sem.at[number]))
    if not aligned:
        sends.append(fetch(send_ref, send_hbm, send_sem.at[0]))

    tend_ref[...] = jnp.zeros_like(tend_ref)
    for f in range(field_count):
        for z in range(levels):
            gained = jnp.sum(second_ref[f, z] - crm_ref[f, z], axis=0, keepdims=True) * (1.0 / width)
            tend_ref[pl.ds(f * levels + z, 1), :] = gained
    small[3].wait()
    mass = mass_ref[...]
    fields = jnp.concatenate(
        [gcm_ref[f] for f in range(field_count)] + [mass, jnp.zeros((nodes, nodes - used - levels), jnp.float32)],
        axis=1,
    )
    factors = jnp.concatenate([mass] * field_count + [jnp.ones((nodes, nodes - used), jnp.float32)], axis=1)
    nodes_ref[...] = (fields + tend_ref[...].T) * factors
    return sends


def edges_y(elx, ely, side, nodes_ref, low_ref, high_ref):
    step = side * side
    for a in range(elx):
        first = a * ely * step
        final = (a * ely + ely - 1) * step + side - 1
        low_ref[a * side:(a + 1) * side, :] = nodes_ref[pl.ds(first, side, stride=side), :]
        high_ref[a * side:(a + 1) * side, :] = nodes_ref[pl.ds(final, side, stride=side), :]


def kernel_a(devices, capacity, early, elx, ely, side, *refs):
    sends = cloud_kernel(devices, capacity, early, *refs)
    edges_y(elx, ely, side, *refs[9:12])
    for copy in sends:
        copy.wait()


def kernel_y(elx, ely, side, nodes_ref, south_ref, north_ref, sum_ref, low_ref, high_ref):
    step = side * side
    sum_ref[...] = nodes_ref[...]
    for a in range(elx):
        for b in range(ely):
            base = (a * ely + b) * step
            if b > 0:
                gain = nodes_ref[pl.ds(base - step + side - 1, side, stride=side), :]
            else:
                gain = south_ref[a * side:(a + 1) * side, :]
            here = pl.ds(base, side, stride=side)
            sum_ref[here, :] = nodes_ref[here, :] + gain
            if b + 1 < ely:
                gain = nodes_ref[pl.ds(base + step, side, stride=side), :]
            else:
                gain = north_ref[a * side:(a + 1) * side, :]
            here = pl.ds(base + side - 1, side, stride=side)
            sum_ref[here, :] = nodes_ref[here, :] + gain
    for b in range(ely):
        low_ref[b * side:(b + 1) * side, :] = sum_ref[b * step:b * step + side, :]
        start = (elx - 1) * ely * step + b * step + (side - 1) * side
        high_ref[b * side:(b + 1) * side, :] = sum_ref[start:start + side, :]


def kernel_x(elx, ely, side, sum_ref, west_ref, east_ref, out_ref, full_ref):
    step = side * side
    field_count, nodes, levels = out_ref.shape
    full_ref[...] = sum_ref[...]
    for a in range(elx):
        for b in range(ely):
            base = (a * ely + b) * step
            last = base + (side - 1) * side
            if a > 0:
                before = ((a - 1) * ely + b) * step + (side - 1) * side
                gain = sum_ref[before:before + side, :]
            else:
                gain = west_ref[b * side:(b + 1) * side, :]
            full_ref[base:base + side, :] = sum_ref[base:base + side, :] + gain
            if a + 1 < elx:
                after = ((a + 1) * ely + b) * step
                gain = sum_ref[after:after + side, :]
            else:
                gain = east_ref[b * side:(b + 1) * side, :]
            full_ref[last:last + side, :] = sum_ref[last:last + side, :] + gain
    full = full_ref[...]
    divisor = full[:, field_count * levels:(field_count + 1) * levels]
    for f in range(field_count):
        out_ref[f] = full[:, f * levels:(f + 1) * levels] / divisor


def turned_blocks(rows_of, out_hbm, out_ref, sem):
    block = out_ref.shape[0] // len(rows_of)
    copies = []
    for number, (step, slots_at) in enumerate(rows_of):
        here, there = pl.ds(number * block, block), pl.ds(step * block, block)
        out_ref[here, :] = slots_at().T
        copies.append(fetch(out_ref.at[here], out_hbm.at[there], sem.at[number]))
    for copy in copies:
        copy.wait()


def kernel_out(devices, capacity, groups, field_count, early, recv_ref, *refs):
    out_hbm, out_ref, sem = refs[-3:]
    pitch = recv_ref.shape[0] // devices

    def rows(first):
        ranked = [recv_ref[pl.ds(first + r, devices, stride=pitch), :] for r in range(capacity)]
        return jnp.concatenate(ranked, axis=0)

    blocks = groups * field_count - early
    steps = [(at % field_count) * groups + at // field_count for at in range(blocks)]
    rows_of = [(step, functools.partial(rows, at * capacity)) for at, step in enumerate(steps)]
    turned_blocks(rows_of, out_hbm, out_ref, sem)


def kernel_early(devices, capacity, groups, field_count, early, sources, me_ref, kept_ref, last_ref,
                 out_hbm, row_ref, out_ref, sem):
    slots = devices * capacity
    arrived = [(ref, index) for ref in (kept_ref, last_ref) for index in range(devices // 2)]
    for (ref, index), bits in zip(arrived, sources):
        for e in range(early):
            tile = ref[index, pl.ds(e * capacity, capacity), :]
            row_ref[pl.ds(e * slots + (me_ref[0] ^ bits), capacity, stride=devices), :] = tile
    steps = [(field_count - early + e) * groups + groups - 1 for e in range(early)]
    rows_of = [(step, lambda e=e: row_ref[e * slots:(e + 1) * slots, :]) for e, step in enumerate(steps)]
    turned_blocks(rows_of, out_hbm, out_ref, sem)


def params(mib):
    return pltpu.CompilerParams(vmem_limit_bytes=mib * MIB)


def cost(flops, byte_count):
    return pl.CostEstimate(flops=flops, bytes_accessed=byte_count, transcendentals=0)


def shift(face, axis, by):
    count = lax.axis_size(axis)
    return lax.ppermute(face, axis, [(i, (i + by) % count) for i in range(count)])


def exchange(block, bits):
    count = lax.axis_size(AXES)
    return lax.ppermute(block, AXES, [(i, i ^ bits) for i in range(count)])


def kernel_regroup(kept_ref, last_ref, keep_ref, pass_ref):
    half = kept_ref.shape[1] // 2
    keep_ref[0:1] = kept_ref[:, 0:half]
    keep_ref[1:2] = last_ref[:, 0:half]
    pass_ref[0:1] = kept_ref[:, half:]
    pass_ref[1:2] = last_ref[:, half:]


def regrouped(kept, last, first):
    half = kept.shape[1] // 2
    if first:
        shape = jax.ShapeDtypeStruct((2, half) + kept.shape[2:], kept.dtype)
        return pl.pallas_call(
            kernel_regroup,
            out_shape=(shape, shape),
            compiler_params=params(8),
            cost_estimate=cost(REGROUP_FLOPS, 10**6),
            name="regroup",
        )(kept, last)
    passed = jnp.concatenate([kept[:, half:], last[:, half:]])
    return jnp.concatenate([kept[:, :half], last[:, :half]]), passed


def hops(near, far, devices):
    first, *others = hop_bits(devices)
    kept, last = near[None], exchange(far, 1 << first)[None]
    kept_from, last_from = [0], [1 << first]
    for bit in others:
        kept, passed = regrouped(kept, last, bit == others[0])
        last = exchange(passed, 1 << bit)
        kept_from = kept_from + last_from
        last_from = [source ^ (1 << bit) for source in kept_from]
    return kept[:, 0], last[:, 0], kept_from + last_from


def body(crm_state, gcm_state, mass, dest, cost_class):
    devices = lax.axis_size(("ex", "ey"))
    field_count, levels, width, owned = crm_state.shape
    elx, ely, side = gcm_state.shape[2:5]
    capacity = max(2, 2 * owned // devices)
    slots = capacity * devices
    values = field_count * levels * width
    f32 = jnp.float32
    gcm_nodes = gcm_state.transpose(0, 2, 3, 4, 5, 1).reshape(field_count, owned, levels)
    mass_nodes = mass.transpose(1, 2, 3, 4, 0).reshape(owned, levels)
    sizes = (elx, ely, side)
    face_x = jax.ShapeDtypeStruct((ely * side, owned), f32)
    face_y = jax.ShapeDtypeStruct((elx * side, owned), f32)
    in_hbm = pl.BlockSpec(memory_space=pltpu.HBM)
    in_vmem = pl.BlockSpec(memory_space=pltpu.VMEM)
    square = jax.ShapeDtypeStruct((owned, owned), f32)
    in_smem = pl.BlockSpec(memory_space=pltpu.SMEM)
    me = lax.axis_index(AXES).astype(jnp.int32).reshape(1)
    groups = levels * width // owned
    early = EARLY_BLOCKS if capacity % 8 == 0 and devices & (devices - 1) == 0 else 0
    packed = (devices, (values // owned - early) * capacity, owned)
    apart = (max(2, devices) // 2, max(1, early) * capacity, owned)
    send, far, near, nodes, low, high = pl.pallas_call(
        functools.partial(kernel_a, devices, capacity, early, *sizes),
        out_shape=(
            jax.ShapeDtypeStruct(packed, f32),
            jax.ShapeDtypeStruct(apart, f32),
            jax.ShapeDtypeStruct(apart, f32),
            square,
            face_y,
            face_y,
        ),
        in_specs=[in_smem] + [in_hbm] * 5,
        out_specs=(in_hbm, in_hbm, in_hbm, in_vmem, in_vmem, in_vmem),
        scratch_shapes=[
            pltpu.VMEM(crm_state.shape, f32),
            pltpu.VMEM(crm_state.shape, f32),
            pltpu.VMEM((owned, owned), f32),
            pltpu.VMEM((owned, owned), f32),
            pltpu.VMEM(crm_state.shape, f32),
            pltpu.VMEM(gcm_nodes.shape, f32),
            pltpu.VMEM(mass_nodes.shape, f32),
            pltpu.VMEM((1, owned), jnp.int32),
            pltpu.VMEM((1, owned), jnp.int32),
            pltpu.VMEM(packed, f32),
            pltpu.VMEM((devices,) + apart[1:], f32),
            pltpu.SemaphoreType.DMA((4,)),
            pltpu.SemaphoreType.DMA((groups,)),
            pltpu.SemaphoreType.DMA((groups,)),
            pltpu.SemaphoreType.DMA((2,)),
        ],
        compiler_params=params(63),
        name="cloud_models",
    )(me, crm_state, gcm_nodes, mass_nodes, dest.reshape(1, owned), cost_class.reshape(1, owned))
    received = lax.all_to_all(send, AXES, split_axis=0, concat_axis=0, tiled=True)
    if early:
        kept, last, sources = hops(near, far, devices)
    north = shift(low, "ey", -1)
    south = shift(high, "ey", 1)
    summed, low, high = pl.pallas_call(
        functools.partial(kernel_y, *sizes),
        out_shape=(square, face_x, face_x),
        compiler_params=params(8),
        cost_estimate=cost(10**5, 10**5),
        name="edge_sum_second",
    )(nodes, south, north)
    east = shift(low, "ex", -1)
    west = shift(high, "ex", 1)
    if early:
        summed, last = lax.optimization_barrier((summed, last))
    gcm_out = pl.pallas_call(
        functools.partial(kernel_x, *sizes),
        out_shape=jax.ShapeDtypeStruct((field_count, owned, levels), f32),
        scratch_shapes=[pltpu.VMEM((owned, owned), f32)],
        compiler_params=params(8),
        cost_estimate=cost(EDGE_FLOPS, 10**5),
        name="edge_sum_first",
    )(summed, west, east)
    gcm_out = gcm_out.reshape(field_count, elx, ely, side, side, levels).transpose(0, 5, 1, 2, 3, 4)
    out_shape = jax.ShapeDtypeStruct((values, slots), f32)
    block_count = values // owned
    begun = []
    if early:
        begun.append(pl.pallas_call(
            functools.partial(kernel_early, devices, capacity, groups, field_count, early, sources),
            in_specs=[in_smem, in_vmem, in_vmem],
            out_specs=in_hbm,
            out_shape=out_shape,
            scratch_shapes=[
                pltpu.VMEM((early * slots, owned), f32),
                pltpu.VMEM((early * owned, slots), f32),
                pltpu.SemaphoreType.DMA((early,)),
            ],
            compiler_params=params(8),
            cost_estimate=cost(EARLY_FLOPS, 10**6),
            name="early_slots",
        )(me, kept, last))
    cloud = pl.pallas_call(
        functools.partial(kernel_out, devices, capacity, groups, field_count, early),
        in_specs=[in_vmem] + [in_hbm] * len(begun),
        out_specs=in_hbm,
        out_shape=out_shape,
        input_output_aliases={1: 0} if begun else {},
        scratch_shapes=[
            pltpu.VMEM(((block_count - early) * owned, slots), f32),
            pltpu.SemaphoreType.DMA((block_count - early,)),
        ],
        compiler_params=params(16),
        name="cloud_slots",
    )(received.reshape(-1, owned), *begun)
    return cloud.reshape(field_count, levels, width, slots), gcm_out


def solution(mesh):
    return jax.shard_map(
        body,
        mesh=mesh,
        in_specs=(
            P(None, None, None, ("ex", "ey")),
            P(None, None, "ex", "ey", None, None),
            P(None, "ex", "ey", None, None),
            P(("ex", "ey"), None),
            P(("ex", "ey")),
        ),
        out_specs=(P(None, None, None, ("ex", "ey")), P(None, None, "ex", "ey", None, None)),
        check_vma=False,
    )
```

time: 60.6 us -> 55.9 us (0.922)
  the two profiles are of different devices: /device:TPU:0 before, /device:TPU:17 now
where the time goes in v4:
time: 55.9 us; the launch traced here: 55.5 us
  waiting for transfers between devices  28.1 us (50%)
  starting transfers between devices  18.3 us (33%)
  Pallas kernels  8.22 us (15%)
  between operations  0.8 us (1%)
    ppermute x5, waiting for transfers between devices, exchange(): return lax.ppermute(block, AXES, [(i, i ^ bits) for i in range(count)])  17.5 us
    ppermute x4, waiting for transfers between devices, shift(): lax.ppermute(face, axis, [(i, (i + by) % count) for i in range(count)])  10.6 us
    ppermute x5, starting transfers between devices, exchange(): return lax.ppermute(block, AXES, [(i, i ^ bits) for i in range(count)])  7.51 us
    all_to_all x1, starting transfers between devices, body(): lax.all_to_all(send, AXES, split_axis=0, concat_axis=0, tiled=True)  6.8 us
    pallas_call x1, Pallas kernels, body(): pl.pallas_call(functools.partial(kernel_a, devices, capacity, early, *siz...  4.75 us
    ppermute x4, starting transfers between devices, shift(): lax.ppermute(face, axis, [(i, (i + by) % count) for i in range(count)])  4 us
    pallas_call x1, Pallas kernels, body(): pl.pallas_call(functools.partial(kernel_out, devices, capacity, groups, f...  1.39 us
  transfers between devices with their start and end apart: 10, of which 6 were waited for; matrix products, arithmetic and copies ran while one was open for 0% of the time, Pallas kernels for 4%

profile of v4, /device:TPU:17, one launch (start us, length us, event | category | flops | bytes accessed | tf_op | source)
XLA Modules:
  0.0 55.5 jit_solution(4619779228072158861)
XLA Ops:
  0.6 4.8 %cloud_models.1 = (f32[32,104,128]{2,1,0:T(8,128)}, f32[16,16,128]{2,1,0:T(8,128)}, f32[16,16,128]{2,1,0:T(8,128)}, f32[128,128]{1,0:T(8,128)}, f32[16,128]{1,0:T(8,128)}, /*index=5*/f32[16,128]{1,0:T(8,128)}) custom-call(s32[1]{0:T(128)} %bitcast.refs_0_.me_ref, f32[5,12,32,128]{3,2,1,0:T(8,128)} %refs_1_.1, f32[5,128,12]{2,1,0:T(8,128)} %bitcast.25, ...), custom_call_target="tpu_custom_call" | custom-call | tf_op jit(solution)/shard_map/cloud_models/pallas_call | solution.py:375
  5.4 0.0 copy-start.1
  5.4 0.1 collective-permute-start
  5.5 6.8 %all-to-all-start = ((f32[32,104,128]{2,1,0:T(8,128)}), f32[32,104,128]{2,1,0:T(8,128)S(1)}, u32[]{:S(2)}, u32[]{:S(2)}) async-start(f32[32,104,128]{2,1,0:T(8,128)} %get-tuple-element.15), calls=%async_computation | async-start | bytes 3407872 | tf_op jit(solution)/shard_map/all_to_all | solution.py:407
  12.3 0.0 collective-permute-done
  12.3 0.0 copy-done.1
  12.3 0.0 copy-start.3
  12.3 0.0 copy-start.2
  12.3 0.0 copy-start
  12.4 0.4 collective-permute-start.1
  12.8 1.0 %collective-permute-done.1 = f32[2,8,16,128]{3,2,0,1:T(8,128)S(1)} collective-permute-done((f32[2,8,16,128]{3,2,0,1:T(8,128)S(1)}, f32[2,8,16,128]{3,2,0,1:T(8,128)S(1)}, u32[]{:S(2)}, u32[]{:S(2)}) %collective-permute-start.1) | collective-permute-done | bytes 131104 | tf_op jit(solution)/shard_map/ppermute | solution.py:315
  13.8 1.3 %collective-permute-start.2 = (f32[4,4,16,128]{3,2,0,1:T(8,128)S(1)}, f32[4,4,16,128]{3,2,0,1:T(8,128)S(1)}, u32[]{:S(2)}, u32[]{:S(2)}) collective-permute-start(f32[4,4,16,128]{3,2,0,1:T(8,128)S(1)} %pad_maximum_fusion.2), channel_id=1, source_target_pairs={{0,2},{1,3},{2,0},{3,1},{4,6},{5,7},{6,4},{7,5},{8,10},{9,11},{10,... | collective-permute-start | bytes 393224 | tf_op jit(solution)/shard_map/ppermute | solution.py:315
  15.1 12.1 %collective-permute-done.2 = f32[4,4,16,128]{3,2,0,1:T(8,128)S(1)} collective-permute-done((f32[4,4,16,128]{3,2,0,1:T(8,128)S(1)}, f32[4,4,16,128]{3,2,0,1:T(8,128)S(1)}, u32[]{:S(2)}, u32[]{:S(2)}) %collective-permute-start.2) | collective-permute-done | bytes 131104 | tf_op jit(solution)/shard_map/ppermute | solution.py:315
  27.3 2.4 %collective-permute-start.3 = (f32[8,2,16,128]{3,2,0,1:T(8,128)S(1)}, f32[8,2,16,128]{3,2,0,1:T(8,128)S(1)}, u32[]{:S(2)}, u32[]{:S(2)}) collective-permute-start(f32[8,2,16,128]{3,2,0,1:T(8,128)S(1)} %fusion.1), channel_id=1, source_target_pairs={{0,4},{1,5},{2,6},{3,7},{4,0},{5,1},{6,2},{7,3},{8,12},{9,13},{10,... | collective-permute-start | bytes 393224 | tf_op jit(solution)/shard_map/ppermute | solution.py:315
  29.7 0.0 copy-done.3
  29.7 1.6 %collective-permute-start.4 = (f32[16,128]{1,0:T(8,128)S(1)}, f32[16,128]{1,0:T(8,128)S(1)}, u32[]{:S(2)}, u32[]{:S(2)}) collective-permute-start(f32[16,128]{1,0:T(8,128)S(1)} %copy-done.3), channel_id=1, source_target_pairs={{0,1},{1,2},{2,3},{3,0},{4,5},{5,6},{6,7},{7,4},{8,9},{9,10},{10,1... | collective-permute-start | bytes 24584 | tf_op jit(solution)/shard_map/ppermute | solution.py:310
  31.3 0.0 copy-done.2
  31.3 0.0 collective-permute-start.5
  31.3 0.8 %collective-permute-done.4.south_ref = f32[16,128]{1,0:T(8,128)S(1)} collective-permute-done((f32[16,128]{1,0:T(8,128)S(1)}, f32[16,128]{1,0:T(8,128)S(1)}, u32[]{:S(2)}, u32[]{:S(2)}) %collective-permute-start.4) | collective-permute-done | bytes 8224 | tf_op jit(solution)/shard_map/ppermute | solution.py:310
  32.1 2.6 %collective-permute-done.5.north_ref = f32[16,128]{1,0:T(8,128)S(1)} collective-permute-done((f32[16,128]{1,0:T(8,128)S(1)}, f32[16,128]{1,0:T(8,128)S(1)}, u32[]{:S(2)}, u32[]{:S(2)}) %collective-permute-start.5) | collective-permute-done | bytes 8224 | tf_op jit(solution)/shard_map/ppermute | solution.py:310
  34.7 0.0 copy-done
  34.7 0.1 collective-permute-start.7
  34.8 2.4 %collective-permute-start.8 = (f32[8,128]{1,0:T(8,128)S(1)}, f32[8,128]{1,0:T(8,128)S(1)}, u32[]{:S(2)}, u32[]{:S(2)}) collective-permute-start(f32[8,128]{1,0:T(8,128)S(1)} %get-tuple-element.27), channel_id=1, source_target_pairs={{0,28},{4,0},{8,4},{12,8},{16,12},{20,16},{24,20},{28,24},{1,29},{... | collective-permute-start | bytes 12296 | tf_op jit(solution)/shard_map/ppermute | solution.py:310
  37.1 0.0 collective-permute-done.3
  37.2 3.3 %collective-permute-start.6 = (f32[16,1,16,128]{3,2,0,1:T(8,128)S(1)}, f32[16,1,16,128]{3,2,0,1:T(8,128)S(1)}, u32[]{:S(2)}, u32[]{:S(2)}) collective-permute-start(f32[16,1,16,128]{3,2,0,1:T(8,128)S(1)} %fusion), channel_id=1, source_target_pairs={{0,8},{1,9},{2,10},{3,11},{4,12},{5,13},{6,14},{7,15},{8,0},{9,1},... | collective-permute-start | bytes 393224 | tf_op jit(solution)/shard_map/ppermute | solution.py:315
  40.5 4.3 %collective-permute-done.6 = f32[16,1,16,128]{3,2,0,1:T(8,128)S(1)} collective-permute-done((f32[16,1,16,128]{3,2,0,1:T(8,128)S(1)}, f32[16,1,16,128]{3,2,0,1:T(8,128)S(1)}, u32[]{:S(2)}, u32[]{:S(2)}) %collective-permute-start.6) | collective-permute-done | bytes 131104 | tf_op jit(solution)/shard_map/ppermute | solution.py:315
  44.8 7.3 %collective-permute-done.7.west_ref = f32[8,128]{1,0:T(8,128)S(1)} collective-permute-done((f32[8,128]{1,0:T(8,128)S(1)}, f32[8,128]{1,0:T(8,128)S(1)}, u32[]{:S(2)}, u32[]{:S(2)}) %collective-permute-start.7) | collective-permute-done | bytes 4128 | tf_op jit(solution)/shard_map/ppermute | solution.py:310
  52.1 0.0 collective-permute-done.8.east_ref
  52.1 1.0 %edge_sum_first.1 = f32[5,128,12]{2,1,0:T(8,128)} custom-call(f32[128,128]{1,0:T(8,128)S(1)} %get-tuple-element.25.sum_ref, f32[8,128]{1,0:T(8,128)S(1)} %collective-permute-done.7.west_ref, f32[8,128]{1,0:T(8,128)S(1)} %collective-permute-done.8.east_ref), custom_call_target="tpu_custom_call" | custom-call | flops 100000 | bytes 100000 | tf_op jit(solution)/shard_map/edge_sum_first/pallas_call | solution.py:423
  53.1 1.0 %early_slots.1.refs_0_ = f32[1920,256]{1,0:T(8,128)} custom-call(s32[1]{0:T(128)} %bitcast.refs_0_.me_ref, f32[16,16,128]{2,1,0:T(8,128)S(1)} %maximum_bitcast_fusion.kept_ref, f32[16,16,128]{2,1,0:T(8,128)S(1)} %bitcast.20), custom_call_target="tpu_custom_call" | custom-call | flops 12999999488 | bytes 1000000 | tf_op jit(solution)/shard_map/early_slots/pallas_call | solution.py:436
  54.1 0.0 all-to-all-done
  54.2 1.4 %cloud_slots.1 = f32[1920,256]{1,0:T(8,128)} custom-call(f32[3328,128]{1,0:T(8,128)S(1)} %bitcast.19, f32[1920,256]{1,0:T(8,128)} %early_slots.1.refs_0_), custom_call_target="tpu_custom_call", output_to_operand_aliasing={{}: (1, {})} | custom-call | tf_op jit(solution)/shard_map/cloud_slots/pallas_call | solution.py:450
  (13 shorter events, 0.1 us)
Async XLA Ops:
  5.4 6.9 %copy-start.1 = (f32[16,16,128]{2,1,0:T(8,128)S(1)}, f32[16,16,128]{2,1,0:T(8,128)}, u32[]{:S(2)}) copy-start(f32[16,16,128]{2,1,0:T(8,128)} %get-tuple-element.16) | copy-start | bytes 393220
  5.4 6.9 %collective-permute-start = (f32[16,16,128]{2,1,0:T(8,128)}, f32[16,16,128]{2,1,0:T(8,128)S(1)}, u32[]{:S(2)}, u32[]{:S(2)}) collective-permute-start(f32[16,16,128]{2,1,0:T(8,128)} %get-tuple-element.17), channel_id=1, source_target_pairs={{0,16},{1,17},{2,18},{3,19},{4,20},{5,21},{6,22},{7,23},{8,24},{9,... | collective-permute-start | bytes 393224 | tf_op jit(solution)/shard_map/ppermute | solution.py:315
  5.5 48.7 %all-to-all-start = ((f32[32,104,128]{2,1,0:T(8,128)}), f32[32,104,128]{2,1,0:T(8,128)S(1)}, u32[]{:S(2)}, u32[]{:S(2)}) async-start(f32[32,104,128]{2,1,0:T(8,128)} %get-tuple-element.15), calls=%async_computation | async-start | bytes 3407872 | tf_op jit(solution)/shard_map/all_to_all | solution.py:407
  12.3 17.4 %copy-start.3 = (f32[16,128]{1,0:T(8,128)S(1)}, f32[16,128]{1,0:T(8,128)}, u32[]{:S(2)}) copy-start(f32[16,128]{1,0:T(8,128)} %get-tuple-element.21) | copy-start | bytes 24580
  12.3 19.0 %copy-start.2 = (f32[16,128]{1,0:T(8,128)S(1)}, f32[16,128]{1,0:T(8,128)}, u32[]{:S(2)}) copy-start(f32[16,128]{1,0:T(8,128)} %get-tuple-element.22) | copy-start | bytes 24580
  12.3 22.3 %copy-start = (f32[128,128]{1,0:T(8,128)S(1)}, f32[128,128]{1,0:T(8,128)}, u32[]{:S(2)}) copy-start(f32[128,128]{1,0:T(8,128)} %get-tuple-element.20.nodes_ref) | copy-start | bytes 196612
  12.4 1.4 %collective-permute-start.1 = (f32[2,8,16,128]{3,2,0,1:T(8,128)S(1)}, f32[2,8,16,128]{3,2,0,1:T(8,128)S(1)}, u32[]{:S(2)}, u32[]{:S(2)}) collective-permute-start(f32[2,8,16,128]{3,2,0,1:T(8,128)S(1)} %copy.9), channel_id=1, source_target_pairs={{0,1},{1,0},{2,3},{3,2},{4,5},{5,4},{6,7},{7,6},{8,9},{9,8},{10,11... | collective-permute-start | bytes 393224 | tf_op jit(solution)/shard_map/ppermute | solution.py:315
  13.8 13.4 %collective-permute-start.2 = (f32[4,4,16,128]{3,2,0,1:T(8,128)S(1)}, f32[4,4,16,128]{3,2,0,1:T(8,128)S(1)}, u32[]{:S(2)}, u32[]{:S(2)}) collective-permute-start(f32[4,4,16,128]{3,2,0,1:T(8,128)S(1)} %pad_maximum_fusion.2), channel_id=1, source_target_pairs={{0,2},{1,3},{2,0},{3,1},{4,6},{5,7},{6,4},{7,5},{8,10},{9,11},{10,... | collective-permute-start | bytes 393224 | tf_op jit(solution)/shard_map/ppermute | solution.py:315
  27.3 9.9 %collective-permute-start.3 = (f32[8,2,16,128]{3,2,0,1:T(8,128)S(1)}, f32[8,2,16,128]{3,2,0,1:T(8,128)S(1)}, u32[]{:S(2)}, u32[]{:S(2)}) collective-permute-start(f32[8,2,16,128]{3,2,0,1:T(8,128)S(1)} %fusion.1), channel_id=1, source_target_pairs={{0,4},{1,5},{2,6},{3,7},{4,0},{5,1},{6,2},{7,3},{8,12},{9,13},{10,... | collective-permute-start | bytes 393224 | tf_op jit(solution)/shard_map/ppermute | solution.py:315
  29.7 2.4 %collective-permute-start.4 = (f32[16,128]{1,0:T(8,128)S(1)}, f32[16,128]{1,0:T(8,128)S(1)}, u32[]{:S(2)}, u32[]{:S(2)}) collective-permute-start(f32[16,128]{1,0:T(8,128)S(1)} %copy-done.3), channel_id=1, source_target_pairs={{0,1},{1,2},{2,3},{3,0},{4,5},{5,6},{6,7},{7,4},{8,9},{9,10},{10,1... | collective-permute-start | bytes 24584 | tf_op jit(solution)/shard_map/ppermute | solution.py:310
  31.3 3.4 %collective-permute-start.5 = (f32[16,128]{1,0:T(8,128)S(1)}, f32[16,128]{1,0:T(8,128)S(1)}, u32[]{:S(2)}, u32[]{:S(2)}) collective-permute-start(f32[16,128]{1,0:T(8,128)S(1)} %copy-done.2), channel_id=1, source_target_pairs={{0,3},{1,0},{2,1},{3,2},{4,7},{5,4},{6,5},{7,6},{8,11},{9,8},{10,9... | collective-permute-start | bytes 24584 | tf_op jit(solution)/shard_map/ppermute | solution.py:310
  34.7 17.4 %collective-permute-start.7 = (f32[8,128]{1,0:T(8,128)S(1)}, f32[8,128]{1,0:T(8,128)S(1)}, u32[]{:S(2)}, u32[]{:S(2)}) collective-permute-start(f32[8,128]{1,0:T(8,128)S(1)} %get-tuple-element.26), channel_id=1, source_target_pairs={{0,4},{4,8},{8,12},{12,16},{16,20},{20,24},{24,28},{28,0},{1,5},{5... | collective-permute-start | bytes 12296 | tf_op jit(solution)/shard_map/ppermute | solution.py:310
  34.8 17.3 %collective-permute-start.8 = (f32[8,128]{1,0:T(8,128)S(1)}, f32[8,128]{1,0:T(8,128)S(1)}, u32[]{:S(2)}, u32[]{:S(2)}) collective-permute-start(f32[8,128]{1,0:T(8,128)S(1)} %get-tuple-element.27), channel_id=1, source_target_pairs={{0,28},{4,0},{8,4},{12,8},{16,12},{20,16},{24,20},{28,24},{1,29},{... | collective-permute-start | bytes 12296 | tf_op jit(solution)/shard_map/ppermute | solution.py:310
  37.2 7.7 %collective-permute-start.6 = (f32[16,1,16,128]{3,2,0,1:T(8,128)S(1)}, f32[16,1,16,128]{3,2,0,1:T(8,128)S(1)}, u32[]{:S(2)}, u32[]{:S(2)}) collective-permute-start(f32[16,1,16,128]{3,2,0,1:T(8,128)S(1)} %fusion), channel_id=1, source_target_pairs={{0,8},{1,9},{2,10},{3,11},{4,12},{5,13},{6,14},{7,15},{8,0},{9,1},... | collective-permute-start | bytes 393224 | tf_op jit(solution)/shard_map/ppermute | solution.py:315

commit v5 on v4

--- a/solution.py
+++ b/solution.py
@@ -19,8 +19,7 @@
 NT = (((1,), (1,)), ((), ()))
 MIB = 1024 * 1024
 REGROUP_FLOPS = 6*10**9
-EDGE_FLOPS = 10**5
-EARLY_BLOCKS = 2
+EARLY_BLOCKS = 3
 EARLY_FLOPS = 13*10**9
 
 
@@ -233,7 +232,7 @@
         high_ref[b * side:(b + 1) * side, :] = sum_ref[start:start + side, :]
 
 
-def kernel_x(elx, ely, side, sum_ref, west_ref, east_ref, out_ref, full_ref):
+def sum_first(elx, ely, side, sum_ref, west_ref, east_ref, out_ref, full_ref):
     step = side * side
     field_count, nodes, levels = out_ref.shape
     full_ref[...] = sum_ref[...]
@@ -266,12 +265,13 @@
         here, there = pl.ds(number * block, block), pl.ds(step * block, block)
         out_ref[here, :] = slots_at().T
         copies.append(fetch(out_ref.at[here], out_hbm.at[there], sem.at[number]))
-    for copy in copies:
-        copy.wait()
-
-
-def kernel_out(devices, capacity, groups, field_count, early, recv_ref, *refs):
-    out_hbm, out_ref, sem = refs[-3:]
+    return copies
+
+
+def kernel_out(devices, capacity, groups, field_count, early, sizes, recv_ref, sum_ref, west_ref, east_ref, *refs):
+    out_hbm, gcm_hbm, out_ref, gcm_ref, full_ref, sem, gcm_sem = refs[-7:]
+    sum_first(*sizes, sum_ref, west_ref, east_ref, gcm_ref, full_ref)
+    gcm_copy = fetch(gcm_ref, gcm_hbm, gcm_sem)
     pitch = recv_ref.shape[0] // devices
 
     def rows(first):
@@ -281,20 +281,22 @@
     blocks = groups * field_count - early
     steps = [(at % field_count) * groups + at // field_count for at in range(blocks)]
     rows_of = [(step, functools.partial(rows, at * capacity)) for at, step in enumerate(steps)]
-    turned_blocks(rows_of, out_hbm, out_ref, sem)
-
-
-def kernel_early(devices, capacity, groups, field_count, early, sources, me_ref, kept_ref, last_ref,
-                 out_hbm, row_ref, out_ref, sem):
+    for copy in [gcm_copy] + turned_blocks(rows_of, out_hbm, out_ref, sem):
+        copy.wait()
+
+
+def kernel_early(devices, capacity, groups, field_count, early, sources, me_ref, *refs):
     slots = devices * capacity
-    arrived = [(ref, index) for ref in (kept_ref, last_ref) for index in range(devices // 2)]
+    *blocks, out_hbm, row_ref, out_ref, sem = refs
+    arrived = [(ref, index) for ref in blocks for index in range(ref.shape[0])]
     for (ref, index), bits in zip(arrived, sources):
         for e in range(early):
             tile = ref[index, pl.ds(e * capacity, capacity), :]
             row_ref[pl.ds(e * slots + (me_ref[0] ^ bits), capacity, stride=devices), :] = tile
     steps = [(field_count - early + e) * groups + groups - 1 for e in range(early)]
     rows_of = [(step, lambda e=e: row_ref[e * slots:(e + 1) * slots, :]) for e, step in enumerate(steps)]
-    turned_blocks(rows_of, out_hbm, out_ref, sem)
+    for copy in turned_blocks(rows_of, out_hbm, out_ref, sem):
+        copy.wait()
 
 
 def params(mib):
@@ -315,39 +317,42 @@
     return lax.ppermute(block, AXES, [(i, i ^ bits) for i in range(count)])
 
 
-def kernel_regroup(kept_ref, last_ref, keep_ref, pass_ref):
-    half = kept_ref.shape[1] // 2
-    keep_ref[0:1] = kept_ref[:, 0:half]
-    keep_ref[1:2] = last_ref[:, 0:half]
-    pass_ref[0:1] = kept_ref[:, half:]
-    pass_ref[1:2] = last_ref[:, half:]
-
-
-def regrouped(kept, last, first):
-    half = kept.shape[1] // 2
+def kernel_regroup(kept_ref, last_ref, *out_refs):
+    count = kept_ref.shape[1] // len(out_refs)
+    for number, out_ref in enumerate(out_refs):
+        part = pl.ds(number * count, count)
+        out_ref[0:1] = kept_ref[:, part]
+        out_ref[1:2] = last_ref[:, part]
+
+
+def regrouped(arrays, ways, first):
+    count = arrays[0].shape[1] // ways
     if first:
-        shape = jax.ShapeDtypeStruct((2, half) + kept.shape[2:], kept.dtype)
+        shape = jax.ShapeDtypeStruct((2, count) + arrays[0].shape[2:], arrays[0].dtype)
         return pl.pallas_call(
             kernel_regroup,
-            out_shape=(shape, shape),
+            out_shape=[shape] * ways,
             compiler_params=params(8),
             cost_estimate=cost(REGROUP_FLOPS, 10**6),
             name="regroup",
-        )(kept, last)
-    passed = jnp.concatenate([kept[:, half:], last[:, half:]])
-    return jnp.concatenate([kept[:, :half], last[:, :half]]), passed
+        )(*arrays)
+    return [jnp.concatenate([a[:, i * count:(i + 1) * count] for a in arrays]) for i in range(ways)]
 
 
 def hops(near, far, devices):
-    first, *others = hop_bits(devices)
-    kept, last = near[None], exchange(far, 1 << first)[None]
-    kept_from, last_from = [0], [1 << first]
-    for bit in others:
-        kept, passed = regrouped(kept, last, bit == others[0])
-        last = exchange(passed, 1 << bit)
-        kept_from = kept_from + last_from
-        last_from = [source ^ (1 << bit) for source in kept_from]
-    return kept[:, 0], last[:, 0], kept_from + last_from
+    top, *others = hop_bits(devices)
+    arrays = [near[None], exchange(far, 1 << top)[None]]
+    senders = [0, 1 << top]
+    middle = len(others) - 1
+    steps = [others[:1], others[1:middle], others[middle:]]
+    for step in steps:
+        moves = [0]
+        for bit in step:
+            moves = [move | flip for move in moves for flip in (0, 1 << bit)]
+        parts = regrouped(arrays, len(moves), step is steps[0])
+        arrays = [exchange(part, move) if move else part for part, move in zip(parts, moves)]
+        senders = [sender ^ move for move in moves for sender in senders]
+    return [array[:, 0] for array in arrays], senders
 
 
 def body(crm_state, gcm_state, mass, dest, cost_class):
@@ -406,7 +411,7 @@
     )(me, crm_state, gcm_nodes, mass_nodes, dest.reshape(1, owned), cost_class.reshape(1, owned))
     received = lax.all_to_all(send, AXES, split_axis=0, concat_axis=0, tiled=True)
     if early:
-        kept, last, sources = hops(near, far, devices)
+        arrived, sources = hops(near, far, devices)
     north = shift(low, "ey", -1)
     south = shift(high, "ey", 1)
     summed, low, high = pl.pallas_call(
@@ -419,23 +424,14 @@
     east = shift(low, "ex", -1)
     west = shift(high, "ex", 1)
     if early:
-        summed, last = lax.optimization_barrier((summed, last))
-    gcm_out = pl.pallas_call(
-        functools.partial(kernel_x, *sizes),
-        out_shape=jax.ShapeDtypeStruct((field_count, owned, levels), f32),
-        scratch_shapes=[pltpu.VMEM((owned, owned), f32)],
-        compiler_params=params(8),
-        cost_estimate=cost(EDGE_FLOPS, 10**5),
-        name="edge_sum_first",
-    )(summed, west, east)
-    gcm_out = gcm_out.reshape(field_count, elx, ely, side, side, levels).transpose(0, 5, 1, 2, 3, 4)
+        summed, arrived[-1] = lax.optimization_barrier((summed, arrived[-1]))
     out_shape = jax.ShapeDtypeStruct((values, slots), f32)
     block_count = values // owned
     begun = []
     if early:
         begun.append(pl.pallas_call(
             functools.partial(kernel_early, devices, capacity, groups, field_count, early, sources),
-            in_specs=[in_smem, in_vmem, in_vmem],
+            in_specs=[in_smem] + [in_vmem] * len(arrived),
             out_specs=in_hbm,
             out_shape=out_shape,
             scratch_shapes=[
@@ -446,20 +442,24 @@
             compiler_params=params(8),
             cost_estimate=cost(EARLY_FLOPS, 10**6),
             name="early_slots",
-        )(me, kept, last))
-    cloud = pl.pallas_call(
-        functools.partial(kernel_out, devices, capacity, groups, field_count, early),
-        in_specs=[in_vmem] + [in_hbm] * len(begun),
-        out_specs=in_hbm,
-        out_shape=out_shape,
-        input_output_aliases={1: 0} if begun else {},
+        )(me, *arrived))
+    cloud, gcm_out = pl.pallas_call(
+        functools.partial(kernel_out, devices, capacity, groups, field_count, early, sizes),
+        in_specs=[in_vmem] * 4 + [in_hbm] * len(begun),
+        out_specs=(in_hbm, in_hbm),
+        out_shape=(out_shape, jax.ShapeDtypeStruct((field_count, owned, levels), f32)),
+        input_output_aliases={4: 0} if begun else {},
         scratch_shapes=[
             pltpu.VMEM(((block_count - early) * owned, slots), f32),
+            pltpu.VMEM((field_count, owned, levels), f32),
+            pltpu.VMEM((owned, owned), f32),
             pltpu.SemaphoreType.DMA((block_count - early,)),
+            pltpu.SemaphoreType.DMA,
         ],
         compiler_params=params(16),
         name="cloud_slots",
-    )(received.reshape(-1, owned), *begun)
+    )(received.reshape(-1, owned), summed, west, east, *begun)
+    gcm_out = gcm_out.reshape(field_count, elx, ely, side, side, levels).transpose(0, 5, 1, 2, 3, 4)
     return cloud.reshape(field_count, levels, width, slots), gcm_out
 
 

time: 55.9 us -> 55.2 us (0.987)
  waiting for transfers between devices: 28.1 us -> 15.6 us
  starting transfers between devices: 18.3 us -> 29.7 us
    ppermute x5 -> x6, starting transfers between devices: 7.51 us -> 18.8 us  [exchange(): return lax.ppermute(block, AXES, [(i, i ^ bits) for i in range(count)])]
    ppermute x5 -> x6, waiting for transfers between devices: 17.5 us -> 9.64 us  [exchange(): return lax.ppermute(block, AXES, [(i, i ^ bits) for i in range(count)])]
    ppermute x4, waiting for transfers between devices: 10.6 us -> 5.88 us  [shift(): lax.ppermute(face, axis, [(i, (i + by) % count) for i in range(count)])]
    pallas_call x2 -> x1, Pallas kernels: 1.04 us -> 0.03 us  [regrouped(): pl.pallas_call(kernel_regroup, out_shape=[shape] * ways, compiler_params=...]
    pallas_call x1, Pallas kernels: 1.39 us -> 2.12 us  [body(): pl.pallas_call(functools.partial(kernel_out, devices, capacity, groups, f...]
  transfers between devices with their start and end apart: 10 -> 11, of which waited for: 6 -> 9; matrix products, arithmetic and copies ran while one was open for 0% -> 0% of each run, Pallas kernels for 4% -> 2%
where the time goes in v5:
time: 55.2 us; the launch traced here: 54.5 us
  starting transfers between devices  29.7 us (54%)
  waiting for transfers between devices  15.6 us (28%)
  Pallas kernels  8.23 us (15%)
  between operations  0.78 us (1%)
    ppermute x6, starting transfers between devices, exchange(): return lax.ppermute(block, AXES, [(i, i ^ bits) for i in range(count)])  18.8 us
    ppermute x6, waiting for transfers between devices, exchange(): return lax.ppermute(block, AXES, [(i, i ^ bits) for i in range(count)])  9.64 us
    all_to_all x1, starting transfers between devices, body(): lax.all_to_all(send, AXES, split_axis=0, concat_axis=0, tiled=True)  6.8 us
    ppermute x4, waiting for transfers between devices, shift(): lax.ppermute(face, axis, [(i, (i + by) % count) for i in range(count)])  5.88 us
    pallas_call x1, Pallas kernels, body(): pl.pallas_call(functools.partial(kernel_a, devices, capacity, early, *siz...  4.86 us
    ppermute x4, starting transfers between devices, shift(): lax.ppermute(face, axis, [(i, (i + by) % count) for i in range(count)])  4.07 us
    pallas_call x1, Pallas kernels, body(): pl.pallas_call(functools.partial(kernel_out, devices, capacity, groups, f...  2.12 us
    pallas_call x1, Pallas kernels, body(): pl.pallas_call(functools.partial(kernel_early, devices, capacity, groups,...  1.21 us
  transfers between devices with their start and end apart: 11, of which 9 were waited for; matrix products, arithmetic and copies ran while one was open for 0% of the time, Pallas kernels for 2%

profile of v5, /device:TPU:17, one launch (start us, length us, event | category | flops | bytes accessed | tf_op | source)
XLA Modules:
  0.0 54.5 jit_solution(9341805814419124513)
XLA Ops:
  0.6 4.9 %cloud_models.1 = (f32[32,96,128]{2,1,0:T(8,128)}, f32[16,24,128]{2,1,0:T(8,128)}, f32[16,24,128]{2,1,0:T(8,128)}, f32[128,128]{1,0:T(8,128)}, f32[16,128]{1,0:T(8,128)}, /*index=5*/f32[16,128]{1,0:T(8,128)}) custom-call(s32[1]{0:T(128)} %bitcast.refs_0_.me_ref, f32[5,12,32,128]{3,2,1,0:T(8,128)} %refs_1_.1, f32[5,128,12]{2,1,0:T(8,128)} %bitcast.24, ...), custom_call_target="tpu_custom_call" | custom-call | tf_op jit(solution)/shard_map/cloud_models/pallas_call | solution.py:380
  5.5 0.0 copy-start.1
  5.5 0.1 collective-permute-start.2
  5.6 6.8 %all-to-all-start = ((f32[32,96,128]{2,1,0:T(8,128)}), f32[32,96,128]{2,1,0:T(8,128)S(1)}, u32[]{:S(2)}, u32[]{:S(2)}) async-start(f32[32,96,128]{2,1,0:T(8,128)} %get-tuple-element.17), calls=%async_computation | async-start | bytes 3145728 | tf_op jit(solution)/shard_map/all_to_all | solution.py:412
  12.4 1.6 %collective-permute-done.2 = f32[16,24,128]{2,1,0:T(8,128)S(1)} collective-permute-done((f32[16,24,128]{2,1,0:T(8,128)}, f32[16,24,128]{2,1,0:T(8,128)S(1)}, u32[]{:S(2)}, u32[]{:S(2)}) %collective-permute-start.2) | collective-permute-done | bytes 196640 | tf_op jit(solution)/shard_map/ppermute | solution.py:317
  14.0 0.0 copy-done.1
  14.1 0.0 copy-start.3
  14.1 0.0 copy-start.2
  14.1 0.0 copy-start
  14.1 2.8 %collective-permute-start.3 = (f32[2,8,24,128]{3,2,0,1:T(8,128)S(1)}, f32[2,8,24,128]{3,2,0,1:T(8,128)S(1)}, u32[]{:S(2)}, u32[]{:S(2)}) collective-permute-start(f32[2,8,24,128]{3,2,0,1:T(8,128)S(1)} %copy.9), channel_id=1, source_target_pairs={{0,1},{1,0},{2,3},{3,2},{4,5},{5,4},{6,7},{7,6},{8,9},{9,8},{10,11... | collective-permute-start | bytes 589832 | tf_op jit(solution)/shard_map/ppermute | solution.py:317
  16.9 1.1 %collective-permute-done.3 = f32[2,8,24,128]{3,2,0,1:T(8,128)S(1)} collective-permute-done((f32[2,8,24,128]{3,2,0,1:T(8,128)S(1)}, f32[2,8,24,128]{3,2,0,1:T(8,128)S(1)}, u32[]{:S(2)}, u32[]{:S(2)}) %collective-permute-start.3) | collective-permute-done | bytes 196640 | tf_op jit(solution)/shard_map/ppermute | solution.py:317
  18.0 5.1 %collective-permute-start.4 = (f32[4,2,24,128]{3,2,0,1:T(8,128)S(1)}, f32[4,2,24,128]{3,2,0,1:T(8,128)S(1)}, u32[]{:S(2)}, u32[]{:S(2)}) collective-permute-start(f32[4,2,24,128]{3,2,0,1:T(8,128)S(1)} %pad_maximum_fusion.2), channel_id=1, source_target_pairs={{0,4},{1,5},{2,6},{3,7},{4,0},{5,1},{6,2},{7,3},{8,12},{9,13},{10,... | collective-permute-start | bytes 294920 | tf_op jit(solution)/shard_map/ppermute | solution.py:317
  23.1 0.1 collective-permute-start.5
  23.2 1.2 %collective-permute-start.6 = (f32[4,2,24,128]{3,2,0,1:T(8,128)S(1)}, f32[4,2,24,128]{3,2,0,1:T(8,128)S(1)}, u32[]{:S(2)}, u32[]{:S(2)}) collective-permute-start(f32[4,2,24,128]{3,2,0,1:T(8,128)S(1)} %pad_maximum_fusion.4), channel_id=1, source_target_pairs={{0,6},{1,7},{2,4},{3,5},{4,2},{5,3},{6,0},{7,1},{8,14},{9,15},{10,... | collective-permute-start | bytes 294920 | tf_op jit(solution)/shard_map/ppermute | solution.py:317
  24.4 3.1 %collective-permute-done.4 = f32[4,2,24,128]{3,2,0,1:T(8,128)S(1)} collective-permute-done((f32[4,2,24,128]{3,2,0,1:T(8,128)S(1)}, f32[4,2,24,128]{3,2,0,1:T(8,128)S(1)}, u32[]{:S(2)}, u32[]{:S(2)}) %collective-permute-start.4) | collective-permute-done | bytes 98336 | tf_op jit(solution)/shard_map/ppermute | solution.py:317
  27.5 0.4 collective-permute-done.5
  28.0 3.4 %collective-permute-done.6 = f32[4,2,24,128]{3,2,0,1:T(8,128)S(1)} collective-permute-done((f32[4,2,24,128]{3,2,0,1:T(8,128)S(1)}, f32[4,2,24,128]{3,2,0,1:T(8,128)S(1)}, u32[]{:S(2)}, u32[]{:S(2)}) %collective-permute-start.6) | collective-permute-done | bytes 98336 | tf_op jit(solution)/shard_map/ppermute | solution.py:317
  31.4 9.6 %collective-permute-start.7 = (f32[16,1,24,128]{3,2,0,1:T(8,128)S(1)}, f32[16,1,24,128]{3,2,0,1:T(8,128)S(1)}, u32[]{:S(2)}, u32[]{:S(2)}) collective-permute-start(f32[16,1,24,128]{3,2,0,1:T(8,128)S(1)} %pad_maximum_fusion.1), channel_id=1, source_target_pairs={{0,8},{1,9},{2,10},{3,11},{4,12},{5,13},{6,14},{7,15},{8,0},{9,1},... | collective-permute-start | bytes 589832 | tf_op jit(solution)/shard_map/ppermute | solution.py:317
  41.0 0.0 copy-done.3
  41.0 1.7 %collective-permute-start = (f32[16,128]{1,0:T(8,128)S(1)}, f32[16,128]{1,0:T(8,128)S(1)}, u32[]{:S(2)}, u32[]{:S(2)}) collective-permute-start(f32[16,128]{1,0:T(8,128)S(1)} %copy-done.3), channel_id=1, source_target_pairs={{0,1},{1,2},{2,3},{3,0},{4,5},{5,6},{6,7},{7,4},{8,9},{9,10},{10,1... | collective-permute-start | bytes 24584 | tf_op jit(solution)/shard_map/ppermute | solution.py:312
  42.7 0.0 copy-done.2
  42.7 0.0 collective-permute-start.1
  42.7 0.8 %collective-permute-done.south_ref = f32[16,128]{1,0:T(8,128)S(1)} collective-permute-done((f32[16,128]{1,0:T(8,128)S(1)}, f32[16,128]{1,0:T(8,128)S(1)}, u32[]{:S(2)}, u32[]{:S(2)}) %collective-permute-start) | collective-permute-done | bytes 8224 | tf_op jit(solution)/shard_map/ppermute | solution.py:312
  43.5 2.8 %collective-permute-done.1.north_ref = f32[16,128]{1,0:T(8,128)S(1)} collective-permute-done((f32[16,128]{1,0:T(8,128)S(1)}, f32[16,128]{1,0:T(8,128)S(1)}, u32[]{:S(2)}, u32[]{:S(2)}) %collective-permute-start.1) | collective-permute-done | bytes 8224 | tf_op jit(solution)/shard_map/ppermute | solution.py:312
  46.3 0.1 collective-permute-start.8
  46.3 2.4 %collective-permute-start.9 = (f32[8,128]{1,0:T(8,128)S(1)}, f32[8,128]{1,0:T(8,128)S(1)}, u32[]{:S(2)}, u32[]{:S(2)}) collective-permute-start(f32[8,128]{1,0:T(8,128)S(1)} %get-tuple-element.28), channel_id=1, source_target_pairs={{0,28},{4,0},{8,4},{12,8},{16,12},{20,16},{24,20},{28,24},{1,29},{... | collective-permute-start | bytes 12296 | tf_op jit(solution)/shard_map/ppermute | solution.py:312
  48.7 0.0 collective-permute-done.7
  48.7 1.2 %early_slots.1.refs_0_ = f32[1920,256]{1,0:T(8,128)} custom-call(s32[1]{0:T(128)} %bitcast.refs_0_.me_ref, f32[16,24,128]{2,1,0:T(8,128)S(1)} %fusion.3.refs_0_, f32[16,24,128]{2,1,0:T(8,128)S(1)} %bitcast.20), custom_call_target="tpu_custom_call" | custom-call | flops 12999999488 | bytes 1000000 | tf_op jit(solution)/shard_map/early_slots/pallas_call | solution.py:432
  49.9 2.3 %collective-permute-done.8.west_ref = f32[8,128]{1,0:T(8,128)S(1)} collective-permute-done((f32[8,128]{1,0:T(8,128)S(1)}, f32[8,128]{1,0:T(8,128)S(1)}, u32[]{:S(2)}, u32[]{:S(2)}) %collective-permute-start.8) | collective-permute-done | bytes 4128 | tf_op jit(solution)/shard_map/ppermute | solution.py:312
  52.2 0.0 collective-permute-done.9.east_ref
  52.2 0.1 all-to-all-done
  52.3 2.1 %cloud_slots.1 = (f32[1920,256]{1,0:T(8,128)}, f32[5,128,12]{2,1,0:T(8,128)}) custom-call(f32[3072,128]{1,0:T(8,128)S(1)} %bitcast.19, f32[128,128]{1,0:T(8,128)S(1)} %get-tuple-element.26.sum_ref, f32[8,128]{1,0:T(8,128)S(1)} %collective-permute-done.8.west_ref, f32[8,128]{1,0:T(8,128)S(1)} %collective-permute-done.9.east_ref, ...), custom_call_target="tpu_custom_call", output_to_operand_aliasing={{0}: (4, {})} | custom-call | tf_op jit(solution)/shard_map/cloud_slots/pallas_call | solution.py:446
  (15 shorter events, 0.2 us)
Async XLA Ops:
  5.5 8.5 %copy-start.1 = (f32[16,24,128]{2,1,0:T(8,128)S(1)}, f32[16,24,128]{2,1,0:T(8,128)}, u32[]{:S(2)}) copy-start(f32[16,24,128]{2,1,0:T(8,128)} %get-tuple-element.22) | copy-start | bytes 589828
  5.5 8.5 %collective-permute-start.2 = (f32[16,24,128]{2,1,0:T(8,128)}, f32[16,24,128]{2,1,0:T(8,128)S(1)}, u32[]{:S(2)}, u32[]{:S(2)}) collective-permute-start(f32[16,24,128]{2,1,0:T(8,128)} %get-tuple-element.23), channel_id=1, source_target_pairs={{0,16},{1,17},{2,18},{3,19},{4,20},{5,21},{6,22},{7,23},{8,24},{9,... | collective-permute-start | bytes 589832 | tf_op jit(solution)/shard_map/ppermute | solution.py:317
  5.6 46.7 %all-to-all-start = ((f32[32,96,128]{2,1,0:T(8,128)}), f32[32,96,128]{2,1,0:T(8,128)S(1)}, u32[]{:S(2)}, u32[]{:S(2)}) async-start(f32[32,96,128]{2,1,0:T(8,128)} %get-tuple-element.17), calls=%async_computation | async-start | bytes 3145728 | tf_op jit(solution)/shard_map/all_to_all | solution.py:412
  14.1 26.9 %copy-start.3 = (f32[16,128]{1,0:T(8,128)S(1)}, f32[16,128]{1,0:T(8,128)}, u32[]{:S(2)}) copy-start(f32[16,128]{1,0:T(8,128)} %get-tuple-element.19) | copy-start | bytes 24580
  14.1 28.6 %copy-start.2 = (f32[16,128]{1,0:T(8,128)S(1)}, f32[16,128]{1,0:T(8,128)}, u32[]{:S(2)}) copy-start(f32[16,128]{1,0:T(8,128)} %get-tuple-element.20) | copy-start | bytes 24580
  14.1 32.2 %copy-start = (f32[128,128]{1,0:T(8,128)S(1)}, f32[128,128]{1,0:T(8,128)}, u32[]{:S(2)}) copy-start(f32[128,128]{1,0:T(8,128)} %get-tuple-element.18.nodes_ref) | copy-start | bytes 196612
  14.1 3.9 %collective-permute-start.3 = (f32[2,8,24,128]{3,2,0,1:T(8,128)S(1)}, f32[2,8,24,128]{3,2,0,1:T(8,128)S(1)}, u32[]{:S(2)}, u32[]{:S(2)}) collective-permute-start(f32[2,8,24,128]{3,2,0,1:T(8,128)S(1)} %copy.9), channel_id=1, source_target_pairs={{0,1},{1,0},{2,3},{3,2},{4,5},{5,4},{6,7},{7,6},{8,9},{9,8},{10,11... | collective-permute-start | bytes 589832 | tf_op jit(solution)/shard_map/ppermute | solution.py:317
  18.0 9.5 %collective-permute-start.4 = (f32[4,2,24,128]{3,2,0,1:T(8,128)S(1)}, f32[4,2,24,128]{3,2,0,1:T(8,128)S(1)}, u32[]{:S(2)}, u32[]{:S(2)}) collective-permute-start(f32[4,2,24,128]{3,2,0,1:T(8,128)S(1)} %pad_maximum_fusion.2), channel_id=1, source_target_pairs={{0,4},{1,5},{2,6},{3,7},{4,0},{5,1},{6,2},{7,3},{8,12},{9,13},{10,... | collective-permute-start | bytes 294920 | tf_op jit(solution)/shard_map/ppermute | solution.py:317
  23.1 4.9 %collective-permute-start.5 = (f32[4,2,24,128]{3,2,0,1:T(8,128)S(1)}, f32[4,2,24,128]{3,2,0,1:T(8,128)S(1)}, u32[]{:S(2)}, u32[]{:S(2)}) collective-permute-start(f32[4,2,24,128]{3,2,0,1:T(8,128)S(1)} %pad_maximum_fusion.3), channel_id=1, source_target_pairs={{0,2},{1,3},{2,0},{3,1},{4,6},{5,7},{6,4},{7,5},{8,10},{9,11},{10,... | collective-permute-start | bytes 294920 | tf_op jit(solution)/shard_map/ppermute | solution.py:317
  23.2 8.2 %collective-permute-start.6 = (f32[4,2,24,128]{3,2,0,1:T(8,128)S(1)}, f32[4,2,24,128]{3,2,0,1:T(8,128)S(1)}, u32[]{:S(2)}, u32[]{:S(2)}) collective-permute-start(f32[4,2,24,128]{3,2,0,1:T(8,128)S(1)} %pad_maximum_fusion.4), channel_id=1, source_target_pairs={{0,6},{1,7},{2,4},{3,5},{4,2},{5,3},{6,0},{7,1},{8,14},{9,15},{10,... | collective-permute-start | bytes 294920 | tf_op jit(solution)/shard_map/ppermute | solution.py:317
  31.4 17.3 %collective-permute-start.7 = (f32[16,1,24,128]{3,2,0,1:T(8,128)S(1)}, f32[16,1,24,128]{3,2,0,1:T(8,128)S(1)}, u32[]{:S(2)}, u32[]{:S(2)}) collective-permute-start(f32[16,1,24,128]{3,2,0,1:T(8,128)S(1)} %pad_maximum_fusion.1), channel_id=1, source_target_pairs={{0,8},{1,9},{2,10},{3,11},{4,12},{5,13},{6,14},{7,15},{8,0},{9,1},... | collective-permute-start | bytes 589832 | tf_op jit(solution)/shard_map/ppermute | solution.py:317
  41.0 2.5 %collective-permute-start = (f32[16,128]{1,0:T(8,128)S(1)}, f32[16,128]{1,0:T(8,128)S(1)}, u32[]{:S(2)}, u32[]{:S(2)}) collective-permute-start(f32[16,128]{1,0:T(8,128)S(1)} %copy-done.3), channel_id=1, source_target_pairs={{0,1},{1,2},{2,3},{3,0},{4,5},{5,6},{6,7},{7,4},{8,9},{9,10},{10,1... | collective-permute-start | bytes 24584 | tf_op jit(solution)/shard_map/ppermute | solution.py:312
  42.7 3.6 %collective-permute-start.1 = (f32[16,128]{1,0:T(8,128)S(1)}, f32[16,128]{1,0:T(8,128)S(1)}, u32[]{:S(2)}, u32[]{:S(2)}) collective-permute-start(f32[16,128]{1,0:T(8,128)S(1)} %copy-done.2), channel_id=1, source_target_pairs={{0,3},{1,0},{2,1},{3,2},{4,7},{5,4},{6,5},{7,6},{8,11},{9,8},{10,9... | collective-permute-start | bytes 24584 | tf_op jit(solution)/shard_map/ppermute | solution.py:312
  46.3 6.0 %collective-permute-start.8 = (f32[8,128]{1,0:T(8,128)S(1)}, f32[8,128]{1,0:T(8,128)S(1)}, u32[]{:S(2)}, u32[]{:S(2)}) collective-permute-start(f32[8,128]{1,0:T(8,128)S(1)} %get-tuple-element.27), channel_id=1, source_target_pairs={{0,4},{4,8},{8,12},{12,16},{16,20},{20,24},{24,28},{28,0},{1,5},{5... | collective-permute-start | bytes 12296 | tf_op jit(solution)/shard_map/ppermute | solution.py:312
  46.3 5.9 %collective-permute-start.9 = (f32[8,128]{1,0:T(8,128)S(1)}, f32[8,128]{1,0:T(8,128)S(1)}, u32[]{:S(2)}, u32[]{:S(2)}) collective-permute-start(f32[8,128]{1,0:T(8,128)S(1)} %get-tuple-element.28), channel_id=1, source_target_pairs={{0,28},{4,0},{8,4},{12,8},{16,12},{20,16},{24,20},{28,24},{1,29},{... | collective-permute-start | bytes 12296 | tf_op jit(solution)/shard_map/ppermute | solution.py:312

commit v6 on v5

--- a/solution.py
+++ b/solution.py
@@ -208,8 +208,20 @@
         copy.wait()
 
 
-def kernel_y(elx, ely, side, nodes_ref, south_ref, north_ref, sum_ref, low_ref, high_ref):
+def divided(rows, levels, field, fields):
+    mass = rows[:, fields * levels:(fields + 1) * levels]
+    return rows[:, field * levels:(field + 1) * levels] / mass
+
+
+def face_rows(elx, ely, side):
     step = side * side
+    low = [b * step for b in range(ely)]
+    return low, [((elx - 1) * ely + b) * step + (side - 1) * side for b in range(ely)]
+
+
+def kernel_y(elx, ely, side, nodes_ref, south_ref, north_ref, part_ref, low_ref, high_ref, sum_ref, full_ref):
+    step = side * side
+    field_count, _, levels = part_ref.shape
     sum_ref[...] = nodes_ref[...]
     for a in range(elx):
         for b in range(ely):
@@ -226,36 +238,31 @@
                 gain = north_ref[a * side:(a + 1) * side, :]
             here = pl.ds(base + side - 1, side, stride=side)
             sum_ref[here, :] = nodes_ref[here, :] + gain
-    for b in range(ely):
-        low_ref[b * side:(b + 1) * side, :] = sum_ref[b * step:b * step + side, :]
-        start = (elx - 1) * ely * step + b * step + (side - 1) * side
-        high_ref[b * side:(b + 1) * side, :] = sum_ref[start:start + side, :]
-
-
-def sum_first(elx, ely, side, sum_ref, west_ref, east_ref, out_ref, full_ref):
-    step = side * side
-    field_count, nodes, levels = out_ref.shape
+    for face_ref, starts in zip((low_ref, high_ref), face_rows(elx, ely, side)):
+        for b, start in enumerate(starts):
+            face_ref[b * side:(b + 1) * side, :] = sum_ref[start:start + side, :]
     full_ref[...] = sum_ref[...]
-    for a in range(elx):
+    for a in range(elx - 1):
         for b in range(ely):
-            base = (a * ely + b) * step
-            last = base + (side - 1) * side
-            if a > 0:
-                before = ((a - 1) * ely + b) * step + (side - 1) * side
-                gain = sum_ref[before:before + side, :]
-            else:
-                gain = west_ref[b * side:(b + 1) * side, :]
-            full_ref[base:base + side, :] = sum_ref[base:base + side, :] + gain
-            if a + 1 < elx:
-                after = ((a + 1) * ely + b) * step
-                gain = sum_ref[after:after + side, :]
-            else:
-                gain = east_ref[b * side:(b + 1) * side, :]
-            full_ref[last:last + side, :] = sum_ref[last:last + side, :] + gain
+            last = (a * ely + b) * step + (side - 1) * side
+            after = ((a + 1) * ely + b) * step
+            joined = sum_ref[last:last + side, :] + sum_ref[after:after + side, :]
+            full_ref[last:last + side, :] = joined
+            full_ref[after:after + side, :] = joined
     full = full_ref[...]
-    divisor = full[:, field_count * levels:(field_count + 1) * levels]
     for f in range(field_count):
-        out_ref[f] = full[:, f * levels:(f + 1) * levels] / divisor
+        part_ref[f] = divided(full, levels, f, field_count)
+
+
+def complete_faces(elx, ely, side, low_ref, high_ref, west_ref, east_ref, gcm_ref):
+    field_count, _, levels = gcm_ref.shape
+    lows, highs = face_rows(elx, ely, side)
+    for own_ref, sent_ref, starts in ((low_ref, west_ref, lows), (high_ref, east_ref, highs)):
+        rows = own_ref[...] + sent_ref[...]
+        for f in range(field_count):
+            quotient = divided(rows, levels, f, field_count)
+            for b, start in enumerate(starts):
+                gcm_ref[f, start:start + side, :] = quotient[b * side:(b + 1) * side]
 
 
 def turned_blocks(rows_of, out_hbm, out_ref, sem):
@@ -268,14 +275,23 @@
     return copies
 
 
-def kernel_out(devices, capacity, groups, field_count, early, sizes, recv_ref, sum_ref, west_ref, east_ref, *refs):
-    out_hbm, gcm_hbm, out_ref, gcm_ref, full_ref, sem, gcm_sem = refs[-7:]
-    sum_first(*sizes, sum_ref, west_ref, east_ref, gcm_ref, full_ref)
+def kernel_out(devices, capacity, groups, field_count, early, sizes, recv_ref, part_ref, west_ref, east_ref,
+               low_ref, high_ref, *refs):
+    out_hbm, gcm_hbm, out_ref, gcm_ref, spread_ref, sem, gcm_sem = refs[-7:]
+    gcm_ref[...] = part_ref[...]
+    complete_faces(*sizes, low_ref, high_ref, west_ref, east_ref, gcm_ref)
     gcm_copy = fetch(gcm_ref, gcm_hbm, gcm_sem)
     pitch = recv_ref.shape[0] // devices
 
+    rows_ref = recv_ref
+    if pitch % 16 == 0:
+        rows_ref = spread_ref
+        for source in range(devices):
+            spread_ref[pl.ds(source * (pitch + 8), pitch), :] = recv_ref[pl.ds(source * pitch, pitch), :]
+        pitch = pitch + 8
+
     def rows(first):
-        ranked = [recv_ref[pl.ds(first + r, devices, stride=pitch), :] for r in range(capacity)]
+        ranked = [rows_ref[pl.ds(first + r, devices, stride=pitch), :] for r in range(capacity)]
         return jnp.concatenate(ranked, axis=0)
 
     blocks = groups * field_count - early
@@ -286,15 +302,21 @@
 
 
 def kernel_early(devices, capacity, groups, field_count, early, sources, me_ref, *refs):
-    slots = devices * capacity
+    apart = devices + 8
+    slots = apart * capacity
     *blocks, out_hbm, row_ref, out_ref, sem = refs
     arrived = [(ref, index) for ref in blocks for index in range(ref.shape[0])]
     for (ref, index), bits in zip(arrived, sources):
         for e in range(early):
             tile = ref[index, pl.ds(e * capacity, capacity), :]
-            row_ref[pl.ds(e * slots + (me_ref[0] ^ bits), capacity, stride=devices), :] = tile
+            row_ref[pl.ds(e * slots + (me_ref[0] ^ bits), capacity, stride=apart), :] = tile
     steps = [(field_count - early + e) * groups + groups - 1 for e in range(early)]
-    rows_of = [(step, lambda e=e: row_ref[e * slots:(e + 1) * slots, :]) for e, step in enumerate(steps)]
+
+    def slots_at(first):
+        ranked = [row_ref[first + r * apart:first + r * apart + devices, :] for r in range(capacity)]
+        return jnp.concatenate(ranked, axis=0)
+
+    rows_of = [(step, functools.partial(slots_at, e * slots)) for e, step in enumerate(steps)]
     for copy in turned_blocks(rows_of, out_hbm, out_ref, sem):
         copy.wait()
 
@@ -414,9 +436,10 @@
         arrived, sources = hops(near, far, devices)
     north = shift(low, "ey", -1)
     south = shift(high, "ey", 1)
-    summed, low, high = pl.pallas_call(
+    part, low, high = pl.pallas_call(
         functools.partial(kernel_y, *sizes),
-        out_shape=(square, face_x, face_x),
+        out_shape=(jax.ShapeDtypeStruct((field_count, owned, levels), f32), face_x, face_x),
+        scratch_shapes=[pltpu.VMEM((owned, owned), f32)] * 2,
         compiler_params=params(8),
         cost_estimate=cost(10**5, 10**5),
         name="edge_sum_second",
@@ -424,7 +447,7 @@
     east = shift(low, "ex", -1)
     west = shift(high, "ex", 1)
     if early:
-        summed, arrived[-1] = lax.optimization_barrier((summed, arrived[-1]))
+        part, arrived[-1] = lax.optimization_barrier((part, arrived[-1]))
     out_shape = jax.ShapeDtypeStruct((values, slots), f32)
     block_count = values // owned
     begun = []
@@ -435,7 +458,7 @@
             out_specs=in_hbm,
             out_shape=out_shape,
             scratch_shapes=[
-                pltpu.VMEM((early * slots, owned), f32),
+                pltpu.VMEM((early * (devices + 8) * capacity, owned), f32),
                 pltpu.VMEM((early * owned, slots), f32),
                 pltpu.SemaphoreType.DMA((early,)),
             ],
@@ -445,20 +468,20 @@
         )(me, *arrived))
     cloud, gcm_out = pl.pallas_call(
         functools.partial(kernel_out, devices, capacity, groups, field_count, early, sizes),
-        in_specs=[in_vmem] * 4 + [in_hbm] * len(begun),
+        in_specs=[in_vmem] * 6 + [in_hbm] * len(begun),
         out_specs=(in_hbm, in_hbm),
         out_shape=(out_shape, jax.ShapeDtypeStruct((field_count, owned, levels), f32)),
-        input_output_aliases={4: 0} if begun else {},
+        input_output_aliases={6: 0} if begun else {},
         scratch_shapes=[
             pltpu.VMEM(((block_count - early) * owned, slots), f32),
             pltpu.VMEM((field_count, owned, levels), f32),
-            pltpu.VMEM((owned, owned), f32),
+            pltpu.VMEM((devices * ((block_count - early) * capacity + 8), owned), f32),
             pltpu.SemaphoreType.DMA((block_count - early,)),
             pltpu.SemaphoreType.DMA,
         ],
         compiler_params=params(16),
         name="cloud_slots",
-    )(received.reshape(-1, owned), summed, west, east, *begun)
+    )(received.reshape(-1, owned), part, west, east, low, high, *begun)
     gcm_out = gcm_out.reshape(field_count, elx, ely, side, side, levels).transpose(0, 5, 1, 2, 3, 4)
     return cloud.reshape(field_count, levels, width, slots), gcm_out
 

time: 55.2 us -> 54.6 us (0.989)
  no operation moved by 1% of the time
where the time goes in v6:
time: 54.6 us; the launch traced here: 53.9 us
  starting transfers between devices  29.7 us (54%)
  waiting for transfers between devices  15.6 us (29%)
  Pallas kernels  7.74 us (14%)
  between operations  0.78 us (1%)
    ppermute x6, starting transfers between devices, exchange(): return lax.ppermute(block, AXES, [(i, i ^ bits) for i in range(count)])  18.8 us
    ppermute x6, waiting for transfers between devices, exchange(): return lax.ppermute(block, AXES, [(i, i ^ bits) for i in range(count)])  9.64 us
    all_to_all x1, starting transfers between devices, body(): lax.all_to_all(send, AXES, split_axis=0, concat_axis=0, tiled=True)  6.8 us
    ppermute x4, waiting for transfers between devices, shift(): lax.ppermute(face, axis, [(i, (i + by) % count) for i in range(count)])  5.83 us
    pallas_call x1, Pallas kernels, body(): pl.pallas_call(functools.partial(kernel_a, devices, capacity, early, *siz...  4.86 us
    ppermute x4, starting transfers between devices, shift(): lax.ppermute(face, axis, [(i, (i + by) % count) for i in range(count)])  4.07 us
    pallas_call x1, Pallas kernels, body(): pl.pallas_call(functools.partial(kernel_out, devices, capacity, groups, f...  1.58 us
  transfers between devices with their start and end apart: 11, of which 9 were waited for; matrix products, arithmetic and copies ran while one was open for 0% of the time, Pallas kernels for 2%

profile of v6, /device:TPU:17, one launch (start us, length us, event | category | flops | bytes accessed | tf_op | source)
XLA Modules:
  0.0 53.9 jit_solution(18379306329784529177)
XLA Ops:
  0.6 4.9 %cloud_models.1 = (f32[32,96,128]{2,1,0:T(8,128)}, f32[16,24,128]{2,1,0:T(8,128)}, f32[16,24,128]{2,1,0:T(8,128)}, f32[128,128]{1,0:T(8,128)}, f32[16,128]{1,0:T(8,128)}, /*index=5*/f32[16,128]{1,0:T(8,128)}) custom-call(s32[1]{0:T(128)} %bitcast.refs_0_.me_ref, f32[5,12,32,128]{3,2,1,0:T(8,128)} %refs_1_.1, f32[5,128,12]{2,1,0:T(8,128)} %bitcast.24, ...), custom_call_target="tpu_custom_call" | custom-call | tf_op jit(solution)/shard_map/cloud_models/pallas_call | solution.py:402
  5.5 0.0 copy-start.1
  5.5 0.1 collective-permute-start.2
  5.6 6.8 %all-to-all-start = ((f32[32,96,128]{2,1,0:T(8,128)}), f32[32,96,128]{2,1,0:T(8,128)S(1)}, u32[]{:S(2)}, u32[]{:S(2)}) async-start(f32[32,96,128]{2,1,0:T(8,128)} %get-tuple-element.17), calls=%async_computation | async-start | bytes 3145728 | tf_op jit(solution)/shard_map/all_to_all | solution.py:434
  12.4 1.6 %collective-permute-done.2 = f32[16,24,128]{2,1,0:T(8,128)S(1)} collective-permute-done((f32[16,24,128]{2,1,0:T(8,128)}, f32[16,24,128]{2,1,0:T(8,128)S(1)}, u32[]{:S(2)}, u32[]{:S(2)}) %collective-permute-start.2) | collective-permute-done | bytes 196640 | tf_op jit(solution)/shard_map/ppermute | solution.py:339
  14.0 0.0 copy-done.1
  14.1 0.0 copy-start.3
  14.1 0.0 copy-start.2
  14.1 0.0 copy-start
  14.1 2.8 %collective-permute-start.3 = (f32[2,8,24,128]{3,2,0,1:T(8,128)S(1)}, f32[2,8,24,128]{3,2,0,1:T(8,128)S(1)}, u32[]{:S(2)}, u32[]{:S(2)}) collective-permute-start(f32[2,8,24,128]{3,2,0,1:T(8,128)S(1)} %copy.9), channel_id=1, source_target_pairs={{0,1},{1,0},{2,3},{3,2},{4,5},{5,4},{6,7},{7,6},{8,9},{9,8},{10,11... | collective-permute-start | bytes 589832 | tf_op jit(solution)/shard_map/ppermute | solution.py:339
  16.9 1.1 %collective-permute-done.3 = f32[2,8,24,128]{3,2,0,1:T(8,128)S(1)} collective-permute-done((f32[2,8,24,128]{3,2,0,1:T(8,128)S(1)}, f32[2,8,24,128]{3,2,0,1:T(8,128)S(1)}, u32[]{:S(2)}, u32[]{:S(2)}) %collective-permute-start.3) | collective-permute-done | bytes 196640 | tf_op jit(solution)/shard_map/ppermute | solution.py:339
  18.0 5.1 %collective-permute-start.4 = (f32[4,2,24,128]{3,2,0,1:T(8,128)S(1)}, f32[4,2,24,128]{3,2,0,1:T(8,128)S(1)}, u32[]{:S(2)}, u32[]{:S(2)}) collective-permute-start(f32[4,2,24,128]{3,2,0,1:T(8,128)S(1)} %pad_maximum_fusion.2), channel_id=1, source_target_pairs={{0,4},{1,5},{2,6},{3,7},{4,0},{5,1},{6,2},{7,3},{8,12},{9,13},{10,... | collective-permute-start | bytes 294920 | tf_op jit(solution)/shard_map/ppermute | solution.py:339
  23.1 0.1 collective-permute-start.5
  23.2 1.2 %collective-permute-start.6 = (f32[4,2,24,128]{3,2,0,1:T(8,128)S(1)}, f32[4,2,24,128]{3,2,0,1:T(8,128)S(1)}, u32[]{:S(2)}, u32[]{:S(2)}) collective-permute-start(f32[4,2,24,128]{3,2,0,1:T(8,128)S(1)} %pad_maximum_fusion.4), channel_id=1, source_target_pairs={{0,6},{1,7},{2,4},{3,5},{4,2},{5,3},{6,0},{7,1},{8,14},{9,15},{10,... | collective-permute-start | bytes 294920 | tf_op jit(solution)/shard_map/ppermute | solution.py:339
  24.4 3.1 %collective-permute-done.4 = f32[4,2,24,128]{3,2,0,1:T(8,128)S(1)} collective-permute-done((f32[4,2,24,128]{3,2,0,1:T(8,128)S(1)}, f32[4,2,24,128]{3,2,0,1:T(8,128)S(1)}, u32[]{:S(2)}, u32[]{:S(2)}) %collective-permute-start.4) | collective-permute-done | bytes 98336 | tf_op jit(solution)/shard_map/ppermute | solution.py:339
  27.5 0.4 collective-permute-done.5
  28.0 3.4 %collective-permute-done.6 = f32[4,2,24,128]{3,2,0,1:T(8,128)S(1)} collective-permute-done((f32[4,2,24,128]{3,2,0,1:T(8,128)S(1)}, f32[4,2,24,128]{3,2,0,1:T(8,128)S(1)}, u32[]{:S(2)}, u32[]{:S(2)}) %collective-permute-start.6) | collective-permute-done | bytes 98336 | tf_op jit(solution)/shard_map/ppermute | solution.py:339
  31.4 9.6 %collective-permute-start.7 = (f32[16,1,24,128]{3,2,0,1:T(8,128)S(1)}, f32[16,1,24,128]{3,2,0,1:T(8,128)S(1)}, u32[]{:S(2)}, u32[]{:S(2)}) collective-permute-start(f32[16,1,24,128]{3,2,0,1:T(8,128)S(1)} %pad_maximum_fusion.1), channel_id=1, source_target_pairs={{0,8},{1,9},{2,10},{3,11},{4,12},{5,13},{6,14},{7,15},{8,0},{9,1},... | collective-permute-start | bytes 589832 | tf_op jit(solution)/shard_map/ppermute | solution.py:339
  41.0 1.7 %collective-permute-start = (f32[16,128]{1,0:T(8,128)S(1)}, f32[16,128]{1,0:T(8,128)S(1)}, u32[]{:S(2)}, u32[]{:S(2)}) collective-permute-start(f32[16,128]{1,0:T(8,128)S(1)} %copy-done.3), channel_id=1, source_target_pairs={{0,1},{1,2},{2,3},{3,0},{4,5},{5,6},{6,7},{7,4},{8,9},{9,10},{10,1... | collective-permute-start | bytes 24584 | tf_op jit(solution)/shard_map/ppermute | solution.py:334
  42.7 0.0 copy-done.2
  42.7 0.0 collective-permute-start.1
  42.7 0.8 %collective-permute-done.south_ref = f32[16,128]{1,0:T(8,128)S(1)} collective-permute-done((f32[16,128]{1,0:T(8,128)S(1)}, f32[16,128]{1,0:T(8,128)S(1)}, u32[]{:S(2)}, u32[]{:S(2)}) %collective-permute-start) | collective-permute-done | bytes 8224 | tf_op jit(solution)/shard_map/ppermute | solution.py:334
  43.5 2.8 %collective-permute-done.1.north_ref = f32[16,128]{1,0:T(8,128)S(1)} collective-permute-done((f32[16,128]{1,0:T(8,128)S(1)}, f32[16,128]{1,0:T(8,128)S(1)}, u32[]{:S(2)}, u32[]{:S(2)}) %collective-permute-start.1) | collective-permute-done | bytes 8224 | tf_op jit(solution)/shard_map/ppermute | solution.py:334
  46.3 0.3 edge_sum_second.1
  46.6 0.1 collective-permute-start.8
  46.6 2.4 %collective-permute-start.9 = (f32[8,128]{1,0:T(8,128)S(1)}, f32[8,128]{1,0:T(8,128)S(1)}, u32[]{:S(2)}, u32[]{:S(2)}) collective-permute-start(f32[8,128]{1,0:T(8,128)S(1)} %get-tuple-element.28.low_ref), channel_id=1, source_target_pairs={{0,28},{4,0},{8,4},{12,8},{16,12},{20,16},{24,20},{28,24},{1,29},{... | collective-permute-start | bytes 12296 | tf_op jit(solution)/shard_map/ppermute | solution.py:334
  49.0 0.0 collective-permute-done.7
  49.0 1.0 %early_slots.1.refs_0_ = f32[1920,256]{1,0:T(8,128)} custom-call(s32[1]{0:T(128)} %bitcast.refs_0_.me_ref, f32[16,24,128]{2,1,0:T(8,128)S(1)} %fusion.3.refs_0_, f32[16,24,128]{2,1,0:T(8,128)S(1)} %bitcast.20), custom_call_target="tpu_custom_call" | custom-call | flops 12999999488 | bytes 1000000 | tf_op jit(solution)/shard_map/early_slots/pallas_call | solution.py:455
  50.0 2.3 %collective-permute-done.8.west_ref = f32[8,128]{1,0:T(8,128)S(1)} collective-permute-done((f32[8,128]{1,0:T(8,128)S(1)}, f32[8,128]{1,0:T(8,128)S(1)}, u32[]{:S(2)}, u32[]{:S(2)}) %collective-permute-start.8) | collective-permute-done | bytes 4128 | tf_op jit(solution)/shard_map/ppermute | solution.py:334
  52.2 0.0 collective-permute-done.9.east_ref
  52.2 0.1 all-to-all-done
  52.3 1.6 %cloud_slots.1 = (f32[1920,256]{1,0:T(8,128)}, f32[5,128,12]{2,1,0:T(8,128)}) custom-call(f32[3072,128]{1,0:T(8,128)S(1)} %bitcast.19, f32[5,128,12]{2,1,0:T(8,128)S(1)} %get-tuple-element.26.part_ref, f32[8,128]{1,0:T(8,128)S(1)} %collective-permute-done.8.west_ref, f32[8,128]{1,0:T(8,128)S(1)} %collective-permute-done.9.east_ref, ...), custom_call_target="tpu_custom_call", output_to_operand_aliasing={{0}: (6, {})} | custom-call | tf_op jit(solution)/shard_map/cloud_slots/pallas_call | solution.py:469
  (15 shorter events, 0.2 us)
Async XLA Ops:
  5.5 8.5 %copy-start.1 = (f32[16,24,128]{2,1,0:T(8,128)S(1)}, f32[16,24,128]{2,1,0:T(8,128)}, u32[]{:S(2)}) copy-start(f32[16,24,128]{2,1,0:T(8,128)} %get-tuple-element.22) | copy-start | bytes 589828
  5.5 8.5 %collective-permute-start.2 = (f32[16,24,128]{2,1,0:T(8,128)}, f32[16,24,128]{2,1,0:T(8,128)S(1)}, u32[]{:S(2)}, u32[]{:S(2)}) collective-permute-start(f32[16,24,128]{2,1,0:T(8,128)} %get-tuple-element.23), channel_id=1, source_target_pairs={{0,16},{1,17},{2,18},{3,19},{4,20},{5,21},{6,22},{7,23},{8,24},{9,... | collective-permute-start | bytes 589832 | tf_op jit(solution)/shard_map/ppermute | solution.py:339
  5.6 46.7 %all-to-all-start = ((f32[32,96,128]{2,1,0:T(8,128)}), f32[32,96,128]{2,1,0:T(8,128)S(1)}, u32[]{:S(2)}, u32[]{:S(2)}) async-start(f32[32,96,128]{2,1,0:T(8,128)} %get-tuple-element.17), calls=%async_computation | async-start | bytes 3145728 | tf_op jit(solution)/shard_map/all_to_all | solution.py:434
  14.1 26.9 %copy-start.3 = (f32[16,128]{1,0:T(8,128)S(1)}, f32[16,128]{1,0:T(8,128)}, u32[]{:S(2)}) copy-start(f32[16,128]{1,0:T(8,128)} %get-tuple-element.19) | copy-start | bytes 24580
  14.1 28.6 %copy-start.2 = (f32[16,128]{1,0:T(8,128)S(1)}, f32[16,128]{1,0:T(8,128)}, u32[]{:S(2)}) copy-start(f32[16,128]{1,0:T(8,128)} %get-tuple-element.20) | copy-start | bytes 24580
  14.1 32.2 %copy-start = (f32[128,128]{1,0:T(8,128)S(1)}, f32[128,128]{1,0:T(8,128)}, u32[]{:S(2)}) copy-start(f32[128,128]{1,0:T(8,128)} %get-tuple-element.18.nodes_ref) | copy-start | bytes 196612
  14.1 3.9 %collective-permute-start.3 = (f32[2,8,24,128]{3,2,0,1:T(8,128)S(1)}, f32[2,8,24,128]{3,2,0,1:T(8,128)S(1)}, u32[]{:S(2)}, u32[]{:S(2)}) collective-permute-start(f32[2,8,24,128]{3,2,0,1:T(8,128)S(1)} %copy.9), channel_id=1, source_target_pairs={{0,1},{1,0},{2,3},{3,2},{4,5},{5,4},{6,7},{7,6},{8,9},{9,8},{10,11... | collective-permute-start | bytes 589832 | tf_op jit(solution)/shard_map/ppermute | solution.py:339
  18.0 9.5 %collective-permute-start.4 = (f32[4,2,24,128]{3,2,0,1:T(8,128)S(1)}, f32[4,2,24,128]{3,2,0,1:T(8,128)S(1)}, u32[]{:S(2)}, u32[]{:S(2)}) collective-permute-start(f32[4,2,24,128]{3,2,0,1:T(8,128)S(1)} %pad_maximum_fusion.2), channel_id=1, source_target_pairs={{0,4},{1,5},{2,6},{3,7},{4,0},{5,1},{6,2},{7,3},{8,12},{9,13},{10,... | collective-permute-start | bytes 294920 | tf_op jit(solution)/shard_map/ppermute | solution.py:339
  23.1 4.9 %collective-permute-start.5 = (f32[4,2,24,128]{3,2,0,1:T(8,128)S(1)}, f32[4,2,24,128]{3,2,0,1:T(8,128)S(1)}, u32[]{:S(2)}, u32[]{:S(2)}) collective-permute-start(f32[4,2,24,128]{3,2,0,1:T(8,128)S(1)} %pad_maximum_fusion.3), channel_id=1, source_target_pairs={{0,2},{1,3},{2,0},{3,1},{4,6},{5,7},{6,4},{7,5},{8,10},{9,11},{10,... | collective-permute-start | bytes 294920 | tf_op jit(solution)/shard_map/ppermute | solution.py:339
  23.2 8.2 %collective-permute-start.6 = (f32[4,2,24,128]{3,2,0,1:T(8,128)S(1)}, f32[4,2,24,128]{3,2,0,1:T(8,128)S(1)}, u32[]{:S(2)}, u32[]{:S(2)}) collective-permute-start(f32[4,2,24,128]{3,2,0,1:T(8,128)S(1)} %pad_maximum_fusion.4), channel_id=1, source_target_pairs={{0,6},{1,7},{2,4},{3,5},{4,2},{5,3},{6,0},{7,1},{8,14},{9,15},{10,... | collective-permute-start | bytes 294920 | tf_op jit(solution)/shard_map/ppermute | solution.py:339
  31.4 17.6 %collective-permute-start.7 = (f32[16,1,24,128]{3,2,0,1:T(8,128)S(1)}, f32[16,1,24,128]{3,2,0,1:T(8,128)S(1)}, u32[]{:S(2)}, u32[]{:S(2)}) collective-permute-start(f32[16,1,24,128]{3,2,0,1:T(8,128)S(1)} %pad_maximum_fusion.1), channel_id=1, source_target_pairs={{0,8},{1,9},{2,10},{3,11},{4,12},{5,13},{6,14},{7,15},{8,0},{9,1},... | collective-permute-start | bytes 589832 | tf_op jit(solution)/shard_map/ppermute | solution.py:339
  41.0 2.5 %collective-permute-start = (f32[16,128]{1,0:T(8,128)S(1)}, f32[16,128]{1,0:T(8,128)S(1)}, u32[]{:S(2)}, u32[]{:S(2)}) collective-permute-start(f32[16,128]{1,0:T(8,128)S(1)} %copy-done.3), channel_id=1, source_target_pairs={{0,1},{1,2},{2,3},{3,0},{4,5},{5,6},{6,7},{7,4},{8,9},{9,10},{10,1... | collective-permute-start | bytes 24584 | tf_op jit(solution)/shard_map/ppermute | solution.py:334
  42.7 3.6 %collective-permute-start.1 = (f32[16,128]{1,0:T(8,128)S(1)}, f32[16,128]{1,0:T(8,128)S(1)}, u32[]{:S(2)}, u32[]{:S(2)}) collective-permute-start(f32[16,128]{1,0:T(8,128)S(1)} %copy-done.2), channel_id=1, source_target_pairs={{0,3},{1,0},{2,1},{3,2},{4,7},{5,4},{6,5},{7,6},{8,11},{9,8},{10,9... | collective-permute-start | bytes 24584 | tf_op jit(solution)/shard_map/ppermute | solution.py:334
  46.6 5.7 %collective-permute-start.8 = (f32[8,128]{1,0:T(8,128)S(1)}, f32[8,128]{1,0:T(8,128)S(1)}, u32[]{:S(2)}, u32[]{:S(2)}) collective-permute-start(f32[8,128]{1,0:T(8,128)S(1)} %get-tuple-element.27.high_ref), channel_id=1, source_target_pairs={{0,4},{4,8},{8,12},{12,16},{16,20},{20,24},{24,28},{28,0},{1,5},{5... | collective-permute-start | bytes 12296 | tf_op jit(solution)/shard_map/ppermute | solution.py:334
  46.6 5.6 %collective-permute-start.9 = (f32[8,128]{1,0:T(8,128)S(1)}, f32[8,128]{1,0:T(8,128)S(1)}, u32[]{:S(2)}, u32[]{:S(2)}) collective-permute-start(f32[8,128]{1,0:T(8,128)S(1)} %get-tuple-element.28.low_ref), channel_id=1, source_target_pairs={{0,28},{4,0},{8,4},{12,8},{16,12},{20,16},{24,20},{28,24},{1,29},{... | collective-permute-start | bytes 12296 | tf_op jit(solution)/shard_map/ppermute | solution.py:334

commit v7 on v6

--- a/solution.py
+++ b/solution.py
@@ -441,7 +441,7 @@
         out_shape=(jax.ShapeDtypeStruct((field_count, owned, levels), f32), face_x, face_x),
         scratch_shapes=[pltpu.VMEM((owned, owned), f32)] * 2,
         compiler_params=params(8),
-        cost_estimate=cost(10**5, 10**5),
+        cost_estimate=cost(10**9, 10**5),
         name="edge_sum_second",
     )(nodes, south, north)
     east = shift(low, "ex", -1)

time: 54.6 us -> 54.6 us (level)
    ppermute x6, waiting for transfers between devices: 9.64 us -> 12.6 us  [exchange(): return lax.ppermute(block, AXES, [(i, i ^ bits) for i in range(count)])]
    ppermute x4, waiting for transfers between devices: 5.83 us -> 3.01 us  [shift(): lax.ppermute(face, axis, [(i, (i + by) % count) for i in range(count)])]
  transfers between devices with their start and end apart: 11 -> 11, of which waited for: 9 -> 8; matrix products, arithmetic and copies ran while one was open for 0% -> 0% of each run, Pallas kernels for 2% -> 2%
where the time goes in v7:
time: 54.6 us; the launch traced here: 53.9 us
  starting transfers between devices  29.6 us (54%)
  waiting for transfers between devices  15.7 us (29%)
  Pallas kernels  7.74 us (14%)
  between operations  0.78 us (1%)
    ppermute x6, starting transfers between devices, exchange(): return lax.ppermute(block, AXES, [(i, i ^ bits) for i in range(count)])  18.8 us
    ppermute x6, waiting for transfers between devices, exchange(): return lax.ppermute(block, AXES, [(i, i ^ bits) for i in range(count)])  12.6 us
    all_to_all x1, starting transfers between devices, body(): lax.all_to_all(send, AXES, split_axis=0, concat_axis=0, tiled=True)  6.8 us
    pallas_call x1, Pallas kernels, body(): pl.pallas_call(functools.partial(kernel_a, devices, capacity, early, *siz...  4.86 us
    ppermute x4, starting transfers between devices, shift(): lax.ppermute(face, axis, [(i, (i + by) % count) for i in range(count)])  3.91 us
    ppermute x4, waiting for transfers between devices, shift(): lax.ppermute(face, axis, [(i, (i + by) % count) for i in range(count)])  3.01 us
    pallas_call x1, Pallas kernels, body(): pl.pallas_call(functools.partial(kernel_out, devices, capacity, groups, f...  1.58 us
  transfers between devices with their start and end apart: 11, of which 8 were waited for; matrix products, arithmetic and copies ran while one was open for 0% of the time, Pallas kernels for 2%

profile of v7, /device:TPU:17, one launch (start us, length us, event | category | flops | bytes accessed | tf_op | source)
XLA Modules:
  0.0 53.9 jit_solution(9806806473241531335)
XLA Ops:
  0.6 4.9 %cloud_models.1 = (f32[32,96,128]{2,1,0:T(8,128)}, f32[16,24,128]{2,1,0:T(8,128)}, f32[16,24,128]{2,1,0:T(8,128)}, f32[128,128]{1,0:T(8,128)}, f32[16,128]{1,0:T(8,128)}, /*index=5*/f32[16,128]{1,0:T(8,128)}) custom-call(s32[1]{0:T(128)} %bitcast.refs_0_.me_ref, f32[5,12,32,128]{3,2,1,0:T(8,128)} %refs_1_.1, f32[5,128,12]{2,1,0:T(8,128)} %bitcast.24, ...), custom_call_target="tpu_custom_call" | custom-call | tf_op jit(solution)/shard_map/cloud_models/pallas_call | solution.py:402
  5.5 0.0 copy-start.3
  5.5 0.0 copy-start
  5.5 0.1 collective-permute-start.2
  5.6 6.8 %all-to-all-start = ((f32[32,96,128]{2,1,0:T(8,128)}), f32[32,96,128]{2,1,0:T(8,128)S(1)}, u32[]{:S(2)}, u32[]{:S(2)}) async-start(f32[32,96,128]{2,1,0:T(8,128)} %get-tuple-element.17), calls=%async_computation | async-start | bytes 3145728 | tf_op jit(solution)/shard_map/all_to_all | solution.py:434
  12.4 0.0 copy-done.3
  12.4 1.5 %collective-permute-start = (f32[16,128]{1,0:T(8,128)S(1)}, f32[16,128]{1,0:T(8,128)S(1)}, u32[]{:S(2)}, u32[]{:S(2)}) collective-permute-start(f32[16,128]{1,0:T(8,128)S(1)} %copy-done.3), channel_id=1, source_target_pairs={{0,1},{1,2},{2,3},{3,0},{4,5},{5,6},{6,7},{7,4},{8,9},{9,10},{10,1... | collective-permute-start | bytes 24584 | tf_op jit(solution)/shard_map/ppermute | solution.py:334
  13.9 0.0 copy-done.2
  13.9 0.0 collective-permute-start.1
  13.9 0.1 collective-permute-done.2
  14.1 0.0 copy-start.1
  14.1 2.8 %collective-permute-start.3 = (f32[2,8,24,128]{3,2,0,1:T(8,128)S(1)}, f32[2,8,24,128]{3,2,0,1:T(8,128)S(1)}, u32[]{:S(2)}, u32[]{:S(2)}) collective-permute-start(f32[2,8,24,128]{3,2,0,1:T(8,128)S(1)} %copy.9), channel_id=1, source_target_pairs={{0,1},{1,0},{2,3},{3,2},{4,5},{5,4},{6,7},{7,6},{8,9},{9,8},{10,11... | collective-permute-start | bytes 589832 | tf_op jit(solution)/shard_map/ppermute | solution.py:339
  16.9 1.1 %collective-permute-done.3 = f32[2,8,24,128]{3,2,0,1:T(8,128)S(1)} collective-permute-done((f32[2,8,24,128]{3,2,0,1:T(8,128)S(1)}, f32[2,8,24,128]{3,2,0,1:T(8,128)S(1)}, u32[]{:S(2)}, u32[]{:S(2)}) %collective-permute-start.3) | collective-permute-done | bytes 196640 | tf_op jit(solution)/shard_map/ppermute | solution.py:339
  18.0 5.1 %collective-permute-start.4 = (f32[4,2,24,128]{3,2,0,1:T(8,128)S(1)}, f32[4,2,24,128]{3,2,0,1:T(8,128)S(1)}, u32[]{:S(2)}, u32[]{:S(2)}) collective-permute-start(f32[4,2,24,128]{3,2,0,1:T(8,128)S(1)} %pad_maximum_fusion.2), channel_id=1, source_target_pairs={{0,4},{1,5},{2,6},{3,7},{4,0},{5,1},{6,2},{7,3},{8,12},{9,13},{10,... | collective-permute-start | bytes 294920 | tf_op jit(solution)/shard_map/ppermute | solution.py:339
  23.1 0.1 collective-permute-start.5
  23.2 1.2 %collective-permute-start.6 = (f32[4,2,24,128]{3,2,0,1:T(8,128)S(1)}, f32[4,2,24,128]{3,2,0,1:T(8,128)S(1)}, u32[]{:S(2)}, u32[]{:S(2)}) collective-permute-start(f32[4,2,24,128]{3,2,0,1:T(8,128)S(1)} %pad_maximum_fusion.4), channel_id=1, source_target_pairs={{0,6},{1,7},{2,4},{3,5},{4,2},{5,3},{6,0},{7,1},{8,14},{9,15},{10,... | collective-permute-start | bytes 294920 | tf_op jit(solution)/shard_map/ppermute | solution.py:339
  24.4 3.1 %collective-permute-done.4 = f32[4,2,24,128]{3,2,0,1:T(8,128)S(1)} collective-permute-done((f32[4,2,24,128]{3,2,0,1:T(8,128)S(1)}, f32[4,2,24,128]{3,2,0,1:T(8,128)S(1)}, u32[]{:S(2)}, u32[]{:S(2)}) %collective-permute-start.4) | collective-permute-done | bytes 98336 | tf_op jit(solution)/shard_map/ppermute | solution.py:339
  27.5 0.4 collective-permute-done.5
  28.0 3.4 %collective-permute-done.6 = f32[4,2,24,128]{3,2,0,1:T(8,128)S(1)} collective-permute-done((f32[4,2,24,128]{3,2,0,1:T(8,128)S(1)}, f32[4,2,24,128]{3,2,0,1:T(8,128)S(1)}, u32[]{:S(2)}, u32[]{:S(2)}) %collective-permute-start.6) | collective-permute-done | bytes 98336 | tf_op jit(solution)/shard_map/ppermute | solution.py:339
  31.4 9.6 %collective-permute-start.7 = (f32[16,1,24,128]{3,2,0,1:T(8,128)S(1)}, f32[16,1,24,128]{3,2,0,1:T(8,128)S(1)}, u32[]{:S(2)}, u32[]{:S(2)}) collective-permute-start(f32[16,1,24,128]{3,2,0,1:T(8,128)S(1)} %pad_maximum_fusion.1), channel_id=1, source_target_pairs={{0,8},{1,9},{2,10},{3,11},{4,12},{5,13},{6,14},{7,15},{8,0},{9,1},... | collective-permute-start | bytes 589832 | tf_op jit(solution)/shard_map/ppermute | solution.py:339
  41.0 0.0 collective-permute-done.south_ref
  41.0 0.0 collective-permute-done.1.north_ref
  41.0 0.0 copy-done.1
  41.0 0.3 edge_sum_second.1
  41.4 1.0 %collective-permute-start.8 = (f32[8,128]{1,0:T(8,128)S(1)}, f32[8,128]{1,0:T(8,128)S(1)}, u32[]{:S(2)}, u32[]{:S(2)}) collective-permute-start(f32[8,128]{1,0:T(8,128)S(1)} %get-tuple-element.27.high_ref), channel_id=1, source_target_pairs={{0,4},{4,8},{8,12},{12,16},{16,20},{20,24},{24,28},{28,0},{1,5},{5... | collective-permute-start | bytes 12296 | tf_op jit(solution)/shard_map/ppermute | solution.py:334
  42.4 1.4 %collective-permute-start.9 = (f32[8,128]{1,0:T(8,128)S(1)}, f32[8,128]{1,0:T(8,128)S(1)}, u32[]{:S(2)}, u32[]{:S(2)}) collective-permute-start(f32[8,128]{1,0:T(8,128)S(1)} %get-tuple-element.28.low_ref), channel_id=1, source_target_pairs={{0,28},{4,0},{8,4},{12,8},{16,12},{20,16},{24,20},{28,24},{1,29},{... | collective-permute-start | bytes 12296 | tf_op jit(solution)/shard_map/ppermute | solution.py:334
  43.8 4.5 %collective-permute-done.7 = f32[16,1,24,128]{3,2,0,1:T(8,128)S(1)} collective-permute-done((f32[16,1,24,128]{3,2,0,1:T(8,128)S(1)}, f32[16,1,24,128]{3,2,0,1:T(8,128)S(1)}, u32[]{:S(2)}, u32[]{:S(2)}) %collective-permute-start.7) | collective-permute-done | bytes 196640 | tf_op jit(solution)/shard_map/ppermute | solution.py:339
  48.3 0.9 %early_slots.1.refs_0_ = f32[1920,256]{1,0:T(8,128)} custom-call(s32[1]{0:T(128)} %bitcast.refs_0_.me_ref, f32[16,24,128]{2,1,0:T(8,128)S(1)} %fusion.3.refs_0_, f32[16,24,128]{2,1,0:T(8,128)S(1)} %bitcast.20), custom_call_target="tpu_custom_call" | custom-call | flops 12999999488 | bytes 1000000 | tf_op jit(solution)/shard_map/early_slots/pallas_call | solution.py:455
  49.3 3.0 %collective-permute-done.8.west_ref = f32[8,128]{1,0:T(8,128)S(1)} collective-permute-done((f32[8,128]{1,0:T(8,128)S(1)}, f32[8,128]{1,0:T(8,128)S(1)}, u32[]{:S(2)}, u32[]{:S(2)}) %collective-permute-start.8) | collective-permute-done | bytes 4128 | tf_op jit(solution)/shard_map/ppermute | solution.py:334
  52.3 0.0 collective-permute-done.9.east_ref
  52.3 0.1 all-to-all-done
  52.4 1.6 %cloud_slots.1 = (f32[1920,256]{1,0:T(8,128)}, f32[5,128,12]{2,1,0:T(8,128)}) custom-call(f32[3072,128]{1,0:T(8,128)S(1)} %bitcast.19, f32[5,128,12]{2,1,0:T(8,128)S(1)} %get-tuple-element.26.part_ref, f32[8,128]{1,0:T(8,128)S(1)} %collective-permute-done.8.west_ref, f32[8,128]{1,0:T(8,128)S(1)} %collective-permute-done.9.east_ref, ...), custom_call_target="tpu_custom_call", output_to_operand_aliasing={{0}: (6, {})} | custom-call | tf_op jit(solution)/shard_map/cloud_slots/pallas_call | solution.py:469
  (15 shorter events, 0.2 us)
Async XLA Ops:
  5.5 6.9 %copy-start.3 = (f32[16,128]{1,0:T(8,128)S(1)}, f32[16,128]{1,0:T(8,128)}, u32[]{:S(2)}) copy-start(f32[16,128]{1,0:T(8,128)} %get-tuple-element.19) | copy-start | bytes 24580
  5.5 8.4 %copy-start.2 = (f32[16,128]{1,0:T(8,128)S(1)}, f32[16,128]{1,0:T(8,128)}, u32[]{:S(2)}) copy-start(f32[16,128]{1,0:T(8,128)} %get-tuple-element.20) | copy-start | bytes 24580
  5.5 8.5 %copy-start = (f32[16,24,128]{2,1,0:T(8,128)S(1)}, f32[16,24,128]{2,1,0:T(8,128)}, u32[]{:S(2)}) copy-start(f32[16,24,128]{2,1,0:T(8,128)} %get-tuple-element.22) | copy-start | bytes 589828
  5.5 8.5 %collective-permute-start.2 = (f32[16,24,128]{2,1,0:T(8,128)}, f32[16,24,128]{2,1,0:T(8,128)S(1)}, u32[]{:S(2)}, u32[]{:S(2)}) collective-permute-start(f32[16,24,128]{2,1,0:T(8,128)} %get-tuple-element.23), channel_id=1, source_target_pairs={{0,16},{1,17},{2,18},{3,19},{4,20},{5,21},{6,22},{7,23},{8,24},{9,... | collective-permute-start | bytes 589832 | tf_op jit(solution)/shard_map/ppermute | solution.py:339
  5.6 46.7 %all-to-all-start = ((f32[32,96,128]{2,1,0:T(8,128)}), f32[32,96,128]{2,1,0:T(8,128)S(1)}, u32[]{:S(2)}, u32[]{:S(2)}) async-start(f32[32,96,128]{2,1,0:T(8,128)} %get-tuple-element.17), calls=%async_computation | async-start | bytes 3145728 | tf_op jit(solution)/shard_map/all_to_all | solution.py:434
  12.4 28.6 %collective-permute-start = (f32[16,128]{1,0:T(8,128)S(1)}, f32[16,128]{1,0:T(8,128)S(1)}, u32[]{:S(2)}, u32[]{:S(2)}) collective-permute-start(f32[16,128]{1,0:T(8,128)S(1)} %copy-done.3), channel_id=1, source_target_pairs={{0,1},{1,2},{2,3},{3,0},{4,5},{5,6},{6,7},{7,4},{8,9},{9,10},{10,1... | collective-permute-start | bytes 24584 | tf_op jit(solution)/shard_map/ppermute | solution.py:334
  13.9 27.1 %collective-permute-start.1 = (f32[16,128]{1,0:T(8,128)S(1)}, f32[16,128]{1,0:T(8,128)S(1)}, u32[]{:S(2)}, u32[]{:S(2)}) collective-permute-start(f32[16,128]{1,0:T(8,128)S(1)} %copy-done.2), channel_id=1, source_target_pairs={{0,3},{1,0},{2,1},{3,2},{4,7},{5,4},{6,5},{7,6},{8,11},{9,8},{10,9... | collective-permute-start | bytes 24584 | tf_op jit(solution)/shard_map/ppermute | solution.py:334
  14.1 26.9 %copy-start.1 = (f32[128,128]{1,0:T(8,128)S(1)}, f32[128,128]{1,0:T(8,128)}, u32[]{:S(2)}) copy-start(f32[128,128]{1,0:T(8,128)} %get-tuple-element.18.nodes_ref) | copy-start | bytes 196612
  14.1 3.9 %collective-permute-start.3 = (f32[2,8,24,128]{3,2,0,1:T(8,128)S(1)}, f32[2,8,24,128]{3,2,0,1:T(8,128)S(1)}, u32[]{:S(2)}, u32[]{:S(2)}) collective-permute-start(f32[2,8,24,128]{3,2,0,1:T(8,128)S(1)} %copy.9), channel_id=1, source_target_pairs={{0,1},{1,0},{2,3},{3,2},{4,5},{5,4},{6,7},{7,6},{8,9},{9,8},{10,11... | collective-permute-start | bytes 589832 | tf_op jit(solution)/shard_map/ppermute | solution.py:339
  18.0 9.5 %collective-permute-start.4 = (f32[4,2,24,128]{3,2,0,1:T(8,128)S(1)}, f32[4,2,24,128]{3,2,0,1:T(8,128)S(1)}, u32[]{:S(2)}, u32[]{:S(2)}) collective-permute-start(f32[4,2,24,128]{3,2,0,1:T(8,128)S(1)} %pad_maximum_fusion.2), channel_id=1, source_target_pairs={{0,4},{1,5},{2,6},{3,7},{4,0},{5,1},{6,2},{7,3},{8,12},{9,13},{10,... | collective-permute-start | bytes 294920 | tf_op jit(solution)/shard_map/ppermute | solution.py:339
  23.1 4.9 %collective-permute-start.5 = (f32[4,2,24,128]{3,2,0,1:T(8,128)S(1)}, f32[4,2,24,128]{3,2,0,1:T(8,128)S(1)}, u32[]{:S(2)}, u32[]{:S(2)}) collective-permute-start(f32[4,2,24,128]{3,2,0,1:T(8,128)S(1)} %pad_maximum_fusion.3), channel_id=1, source_target_pairs={{0,2},{1,3},{2,0},{3,1},{4,6},{5,7},{6,4},{7,5},{8,10},{9,11},{10,... | collective-permute-start | bytes 294920 | tf_op jit(solution)/shard_map/ppermute | solution.py:339
  23.2 8.2 %collective-permute-start.6 = (f32[4,2,24,128]{3,2,0,1:T(8,128)S(1)}, f32[4,2,24,128]{3,2,0,1:T(8,128)S(1)}, u32[]{:S(2)}, u32[]{:S(2)}) collective-permute-start(f32[4,2,24,128]{3,2,0,1:T(8,128)S(1)} %pad_maximum_fusion.4), channel_id=1, source_target_pairs={{0,6},{1,7},{2,4},{3,5},{4,2},{5,3},{6,0},{7,1},{8,14},{9,15},{10,... | collective-permute-start | bytes 294920 | tf_op jit(solution)/shard_map/ppermute | solution.py:339
  31.4 16.9 %collective-permute-start.7 = (f32[16,1,24,128]{3,2,0,1:T(8,128)S(1)}, f32[16,1,24,128]{3,2,0,1:T(8,128)S(1)}, u32[]{:S(2)}, u32[]{:S(2)}) collective-permute-start(f32[16,1,24,128]{3,2,0,1:T(8,128)S(1)} %pad_maximum_fusion.1), channel_id=1, source_target_pairs={{0,8},{1,9},{2,10},{3,11},{4,12},{5,13},{6,14},{7,15},{8,0},{9,1},... | collective-permute-start | bytes 589832 | tf_op jit(solution)/shard_map/ppermute | solution.py:339
  41.4 10.9 %collective-permute-start.8 = (f32[8,128]{1,0:T(8,128)S(1)}, f32[8,128]{1,0:T(8,128)S(1)}, u32[]{:S(2)}, u32[]{:S(2)}) collective-permute-start(f32[8,128]{1,0:T(8,128)S(1)} %get-tuple-element.27.high_ref), channel_id=1, source_target_pairs={{0,4},{4,8},{8,12},{12,16},{16,20},{20,24},{24,28},{28,0},{1,5},{5... | collective-permute-start | bytes 12296 | tf_op jit(solution)/shard_map/ppermute | solution.py:334
  42.4 9.9 %collective-permute-start.9 = (f32[8,128]{1,0:T(8,128)S(1)}, f32[8,128]{1,0:T(8,128)S(1)}, u32[]{:S(2)}, u32[]{:S(2)}) collective-permute-start(f32[8,128]{1,0:T(8,128)S(1)} %get-tuple-element.28.low_ref), channel_id=1, source_target_pairs={{0,28},{4,0},{8,4},{12,8},{16,12},{20,16},{24,20},{28,24},{1,29},{... | collective-permute-start | bytes 12296 | tf_op jit(solution)/shard_map/ppermute | solution.py:334

commit v8 on v7

--- a/solution.py
+++ b/solution.py
@@ -283,15 +283,17 @@
     gcm_copy = fetch(gcm_ref, gcm_hbm, gcm_sem)
     pitch = recv_ref.shape[0] // devices
 
-    rows_ref = recv_ref
-    if pitch % 16 == 0:
-        rows_ref = spread_ref
+    slots = devices * capacity
+
+    def rows(first):
+        if pitch % 16:
+            ranked = [recv_ref[pl.ds(first + r, devices, stride=pitch), :] for r in range(capacity)]
+            return jnp.concatenate(ranked, axis=0)
+        base = first // capacity * slots
         for source in range(devices):
-            spread_ref[pl.ds(source * (pitch + 8), pitch), :] = recv_ref[pl.ds(source * pitch, pitch), :]
-        pitch = pitch + 8
-
-    def rows(first):
-        ranked = [rows_ref[pl.ds(first + r, devices, stride=pitch), :] for r in range(capacity)]
+            tile = recv_ref[pl.ds(source * pitch + first, capacity), :]
+            spread_ref[pl.ds(base + source * capacity, capacity), :] = tile
+        ranked = [spread_ref[pl.ds(base + r, devices, stride=capacity), :] for r in range(capacity)]
         return jnp.concatenate(ranked, axis=0)
 
     blocks = groups * field_count - early

time: 54.6 us -> 54.6 us (level)
  no operation moved by 1% of the time
where the time goes in v8:
time: 54.6 us; the launch traced here: 53.9 us
  starting transfers between devices  29.6 us (54%)
  waiting for transfers between devices  15.7 us (29%)
  Pallas kernels  7.74 us (14%)
  between operations  0.78 us (1%)
    ppermute x6, starting transfers between devices, exchange(): return lax.ppermute(block, AXES, [(i, i ^ bits) for i in range(count)])  18.8 us
    ppermute x6, waiting for transfers between devices, exchange(): return lax.ppermute(block, AXES, [(i, i ^ bits) for i in range(count)])  12.6 us
    all_to_all x1, starting transfers between devices, body(): lax.all_to_all(send, AXES, split_axis=0, concat_axis=0, tiled=True)  6.8 us
    pallas_call x1, Pallas kernels, body(): pl.pallas_call(functools.partial(kernel_a, devices, capacity, early, *siz...  4.86 us
    ppermute x4, starting transfers between devices, shift(): lax.ppermute(face, axis, [(i, (i + by) % count) for i in range(count)])  3.91 us
    ppermute x4, waiting for transfers between devices, shift(): lax.ppermute(face, axis, [(i, (i + by) % count) for i in range(count)])  3.01 us
    pallas_call x1, Pallas kernels, body(): pl.pallas_call(functools.partial(kernel_out, devices, capacity, groups, f...  1.58 us
  transfers between devices with their start and end apart: 11, of which 8 were waited for; matrix products, arithmetic and copies ran while one was open for 0% of the time, Pallas kernels for 2%

profile of v8, /device:TPU:17, one launch (start us, length us, event | category | flops | bytes accessed | tf_op | source)
XLA Modules:
  0.0 53.9 jit_solution(12141380600811820283)
XLA Ops:
  0.6 4.9 %cloud_models.1 = (f32[32,96,128]{2,1,0:T(8,128)}, f32[16,24,128]{2,1,0:T(8,128)}, f32[16,24,128]{2,1,0:T(8,128)}, f32[128,128]{1,0:T(8,128)}, f32[16,128]{1,0:T(8,128)}, /*index=5*/f32[16,128]{1,0:T(8,128)}) custom-call(s32[1]{0:T(128)} %bitcast.refs_0_.me_ref, f32[5,12,32,128]{3,2,1,0:T(8,128)} %refs_1_.1, f32[5,128,12]{2,1,0:T(8,128)} %bitcast.24, ...), custom_call_target="tpu_custom_call" | custom-call | tf_op jit(solution)/shard_map/cloud_models/pallas_call | solution.py:404
  5.5 0.0 copy-start.3
  5.5 0.0 copy-start
  5.5 0.1 collective-permute-start.2
  5.6 6.8 %all-to-all-start = ((f32[32,96,128]{2,1,0:T(8,128)}), f32[32,96,128]{2,1,0:T(8,128)S(1)}, u32[]{:S(2)}, u32[]{:S(2)}) async-start(f32[32,96,128]{2,1,0:T(8,128)} %get-tuple-element.17), calls=%async_computation | async-start | bytes 3145728 | tf_op jit(solution)/shard_map/all_to_all | solution.py:436
  12.4 0.0 copy-done.3
  12.4 1.5 %collective-permute-start = (f32[16,128]{1,0:T(8,128)S(1)}, f32[16,128]{1,0:T(8,128)S(1)}, u32[]{:S(2)}, u32[]{:S(2)}) collective-permute-start(f32[16,128]{1,0:T(8,128)S(1)} %copy-done.3), channel_id=1, source_target_pairs={{0,1},{1,2},{2,3},{3,0},{4,5},{5,6},{6,7},{7,4},{8,9},{9,10},{10,1... | collective-permute-start | bytes 24584 | tf_op jit(solution)/shard_map/ppermute | solution.py:336
  13.9 0.0 copy-done.2
  13.9 0.0 collective-permute-start.1
  13.9 0.1 collective-permute-done.2
  14.1 0.0 copy-start.1
  14.1 2.8 %collective-permute-start.3 = (f32[2,8,24,128]{3,2,0,1:T(8,128)S(1)}, f32[2,8,24,128]{3,2,0,1:T(8,128)S(1)}, u32[]{:S(2)}, u32[]{:S(2)}) collective-permute-start(f32[2,8,24,128]{3,2,0,1:T(8,128)S(1)} %copy.9), channel_id=1, source_target_pairs={{0,1},{1,0},{2,3},{3,2},{4,5},{5,4},{6,7},{7,6},{8,9},{9,8},{10,11... | collective-permute-start | bytes 589832 | tf_op jit(solution)/shard_map/ppermute | solution.py:341
  16.9 1.1 %collective-permute-done.3 = f32[2,8,24,128]{3,2,0,1:T(8,128)S(1)} collective-permute-done((f32[2,8,24,128]{3,2,0,1:T(8,128)S(1)}, f32[2,8,24,128]{3,2,0,1:T(8,128)S(1)}, u32[]{:S(2)}, u32[]{:S(2)}) %collective-permute-start.3) | collective-permute-done | bytes 196640 | tf_op jit(solution)/shard_map/ppermute | solution.py:341
  18.0 5.1 %collective-permute-start.4 = (f32[4,2,24,128]{3,2,0,1:T(8,128)S(1)}, f32[4,2,24,128]{3,2,0,1:T(8,128)S(1)}, u32[]{:S(2)}, u32[]{:S(2)}) collective-permute-start(f32[4,2,24,128]{3,2,0,1:T(8,128)S(1)} %pad_maximum_fusion.2), channel_id=1, source_target_pairs={{0,4},{1,5},{2,6},{3,7},{4,0},{5,1},{6,2},{7,3},{8,12},{9,13},{10,... | collective-permute-start | bytes 294920 | tf_op jit(solution)/shard_map/ppermute | solution.py:341
  23.1 0.1 collective-permute-start.5
  23.2 1.2 %collective-permute-start.6 = (f32[4,2,24,128]{3,2,0,1:T(8,128)S(1)}, f32[4,2,24,128]{3,2,0,1:T(8,128)S(1)}, u32[]{:S(2)}, u32[]{:S(2)}) collective-permute-start(f32[4,2,24,128]{3,2,0,1:T(8,128)S(1)} %pad_maximum_fusion.4), channel_id=1, source_target_pairs={{0,6},{1,7},{2,4},{3,5},{4,2},{5,3},{6,0},{7,1},{8,14},{9,15},{10,... | collective-permute-start | bytes 294920 | tf_op jit(solution)/shard_map/ppermute | solution.py:341
  24.4 3.1 %collective-permute-done.4 = f32[4,2,24,128]{3,2,0,1:T(8,128)S(1)} collective-permute-done((f32[4,2,24,128]{3,2,0,1:T(8,128)S(1)}, f32[4,2,24,128]{3,2,0,1:T(8,128)S(1)}, u32[]{:S(2)}, u32[]{:S(2)}) %collective-permute-start.4) | collective-permute-done | bytes 98336 | tf_op jit(solution)/shard_map/ppermute | solution.py:341
  27.5 0.4 collective-permute-done.5
  28.0 3.4 %collective-permute-done.6 = f32[4,2,24,128]{3,2,0,1:T(8,128)S(1)} collective-permute-done((f32[4,2,24,128]{3,2,0,1:T(8,128)S(1)}, f32[4,2,24,128]{3,2,0,1:T(8,128)S(1)}, u32[]{:S(2)}, u32[]{:S(2)}) %collective-permute-start.6) | collective-permute-done | bytes 98336 | tf_op jit(solution)/shard_map/ppermute | solution.py:341
  31.4 9.6 %collective-permute-start.7 = (f32[16,1,24,128]{3,2,0,1:T(8,128)S(1)}, f32[16,1,24,128]{3,2,0,1:T(8,128)S(1)}, u32[]{:S(2)}, u32[]{:S(2)}) collective-permute-start(f32[16,1,24,128]{3,2,0,1:T(8,128)S(1)} %pad_maximum_fusion.1), channel_id=1, source_target_pairs={{0,8},{1,9},{2,10},{3,11},{4,12},{5,13},{6,14},{7,15},{8,0},{9,1},... | collective-permute-start | bytes 589832 | tf_op jit(solution)/shard_map/ppermute | solution.py:341
  41.0 0.0 collective-permute-done.south_ref
  41.0 0.0 collective-permute-done.1.north_ref
  41.0 0.0 copy-done.1
  41.0 0.3 edge_sum_second.1
  41.4 1.0 %collective-permute-start.8 = (f32[8,128]{1,0:T(8,128)S(1)}, f32[8,128]{1,0:T(8,128)S(1)}, u32[]{:S(2)}, u32[]{:S(2)}) collective-permute-start(f32[8,128]{1,0:T(8,128)S(1)} %get-tuple-element.27.high_ref), channel_id=1, source_target_pairs={{0,4},{4,8},{8,12},{12,16},{16,20},{20,24},{24,28},{28,0},{1,5},{5... | collective-permute-start | bytes 12296 | tf_op jit(solution)/shard_map/ppermute | solution.py:336
  42.4 1.4 %collective-permute-start.9 = (f32[8,128]{1,0:T(8,128)S(1)}, f32[8,128]{1,0:T(8,128)S(1)}, u32[]{:S(2)}, u32[]{:S(2)}) collective-permute-start(f32[8,128]{1,0:T(8,128)S(1)} %get-tuple-element.28.low_ref), channel_id=1, source_target_pairs={{0,28},{4,0},{8,4},{12,8},{16,12},{20,16},{24,20},{28,24},{1,29},{... | collective-permute-start | bytes 12296 | tf_op jit(solution)/shard_map/ppermute | solution.py:336
  43.8 4.5 %collective-permute-done.7 = f32[16,1,24,128]{3,2,0,1:T(8,128)S(1)} collective-permute-done((f32[16,1,24,128]{3,2,0,1:T(8,128)S(1)}, f32[16,1,24,128]{3,2,0,1:T(8,128)S(1)}, u32[]{:S(2)}, u32[]{:S(2)}) %collective-permute-start.7) | collective-permute-done | bytes 196640 | tf_op jit(solution)/shard_map/ppermute | solution.py:341
  48.3 0.9 %early_slots.1.refs_0_ = f32[1920,256]{1,0:T(8,128)} custom-call(s32[1]{0:T(128)} %bitcast.refs_0_.me_ref, f32[16,24,128]{2,1,0:T(8,128)S(1)} %fusion.3.refs_0_, f32[16,24,128]{2,1,0:T(8,128)S(1)} %bitcast.20), custom_call_target="tpu_custom_call" | custom-call | flops 12999999488 | bytes 1000000 | tf_op jit(solution)/shard_map/early_slots/pallas_call | solution.py:457
  49.3 3.0 %collective-permute-done.8.west_ref = f32[8,128]{1,0:T(8,128)S(1)} collective-permute-done((f32[8,128]{1,0:T(8,128)S(1)}, f32[8,128]{1,0:T(8,128)S(1)}, u32[]{:S(2)}, u32[]{:S(2)}) %collective-permute-start.8) | collective-permute-done | bytes 4128 | tf_op jit(solution)/shard_map/ppermute | solution.py:336
  52.3 0.0 collective-permute-done.9.east_ref
  52.3 0.1 all-to-all-done
  52.4 1.6 %cloud_slots.1 = (f32[1920,256]{1,0:T(8,128)}, f32[5,128,12]{2,1,0:T(8,128)}) custom-call(f32[3072,128]{1,0:T(8,128)S(1)} %bitcast.19, f32[5,128,12]{2,1,0:T(8,128)S(1)} %get-tuple-element.26.part_ref, f32[8,128]{1,0:T(8,128)S(1)} %collective-permute-done.8.west_ref, f32[8,128]{1,0:T(8,128)S(1)} %collective-permute-done.9.east_ref, ...), custom_call_target="tpu_custom_call", output_to_operand_aliasing={{0}: (6, {})} | custom-call | tf_op jit(solution)/shard_map/cloud_slots/pallas_call | solution.py:471
  (15 shorter events, 0.2 us)
Async XLA Ops:
  5.5 6.9 %copy-start.3 = (f32[16,128]{1,0:T(8,128)S(1)}, f32[16,128]{1,0:T(8,128)}, u32[]{:S(2)}) copy-start(f32[16,128]{1,0:T(8,128)} %get-tuple-element.19) | copy-start | bytes 24580
  5.5 8.4 %copy-start.2 = (f32[16,128]{1,0:T(8,128)S(1)}, f32[16,128]{1,0:T(8,128)}, u32[]{:S(2)}) copy-start(f32[16,128]{1,0:T(8,128)} %get-tuple-element.20) | copy-start | bytes 24580
  5.5 8.5 %copy-start = (f32[16,24,128]{2,1,0:T(8,128)S(1)}, f32[16,24,128]{2,1,0:T(8,128)}, u32[]{:S(2)}) copy-start(f32[16,24,128]{2,1,0:T(8,128)} %get-tuple-element.22) | copy-start | bytes 589828
  5.5 8.5 %collective-permute-start.2 = (f32[16,24,128]{2,1,0:T(8,128)}, f32[16,24,128]{2,1,0:T(8,128)S(1)}, u32[]{:S(2)}, u32[]{:S(2)}) collective-permute-start(f32[16,24,128]{2,1,0:T(8,128)} %get-tuple-element.23), channel_id=1, source_target_pairs={{0,16},{1,17},{2,18},{3,19},{4,20},{5,21},{6,22},{7,23},{8,24},{9,... | collective-permute-start | bytes 589832 | tf_op jit(solution)/shard_map/ppermute | solution.py:341
  5.6 46.7 %all-to-all-start = ((f32[32,96,128]{2,1,0:T(8,128)}), f32[32,96,128]{2,1,0:T(8,128)S(1)}, u32[]{:S(2)}, u32[]{:S(2)}) async-start(f32[32,96,128]{2,1,0:T(8,128)} %get-tuple-element.17), calls=%async_computation | async-start | bytes 3145728 | tf_op jit(solution)/shard_map/all_to_all | solution.py:436
  12.4 28.6 %collective-permute-start = (f32[16,128]{1,0:T(8,128)S(1)}, f32[16,128]{1,0:T(8,128)S(1)}, u32[]{:S(2)}, u32[]{:S(2)}) collective-permute-start(f32[16,128]{1,0:T(8,128)S(1)} %copy-done.3), channel_id=1, source_target_pairs={{0,1},{1,2},{2,3},{3,0},{4,5},{5,6},{6,7},{7,4},{8,9},{9,10},{10,1... | collective-permute-start | bytes 24584 | tf_op jit(solution)/shard_map/ppermute | solution.py:336
  13.9 27.1 %collective-permute-start.1 = (f32[16,128]{1,0:T(8,128)S(1)}, f32[16,128]{1,0:T(8,128)S(1)}, u32[]{:S(2)}, u32[]{:S(2)}) collective-permute-start(f32[16,128]{1,0:T(8,128)S(1)} %copy-done.2), channel_id=1, source_target_pairs={{0,3},{1,0},{2,1},{3,2},{4,7},{5,4},{6,5},{7,6},{8,11},{9,8},{10,9... | collective-permute-start | bytes 24584 | tf_op jit(solution)/shard_map/ppermute | solution.py:336
  14.1 26.9 %copy-start.1 = (f32[128,128]{1,0:T(8,128)S(1)}, f32[128,128]{1,0:T(8,128)}, u32[]{:S(2)}) copy-start(f32[128,128]{1,0:T(8,128)} %get-tuple-element.18.nodes_ref) | copy-start | bytes 196612
  14.1 3.9 %collective-permute-start.3 = (f32[2,8,24,128]{3,2,0,1:T(8,128)S(1)}, f32[2,8,24,128]{3,2,0,1:T(8,128)S(1)}, u32[]{:S(2)}, u32[]{:S(2)}) collective-permute-start(f32[2,8,24,128]{3,2,0,1:T(8,128)S(1)} %copy.9), channel_id=1, source_target_pairs={{0,1},{1,0},{2,3},{3,2},{4,5},{5,4},{6,7},{7,6},{8,9},{9,8},{10,11... | collective-permute-start | bytes 589832 | tf_op jit(solution)/shard_map/ppermute | solution.py:341
  18.0 9.5 %collective-permute-start.4 = (f32[4,2,24,128]{3,2,0,1:T(8,128)S(1)}, f32[4,2,24,128]{3,2,0,1:T(8,128)S(1)}, u32[]{:S(2)}, u32[]{:S(2)}) collective-permute-start(f32[4,2,24,128]{3,2,0,1:T(8,128)S(1)} %pad_maximum_fusion.2), channel_id=1, source_target_pairs={{0,4},{1,5},{2,6},{3,7},{4,0},{5,1},{6,2},{7,3},{8,12},{9,13},{10,... | collective-permute-start | bytes 294920 | tf_op jit(solution)/shard_map/ppermute | solution.py:341
  23.1 4.9 %collective-permute-start.5 = (f32[4,2,24,128]{3,2,0,1:T(8,128)S(1)}, f32[4,2,24,128]{3,2,0,1:T(8,128)S(1)}, u32[]{:S(2)}, u32[]{:S(2)}) collective-permute-start(f32[4,2,24,128]{3,2,0,1:T(8,128)S(1)} %pad_maximum_fusion.3), channel_id=1, source_target_pairs={{0,2},{1,3},{2,0},{3,1},{4,6},{5,7},{6,4},{7,5},{8,10},{9,11},{10,... | collective-permute-start | bytes 294920 | tf_op jit(solution)/shard_map/ppermute | solution.py:341
  23.2 8.2 %collective-permute-start.6 = (f32[4,2,24,128]{3,2,0,1:T(8,128)S(1)}, f32[4,2,24,128]{3,2,0,1:T(8,128)S(1)}, u32[]{:S(2)}, u32[]{:S(2)}) collective-permute-start(f32[4,2,24,128]{3,2,0,1:T(8,128)S(1)} %pad_maximum_fusion.4), channel_id=1, source_target_pairs={{0,6},{1,7},{2,4},{3,5},{4,2},{5,3},{6,0},{7,1},{8,14},{9,15},{10,... | collective-permute-start | bytes 294920 | tf_op jit(solution)/shard_map/ppermute | solution.py:341
  31.4 16.9 %collective-permute-start.7 = (f32[16,1,24,128]{3,2,0,1:T(8,128)S(1)}, f32[16,1,24,128]{3,2,0,1:T(8,128)S(1)}, u32[]{:S(2)}, u32[]{:S(2)}) collective-permute-start(f32[16,1,24,128]{3,2,0,1:T(8,128)S(1)} %pad_maximum_fusion.1), channel_id=1, source_target_pairs={{0,8},{1,9},{2,10},{3,11},{4,12},{5,13},{6,14},{7,15},{8,0},{9,1},... | collective-permute-start | bytes 589832 | tf_op jit(solution)/shard_map/ppermute | solution.py:341
  41.4 10.9 %collective-permute-start.8 = (f32[8,128]{1,0:T(8,128)S(1)}, f32[8,128]{1,0:T(8,128)S(1)}, u32[]{:S(2)}, u32[]{:S(2)}) collective-permute-start(f32[8,128]{1,0:T(8,128)S(1)} %get-tuple-element.27.high_ref), channel_id=1, source_target_pairs={{0,4},{4,8},{8,12},{12,16},{16,20},{20,24},{24,28},{28,0},{1,5},{5... | collective-permute-start | bytes 12296 | tf_op jit(solution)/shard_map/ppermute | solution.py:336
  42.4 9.9 %collective-permute-start.9 = (f32[8,128]{1,0:T(8,128)S(1)}, f32[8,128]{1,0:T(8,128)S(1)}, u32[]{:S(2)}, u32[]{:S(2)}) collective-permute-start(f32[8,128]{1,0:T(8,128)S(1)} %get-tuple-element.28.low_ref), channel_id=1, source_target_pairs={{0,28},{4,0},{8,4},{12,8},{16,12},{20,16},{24,20},{28,24},{1,29},{... | collective-permute-start | bytes 12296 | tf_op jit(solution)/shard_map/ppermute | solution.py:336

commit v9 on v6

--- a/solution.py
+++ b/solution.py
@@ -90,9 +90,9 @@
     return lax.dot_general(picks, parts, NT, preferred_element_type=jnp.float32)
 
 
-def fetch(source, target, sem):
+def fetch(source, target, sem, priority=0):
     copy = pltpu.make_async_copy(source, target, sem)
-    copy.start()
+    copy.start(priority=priority)
     return copy
 
 
@@ -107,7 +107,7 @@
         fetch(cost_hbm, cost_ref, small_sem.at[2]),
     ]
     pieces = [
-        fetch(crm_hbm.at[:, pl.ds(z, group)], crm_ref.at[:, pl.ds(z, group)], crm_sem.at[z // group])
+        fetch(crm_hbm.at[:, pl.ds(z, group)], crm_ref.at[:, pl.ds(z, group)], crm_sem.at[z // group], 1)
         for z in range(0, levels, group)
     ]
     small.append(fetch(mass_hbm, mass_ref, small_sem.at[3]))

time: 54.6 us -> 54.6 us (level)
  no operation moved by 1% of the time
where the time goes in v9:
time: 54.6 us; the launch traced here: 53.9 us
  starting transfers between devices  29.7 us (54%)
  waiting for transfers between devices  15.6 us (29%)
  Pallas kernels  7.74 us (14%)
  between operations  0.78 us (1%)
    ppermute x6, starting transfers between devices, exchange(): return lax.ppermute(block, AXES, [(i, i ^ bits) for i in range(count)])  18.8 us
    ppermute x6, waiting for transfers between devices, exchange(): return lax.ppermute(block, AXES, [(i, i ^ bits) for i in range(count)])  9.64 us
    all_to_all x1, starting transfers between devices, body(): lax.all_to_all(send, AXES, split_axis=0, concat_axis=0, tiled=True)  6.8 us
    ppermute x4, waiting for transfers between devices, shift(): lax.ppermute(face, axis, [(i, (i + by) % count) for i in range(count)])  5.83 us
    pallas_call x1, Pallas kernels, body(): pl.pallas_call(functools.partial(kernel_a, devices, capacity, early, *siz...  4.86 us
    ppermute x4, starting transfers between devices, shift(): lax.ppermute(face, axis, [(i, (i + by) % count) for i in range(count)])  4.07 us
    pallas_call x1, Pallas kernels, body(): pl.pallas_call(functools.partial(kernel_out, devices, capacity, groups, f...  1.58 us
  transfers between devices with their start and end apart: 11, of which 9 were waited for; matrix products, arithmetic and copies ran while one was open for 0% of the time, Pallas kernels for 2%

profile of v9, /device:TPU:17, one launch (start us, length us, event | category | flops | bytes accessed | tf_op | source)
XLA Modules:
  0.0 53.9 jit_solution(13661812092430625770)
XLA Ops:
  0.6 4.9 %cloud_models.1 = (f32[32,96,128]{2,1,0:T(8,128)}, f32[16,24,128]{2,1,0:T(8,128)}, f32[16,24,128]{2,1,0:T(8,128)}, f32[128,128]{1,0:T(8,128)}, f32[16,128]{1,0:T(8,128)}, /*index=5*/f32[16,128]{1,0:T(8,128)}) custom-call(s32[1]{0:T(128)} %bitcast.refs_0_.me_ref, f32[5,12,32,128]{3,2,1,0:T(8,128)} %refs_1_.1, f32[5,128,12]{2,1,0:T(8,128)} %bitcast.24, ...), custom_call_target="tpu_custom_call" | custom-call | tf_op jit(solution)/shard_map/cloud_models/pallas_call | solution.py:402
  5.5 0.0 copy-start.1
  5.5 0.1 collective-permute-start.2
  5.6 6.8 %all-to-all-start = ((f32[32,96,128]{2,1,0:T(8,128)}), f32[32,96,128]{2,1,0:T(8,128)S(1)}, u32[]{:S(2)}, u32[]{:S(2)}) async-start(f32[32,96,128]{2,1,0:T(8,128)} %get-tuple-element.17), calls=%async_computation | async-start | bytes 3145728 | tf_op jit(solution)/shard_map/all_to_all | solution.py:434
  12.4 1.6 %collective-permute-done.2 = f32[16,24,128]{2,1,0:T(8,128)S(1)} collective-permute-done((f32[16,24,128]{2,1,0:T(8,128)}, f32[16,24,128]{2,1,0:T(8,128)S(1)}, u32[]{:S(2)}, u32[]{:S(2)}) %collective-permute-start.2) | collective-permute-done | bytes 196640 | tf_op jit(solution)/shard_map/ppermute | solution.py:339
  14.0 0.0 copy-done.1
  14.1 0.0 copy-start.3
  14.1 0.0 copy-start.2
  14.1 0.0 copy-start
  14.1 2.8 %collective-permute-start.3 = (f32[2,8,24,128]{3,2,0,1:T(8,128)S(1)}, f32[2,8,24,128]{3,2,0,1:T(8,128)S(1)}, u32[]{:S(2)}, u32[]{:S(2)}) collective-permute-start(f32[2,8,24,128]{3,2,0,1:T(8,128)S(1)} %copy.9), channel_id=1, source_target_pairs={{0,1},{1,0},{2,3},{3,2},{4,5},{5,4},{6,7},{7,6},{8,9},{9,8},{10,11... | collective-permute-start | bytes 589832 | tf_op jit(solution)/shard_map/ppermute | solution.py:339
  16.9 1.1 %collective-permute-done.3 = f32[2,8,24,128]{3,2,0,1:T(8,128)S(1)} collective-permute-done((f32[2,8,24,128]{3,2,0,1:T(8,128)S(1)}, f32[2,8,24,128]{3,2,0,1:T(8,128)S(1)}, u32[]{:S(2)}, u32[]{:S(2)}) %collective-permute-start.3) | collective-permute-done | bytes 196640 | tf_op jit(solution)/shard_map/ppermute | solution.py:339
  18.0 5.1 %collective-permute-start.4 = (f32[4,2,24,128]{3,2,0,1:T(8,128)S(1)}, f32[4,2,24,128]{3,2,0,1:T(8,128)S(1)}, u32[]{:S(2)}, u32[]{:S(2)}) collective-permute-start(f32[4,2,24,128]{3,2,0,1:T(8,128)S(1)} %pad_maximum_fusion.2), channel_id=1, source_target_pairs={{0,4},{1,5},{2,6},{3,7},{4,0},{5,1},{6,2},{7,3},{8,12},{9,13},{10,... | collective-permute-start | bytes 294920 | tf_op jit(solution)/shard_map/ppermute | solution.py:339
  23.1 0.1 collective-permute-start.5
  23.2 1.2 %collective-permute-start.6 = (f32[4,2,24,128]{3,2,0,1:T(8,128)S(1)}, f32[4,2,24,128]{3,2,0,1:T(8,128)S(1)}, u32[]{:S(2)}, u32[]{:S(2)}) collective-permute-start(f32[4,2,24,128]{3,2,0,1:T(8,128)S(1)} %pad_maximum_fusion.4), channel_id=1, source_target_pairs={{0,6},{1,7},{2,4},{3,5},{4,2},{5,3},{6,0},{7,1},{8,14},{9,15},{10,... | collective-permute-start | bytes 294920 | tf_op jit(solution)/shard_map/ppermute | solution.py:339
  24.4 3.1 %collective-permute-done.4 = f32[4,2,24,128]{3,2,0,1:T(8,128)S(1)} collective-permute-done((f32[4,2,24,128]{3,2,0,1:T(8,128)S(1)}, f32[4,2,24,128]{3,2,0,1:T(8,128)S(1)}, u32[]{:S(2)}, u32[]{:S(2)}) %collective-permute-start.4) | collective-permute-done | bytes 98336 | tf_op jit(solution)/shard_map/ppermute | solution.py:339
  27.5 0.4 collective-permute-done.5
  28.0 3.4 %collective-permute-done.6 = f32[4,2,24,128]{3,2,0,1:T(8,128)S(1)} collective-permute-done((f32[4,2,24,128]{3,2,0,1:T(8,128)S(1)}, f32[4,2,24,128]{3,2,0,1:T(8,128)S(1)}, u32[]{:S(2)}, u32[]{:S(2)}) %collective-permute-start.6) | collective-permute-done | bytes 98336 | tf_op jit(solution)/shard_map/ppermute | solution.py:339
  31.4 9.6 %collective-permute-start.7 = (f32[16,1,24,128]{3,2,0,1:T(8,128)S(1)}, f32[16,1,24,128]{3,2,0,1:T(8,128)S(1)}, u32[]{:S(2)}, u32[]{:S(2)}) collective-permute-start(f32[16,1,24,128]{3,2,0,1:T(8,128)S(1)} %pad_maximum_fusion.1), channel_id=1, source_target_pairs={{0,8},{1,9},{2,10},{3,11},{4,12},{5,13},{6,14},{7,15},{8,0},{9,1},... | collective-permute-start | bytes 589832 | tf_op jit(solution)/shard_map/ppermute | solution.py:339
  41.0 1.7 %collective-permute-start = (f32[16,128]{1,0:T(8,128)S(1)}, f32[16,128]{1,0:T(8,128)S(1)}, u32[]{:S(2)}, u32[]{:S(2)}) collective-permute-start(f32[16,128]{1,0:T(8,128)S(1)} %copy-done.3), channel_id=1, source_target_pairs={{0,1},{1,2},{2,3},{3,0},{4,5},{5,6},{6,7},{7,4},{8,9},{9,10},{10,1... | collective-permute-start | bytes 24584 | tf_op jit(solution)/shard_map/ppermute | solution.py:334
  42.7 0.0 copy-done.2
  42.7 0.0 collective-permute-start.1
  42.7 0.8 %collective-permute-done.south_ref = f32[16,128]{1,0:T(8,128)S(1)} collective-permute-done((f32[16,128]{1,0:T(8,128)S(1)}, f32[16,128]{1,0:T(8,128)S(1)}, u32[]{:S(2)}, u32[]{:S(2)}) %collective-permute-start) | collective-permute-done | bytes 8224 | tf_op jit(solution)/shard_map/ppermute | solution.py:334
  43.5 2.8 %collective-permute-done.1.north_ref = f32[16,128]{1,0:T(8,128)S(1)} collective-permute-done((f32[16,128]{1,0:T(8,128)S(1)}, f32[16,128]{1,0:T(8,128)S(1)}, u32[]{:S(2)}, u32[]{:S(2)}) %collective-permute-start.1) | collective-permute-done | bytes 8224 | tf_op jit(solution)/shard_map/ppermute | solution.py:334
  46.3 0.3 edge_sum_second.1
  46.6 0.1 collective-permute-start.8
  46.6 2.4 %collective-permute-start.9 = (f32[8,128]{1,0:T(8,128)S(1)}, f32[8,128]{1,0:T(8,128)S(1)}, u32[]{:S(2)}, u32[]{:S(2)}) collective-permute-start(f32[8,128]{1,0:T(8,128)S(1)} %get-tuple-element.28.low_ref), channel_id=1, source_target_pairs={{0,28},{4,0},{8,4},{12,8},{16,12},{20,16},{24,20},{28,24},{1,29},{... | collective-permute-start | bytes 12296 | tf_op jit(solution)/shard_map/ppermute | solution.py:334
  49.0 0.0 collective-permute-done.7
  49.0 1.0 %early_slots.1.refs_0_ = f32[1920,256]{1,0:T(8,128)} custom-call(s32[1]{0:T(128)} %bitcast.refs_0_.me_ref, f32[16,24,128]{2,1,0:T(8,128)S(1)} %fusion.3.refs_0_, f32[16,24,128]{2,1,0:T(8,128)S(1)} %bitcast.20), custom_call_target="tpu_custom_call" | custom-call | flops 12999999488 | bytes 1000000 | tf_op jit(solution)/shard_map/early_slots/pallas_call | solution.py:455
  50.0 2.3 %collective-permute-done.8.west_ref = f32[8,128]{1,0:T(8,128)S(1)} collective-permute-done((f32[8,128]{1,0:T(8,128)S(1)}, f32[8,128]{1,0:T(8,128)S(1)}, u32[]{:S(2)}, u32[]{:S(2)}) %collective-permute-start.8) | collective-permute-done | bytes 4128 | tf_op jit(solution)/shard_map/ppermute | solution.py:334
  52.2 0.0 collective-permute-done.9.east_ref
  52.2 0.1 all-to-all-done
  52.3 1.6 %cloud_slots.1 = (f32[1920,256]{1,0:T(8,128)}, f32[5,128,12]{2,1,0:T(8,128)}) custom-call(f32[3072,128]{1,0:T(8,128)S(1)} %bitcast.19, f32[5,128,12]{2,1,0:T(8,128)S(1)} %get-tuple-element.26.part_ref, f32[8,128]{1,0:T(8,128)S(1)} %collective-permute-done.8.west_ref, f32[8,128]{1,0:T(8,128)S(1)} %collective-permute-done.9.east_ref, ...), custom_call_target="tpu_custom_call", output_to_operand_aliasing={{0}: (6, {})} | custom-call | tf_op jit(solution)/shard_map/cloud_slots/pallas_call | solution.py:469
  (15 shorter events, 0.2 us)
Async XLA Ops:
  5.5 8.5 %copy-start.1 = (f32[16,24,128]{2,1,0:T(8,128)S(1)}, f32[16,24,128]{2,1,0:T(8,128)}, u32[]{:S(2)}) copy-start(f32[16,24,128]{2,1,0:T(8,128)} %get-tuple-element.22) | copy-start | bytes 589828
  5.5 8.5 %collective-permute-start.2 = (f32[16,24,128]{2,1,0:T(8,128)}, f32[16,24,128]{2,1,0:T(8,128)S(1)}, u32[]{:S(2)}, u32[]{:S(2)}) collective-permute-start(f32[16,24,128]{2,1,0:T(8,128)} %get-tuple-element.23), channel_id=1, source_target_pairs={{0,16},{1,17},{2,18},{3,19},{4,20},{5,21},{6,22},{7,23},{8,24},{9,... | collective-permute-start | bytes 589832 | tf_op jit(solution)/shard_map/ppermute | solution.py:339
  5.6 46.7 %all-to-all-start = ((f32[32,96,128]{2,1,0:T(8,128)}), f32[32,96,128]{2,1,0:T(8,128)S(1)}, u32[]{:S(2)}, u32[]{:S(2)}) async-start(f32[32,96,128]{2,1,0:T(8,128)} %get-tuple-element.17), calls=%async_computation | async-start | bytes 3145728 | tf_op jit(solution)/shard_map/all_to_all | solution.py:434
  14.1 26.9 %copy-start.3 = (f32[16,128]{1,0:T(8,128)S(1)}, f32[16,128]{1,0:T(8,128)}, u32[]{:S(2)}) copy-start(f32[16,128]{1,0:T(8,128)} %get-tuple-element.19) | copy-start | bytes 24580
  14.1 28.6 %copy-start.2 = (f32[16,128]{1,0:T(8,128)S(1)}, f32[16,128]{1,0:T(8,128)}, u32[]{:S(2)}) copy-start(f32[16,128]{1,0:T(8,128)} %get-tuple-element.20) | copy-start | bytes 24580
  14.1 32.2 %copy-start = (f32[128,128]{1,0:T(8,128)S(1)}, f32[128,128]{1,0:T(8,128)}, u32[]{:S(2)}) copy-start(f32[128,128]{1,0:T(8,128)} %get-tuple-element.18.nodes_ref) | copy-start | bytes 196612
  14.1 3.9 %collective-permute-start.3 = (f32[2,8,24,128]{3,2,0,1:T(8,128)S(1)}, f32[2,8,24,128]{3,2,0,1:T(8,128)S(1)}, u32[]{:S(2)}, u32[]{:S(2)}) collective-permute-start(f32[2,8,24,128]{3,2,0,1:T(8,128)S(1)} %copy.9), channel_id=1, source_target_pairs={{0,1},{1,0},{2,3},{3,2},{4,5},{5,4},{6,7},{7,6},{8,9},{9,8},{10,11... | collective-permute-start | bytes 589832 | tf_op jit(solution)/shard_map/ppermute | solution.py:339
  18.0 9.5 %collective-permute-start.4 = (f32[4,2,24,128]{3,2,0,1:T(8,128)S(1)}, f32[4,2,24,128]{3,2,0,1:T(8,128)S(1)}, u32[]{:S(2)}, u32[]{:S(2)}) collective-permute-start(f32[4,2,24,128]{3,2,0,1:T(8,128)S(1)} %pad_maximum_fusion.2), channel_id=1, source_target_pairs={{0,4},{1,5},{2,6},{3,7},{4,0},{5,1},{6,2},{7,3},{8,12},{9,13},{10,... | collective-permute-start | bytes 294920 | tf_op jit(solution)/shard_map/ppermute | solution.py:339
  23.1 4.9 %collective-permute-start.5 = (f32[4,2,24,128]{3,2,0,1:T(8,128)S(1)}, f32[4,2,24,128]{3,2,0,1:T(8,128)S(1)}, u32[]{:S(2)}, u32[]{:S(2)}) collective-permute-start(f32[4,2,24,128]{3,2,0,1:T(8,128)S(1)} %pad_maximum_fusion.3), channel_id=1, source_target_pairs={{0,2},{1,3},{2,0},{3,1},{4,6},{5,7},{6,4},{7,5},{8,10},{9,11},{10,... | collective-permute-start | bytes 294920 | tf_op jit(solution)/shard_map/ppermute | solution.py:339
  23.2 8.2 %collective-permute-start.6 = (f32[4,2,24,128]{3,2,0,1:T(8,128)S(1)}, f32[4,2,24,128]{3,2,0,1:T(8,128)S(1)}, u32[]{:S(2)}, u32[]{:S(2)}) collective-permute-start(f32[4,2,24,128]{3,2,0,1:T(8,128)S(1)} %pad_maximum_fusion.4), channel_id=1, source_target_pairs={{0,6},{1,7},{2,4},{3,5},{4,2},{5,3},{6,0},{7,1},{8,14},{9,15},{10,... | collective-permute-start | bytes 294920 | tf_op jit(solution)/shard_map/ppermute | solution.py:339
  31.4 17.6 %collective-permute-start.7 = (f32[16,1,24,128]{3,2,0,1:T(8,128)S(1)}, f32[16,1,24,128]{3,2,0,1:T(8,128)S(1)}, u32[]{:S(2)}, u32[]{:S(2)}) collective-permute-start(f32[16,1,24,128]{3,2,0,1:T(8,128)S(1)} %pad_maximum_fusion.1), channel_id=1, source_target_pairs={{0,8},{1,9},{2,10},{3,11},{4,12},{5,13},{6,14},{7,15},{8,0},{9,1},... | collective-permute-start | bytes 589832 | tf_op jit(solution)/shard_map/ppermute | solution.py:339
  41.0 2.5 %collective-permute-start = (f32[16,128]{1,0:T(8,128)S(1)}, f32[16,128]{1,0:T(8,128)S(1)}, u32[]{:S(2)}, u32[]{:S(2)}) collective-permute-start(f32[16,128]{1,0:T(8,128)S(1)} %copy-done.3), channel_id=1, source_target_pairs={{0,1},{1,2},{2,3},{3,0},{4,5},{5,6},{6,7},{7,4},{8,9},{9,10},{10,1... | collective-permute-start | bytes 24584 | tf_op jit(solution)/shard_map/ppermute | solution.py:334
  42.7 3.6 %collective-permute-start.1 = (f32[16,128]{1,0:T(8,128)S(1)}, f32[16,128]{1,0:T(8,128)S(1)}, u32[]{:S(2)}, u32[]{:S(2)}) collective-permute-start(f32[16,128]{1,0:T(8,128)S(1)} %copy-done.2), channel_id=1, source_target_pairs={{0,3},{1,0},{2,1},{3,2},{4,7},{5,4},{6,5},{7,6},{8,11},{9,8},{10,9... | collective-permute-start | bytes 24584 | tf_op jit(solution)/shard_map/ppermute | solution.py:334
  46.6 5.7 %collective-permute-start.8 = (f32[8,128]{1,0:T(8,128)S(1)}, f32[8,128]{1,0:T(8,128)S(1)}, u32[]{:S(2)}, u32[]{:S(2)}) collective-permute-start(f32[8,128]{1,0:T(8,128)S(1)} %get-tuple-element.27.high_ref), channel_id=1, source_target_pairs={{0,4},{4,8},{8,12},{12,16},{16,20},{20,24},{24,28},{28,0},{1,5},{5... | collective-permute-start | bytes 12296 | tf_op jit(solution)/shard_map/ppermute | solution.py:334
  46.6 5.6 %collective-permute-start.9 = (f32[8,128]{1,0:T(8,128)S(1)}, f32[8,128]{1,0:T(8,128)S(1)}, u32[]{:S(2)}, u32[]{:S(2)}) collective-permute-start(f32[8,128]{1,0:T(8,128)S(1)} %get-tuple-element.28.low_ref), channel_id=1, source_target_pairs={{0,28},{4,0},{8,4},{12,8},{16,12},{20,16},{24,20},{28,24},{1,29},{... | collective-permute-start | bytes 12296 | tf_op jit(solution)/shard_map/ppermute | solution.py:334
